TPU v7x, 1024 devices: a whole 4x4x32 slice. The times are simulated.
1024 devices in a mesh: layer: 16 (over z_lo), row: 8 (over y, z_hi), col: 8 (over x, core).
Axes of the slice: x: 4, y: 4, z: 32 (z_hi: 2, z_lo: 16; z = z_hi * 16 + z_lo), core: 2. Of those that a mesh axis runs over, the one named last changes fastest.
Arguments:
- momentum: bfloat16 [16, 896, 4096], P('layer', ('row', 'col')), may hold values from -1 to 1
Outputs:
- update: bfloat16 [16, 896, 4096], P('layer', 'row', 'col')
All inputs are finite; a program needn't handle non-finite values.
Results may differ from a plain program's by a relative error of at most 0.024.
Values may be sent and summed in bfloat16 or wider, within the bound.
No kernel may reach another device: no remote copies, remote signals or barrier semaphores. Data moves between devices by JAX's collectives and lax.ppermute only.
A program may use at most 32 MiB of HBM per device.

v0:
```python
import math

import jax
import jax.numpy as jnp
from jax import lax
from jax.sharding import PartitionSpec as P

M = 3584
K = 4096


def swapped(shard, axis, stride):
    return lax.ppermute(shard, axis, [(i, i ^ 1 << stride) for i in range(lax.axis_size(axis))])


def panel_rows(tile):
    merged = lax.all_gather(tile, "row", axis=0, tiled=True)
    for bit in (0, 1):
        merged = jnp.concatenate([merged, swapped(merged, "layer", bit)], 0)
    return merged


def shards(momentum):
    arrived = lax.all_to_all(momentum, "col", split_axis=2, concat_axis=1, tiled=True)
    tile = arrived[0]
    panel = panel_rows(tile)
    partial_value = lax.dot_general(
        tile, panel, (((1,), (1,)), ((), ())), preferred_element_type=jnp.float32
    )
    gram = lax.psum(partial_value.astype(jnp.bfloat16), "col")
    first = jnp.dot(gram, panel, preferred_element_type=jnp.float32).astype(jnp.bfloat16)
    first_panel = panel_rows(first)
    second = jnp.dot(gram, first_panel, preferred_element_type=jnp.float32)
    mixed = 3.4445 * tile.astype(jnp.float32) - 4.775 * first.astype(jnp.float32) + 2.0315 * second
    return (math.sqrt(max(M, K)) * mixed).astype(jnp.bfloat16)[None]


def solution(mesh):
    return jax.shard_map(
        shards,
        mesh=mesh,
        in_specs=(P("layer", ("row", "col"), None),),
        out_specs=P("layer", "row", "col"),
        check_vma=False,
    )
```

profile of v0, /device:TPU:4, one launch (start us, length us, event | category | flops | bytes accessed | tf_op | source)
XLA Modules:
  0.0 738.5 jit_solution(4610549443643245502)
XLA Ops:
  6.5 4.4 copy.6
  10.9 0.5 broadcast
  11.4 22.4 %reduce = bf16[4096,14]{1,0:T(8,128)(2,1)S(1)} reduce(bf16[4096,1,14]{2,1,0:T(2,128)(2,1)S(1)} %bitcast.19, bf16[]{:T(256)} %broadcast), dimensions={1}, to_apply=%bitcast.12.reduce_sub_computation | reduce | bytes 229378
  33.8 1.8 reshape.1
  35.7 18.8 %all_to_all.15 = bf16[8,2,3584]{2,1,0:T(2,128)(2,1)S(1)} all-to-all(bf16[8,2,3584]{2,1,0:T(2,128)(2,1)S(1)} %reshape.1), channel_id=1, replica_groups=mesh['layer'=16,'row'=8,'col'=8] {'col'}, dimensions={0} | all-to-all | bytes 229376 | tf_op jit(solution)/shard_map/all_to_all | solution.py:24
  54.5 2.3 reshape.2
  56.8 2.1 copy.7
  59.1 181.6 %all_gather.6 = bf16[896,512]{1,0:T(8,128)(2,1)S(1)} all-gather(bf16[112,512]{1,0:T(8,128)(2,1)S(1)} %squeeze.3), channel_id=1, replica_groups=mesh['layer'=16,'row'=8,'col'=8] {'row'}, dimensions={0}, use_global_device_ids=true | all-gather | bytes 1032192 | tf_op jit(solution)/shard_map/all_gather | solution.py:17
  240.7 6.7 collective-permute-start
  247.3 12.9 %collective-permute-done = bf16[896,512]{1,0:T(8,128)(2,1)S(1)} collective-permute-done((bf16[896,512]{1,0:T(8,128)(2,1)S(1)}, bf16[896,512]{1,0:T(8,128)(2,1)S(1)}, u32[]{:S(2)}, u32[]{:S(2)}) %collective-permute-start) | collective-permute-done | bytes 917536 | tf_op jit(solution)/shard_map/ppermute | solution.py:13
  260.3 0.1 pad_maximum_fusion
  260.4 10.5 %collective-permute-start.1 = (bf16[1792,512]{1,0:T(8,128)(2,1)S(1)}, bf16[1792,512]{1,0:T(8,128)(2,1)S(1)}, u32[]{:S(2)}, u32[]{:S(2)}) collective-permute-start(bf16[1792,512]{1,0:T(8,128)(2,1)S(1)} %pad_maximum_fusion), channel_id=1, source_target_pairs={{0,128},{64,192},{128,0},{192,64},{256,384},{320,448},{384,256},{4... | collective-permute-start | bytes 5505032 | tf_op jit(solution)/shard_map/ppermute | solution.py:13
  271.1 69.2 %collective-permute-done.1 = bf16[1792,512]{1,0:T(8,128)(2,1)S(1)} collective-permute-done((bf16[1792,512]{1,0:T(8,128)(2,1)S(1)}, bf16[1792,512]{1,0:T(8,128)(2,1)S(1)}, u32[]{:S(2)}, u32[]{:S(2)}) %collective-permute-start.1) | collective-permute-done | bytes 1835040 | tf_op jit(solution)/shard_map/ppermute | solution.py:13
  340.3 0.1 constant_dynamic-update-slice_fusion
  340.4 1.8 copy-done
  342.2 2.2 fusion
  344.4 83.6 %all-reduce.2.cloned.1.call-done = bf16[112,3584]{1,0:T(8,128)(2,1)} async-done(((bf16[112,3584]{1,0:T(8,128)(2,1)}), bf16[112,3584]{1,0:T(8,128)(2,1)}) %all-reduce.2.cloned.1.call-update) | async-done | bytes 802832 | tf_op jit(solution)/shard_map/psum | solution.py:30
  428.0 3.0 convolution_convert_fusion.1
  431.0 198.2 %all_gather.7 = bf16[896,512]{1,0:T(8,128)(2,1)S(1)} all-gather(bf16[112,512]{1,0:T(8,128)(2,1)S(1)} %convolution_convert_fusion.1), channel_id=1, replica_groups=mesh['layer'=16,'row'=8,'col'=8] {'row'}, dimensions={0}, use_global_device_ids=true | all-gather | bytes 1032192 | tf_op jit(solution)/shard_map/all_gather | solution.py:17
  629.2 18.6 %collective-permute-start.2 = (bf16[896,512]{1,0:T(8,128)(2,1)S(1)}, bf16[896,512]{1,0:T(8,128)(2,1)S(1)}, u32[]{:S(2)}, u32[]{:S(2)}) collective-permute-start(bf16[896,512]{1,0:T(8,128)(2,1)S(1)} %all_gather.7), channel_id=1, source_target_pairs={{0,64},{64,0},{128,192},{192,128},{256,320},{320,256},{384,448},{4... | collective-permute-start | bytes 2752520 | tf_op jit(solution)/shard_map/ppermute | solution.py:13
  647.8 20.6 %collective-permute-done.2 = bf16[896,512]{1,0:T(8,128)(2,1)S(1)} collective-permute-done((bf16[896,512]{1,0:T(8,128)(2,1)S(1)}, bf16[896,512]{1,0:T(8,128)(2,1)S(1)}, u32[]{:S(2)}, u32[]{:S(2)}) %collective-permute-start.2) | collective-permute-done | bytes 917536 | tf_op jit(solution)/shard_map/ppermute | solution.py:13
  668.5 1.9 collective-permute-start.3
  670.4 59.8 %collective-permute-done.3 = bf16[1792,512]{1,0:T(8,128)(2,1)S(1)} collective-permute-done((bf16[1792,512]{1,0:T(8,128)(2,1)S(1)}, bf16[1792,512]{1,0:T(8,128)(2,1)S(1)}, u32[]{:S(2)}, u32[]{:S(2)}) %collective-permute-start.3) | collective-permute-done | bytes 1835040 | tf_op jit(solution)/shard_map/ppermute | solution.py:13
  730.2 1.5 fusion.19
  (12 shorter events, 0.4 us)
Async XLA Ops:
  6.5 421.4 %all-reduce.2.cloned.1.call-start = ((), (), s32[]{:S(2)}) async-start(), calls=%async_computation.1 | async-start | bytes 1605632 | tf_op jit(solution)/shard_map/psum | solution.py:30
  240.7 19.6 %collective-permute-start = (bf16[896,512]{1,0:T(8,128)(2,1)S(1)}, bf16[896,512]{1,0:T(8,128)(2,1)S(1)}, u32[]{:S(2)}, u32[]{:S(2)}) collective-permute-start(bf16[896,512]{1,0:T(8,128)(2,1)S(1)} %all_gather.6), channel_id=1, source_target_pairs={{0,64},{64,0},{128,192},{192,128},{256,320},{320,256},{384,448},{4... | collective-permute-start | bytes 2752520 | tf_op jit(solution)/shard_map/ppermute | solution.py:13
  260.4 79.9 %collective-permute-start.1 = (bf16[1792,512]{1,0:T(8,128)(2,1)S(1)}, bf16[1792,512]{1,0:T(8,128)(2,1)S(1)}, u32[]{:S(2)}, u32[]{:S(2)}) collective-permute-start(bf16[1792,512]{1,0:T(8,128)(2,1)S(1)} %pad_maximum_fusion), channel_id=1, source_target_pairs={{0,128},{64,192},{128,0},{192,64},{256,384},{320,448},{384,256},{4... | collective-permute-start | bytes 5505032 | tf_op jit(solution)/shard_map/ppermute | solution.py:13
  340.4 1.8 copy-start
  428.0 302.2 %copy-start.1 = (bf16[112,3584]{1,0:T(8,128)(2,1)S(1)}, bf16[112,3584]{1,0:T(8,128)(2,1)}, u32[]{:S(2)}) copy-start(bf16[112,3584]{1,0:T(8,128)(2,1)} %all-reduce.2.cloned.1.call-done) | copy-start | bytes 2408452
  629.2 39.2 %collective-permute-start.2 = (bf16[896,512]{1,0:T(8,128)(2,1)S(1)}, bf16[896,512]{1,0:T(8,128)(2,1)S(1)}, u32[]{:S(2)}, u32[]{:S(2)}) collective-permute-start(bf16[896,512]{1,0:T(8,128)(2,1)S(1)} %all_gather.7), channel_id=1, source_target_pairs={{0,64},{64,0},{128,192},{192,128},{256,320},{320,256},{384,448},{4... | collective-permute-start | bytes 2752520 | tf_op jit(solution)/shard_map/ppermute | solution.py:13
  668.5 61.7 %collective-permute-start.3 = (bf16[1792,512]{1,0:T(8,128)(2,1)S(1)}, bf16[1792,512]{1,0:T(8,128)(2,1)S(1)}, u32[]{:S(2)}, u32[]{:S(2)}) collective-permute-start(bf16[1792,512]{1,0:T(8,128)(2,1)S(1)} %pad_maximum_fusion.1), channel_id=1, source_target_pairs={{0,128},{64,192},{128,0},{192,64},{256,384},{320,448},{384,256},{4... | collective-permute-start | bytes 5505032 | tf_op jit(solution)/shard_map/ppermute | solution.py:13
Sparse Core Ops, SparseCore 0:
  344.5 83.3 all-reduce.1
where the time goes:
time: 739 us
  blocking collectives  399 us (54%)
  waiting for transfers between devices  246 us (33%)
  starting transfers between devices  37.7 us (5%)
  other arithmetic  22.7 us (3%)
  between operations  13.5 us (2%)
  local copies, waits for them, and re-layouts  13.3 us (2%)
    all_gather x2, blocking collectives, panel_rows(): merged = lax.all_gather(tile, 'row', axis=0, tiled=True)  380 us
    ppermute x4, waiting for transfers between devices, swapped(): lax.ppermute(shard, axis, [(i, i ^ 1 << stride) for i in range(lax.axis_s...  163 us
    psum x1, waiting for transfers between devices, shards(): gram = lax.psum(partial_value.astype(jnp.bfloat16), 'col')  83.6 us
    ppermute x4, starting transfers between devices, swapped(): lax.ppermute(shard, axis, [(i, i ^ 1 << stride) for i in range(lax.axis_s...  37.7 us
    unnamed x1, other arithmetic  22.4 us
    all_to_all x1, blocking collectives, shards(): lax.all_to_all(momentum, 'col', split_axis=2, concat_axis=1, tiled=True)  18.8 us
  transfers between devices with their start and end apart: 5, of which 5 were waited for; matrix products, arithmetic and copies ran while one was open for 0% of the time, Pallas kernels for 0%

commit v1 on v0

v1 whole, which is shorter than its diff:
```python
import math

import jax
import jax.numpy as jnp
from jax import lax
from jax.sharding import Mesh, PartitionSpec as P

AXES = ("layer", "quarter", "y", "half", "x", "core")
SWAP = [(0, 1), (1, 0)]
A1, A2, A3 = 3.4445, -4.775, 2.0315


def dot(lhs, rhs, dims):
    return lax.dot_general(lhs, rhs, (dims, ((), ())), preferred_element_type=jnp.float32)


def total(blocks):
    return jnp.sum(blocks.astype(jnp.float32), 0)


def exchange(blocks, axis):
    return lax.all_to_all(blocks, axis, 0, 0, tiled=True)


def shards(momentum):
    bf16 = jnp.bfloat16
    _, m, k = momentum.shape
    nx, ny, nq, nc = 4, 4, 4, 2
    w = k // nx
    n = nx * m
    own = exchange(momentum[0].reshape(m, nx, w).transpose(1, 0, 2), "x").reshape(n, w)
    other = lax.ppermute(own, "half", SWAP)
    both = jnp.stack([own, other])
    left = lax.all_gather(both, "y", axis=0).reshape(ny * 2 * n, w)
    right = lax.all_gather(both, "quarter", axis=1)
    right = lax.all_gather(right, "core", axis=2).reshape(2 * nq * nc * n, w)
    term = dot(left, right, ((1,), (1,))).astype(bf16)
    mine = total(exchange(term.reshape(nx, 2 * n, 16 * n), "x")).astype(bf16)
    gram = lax.all_gather(mine, "x", axis=0, tiled=True)
    term = dot(gram, right, ((1,), (0,))).astype(bf16)
    first = total(exchange(term.reshape(ny, 2 * n, w), "y")).astype(bf16)
    firsts = lax.all_gather(first, "y", axis=0, tiled=True)
    second = dot(gram[:, : 8 * n], firsts, ((0,), (0,))).reshape(nq, nc, n, w)
    here = (jnp.arange(nq) == lax.axis_index("quarter"))[:, None] & (
        jnp.arange(nc) == lax.axis_index("core")
    )[None]
    pick = jnp.where(here, jnp.float32(A2 / A3), 0.0)[:, :, None, None]
    second = second + pick * first[:n].astype(jnp.float32)[None, None]
    second = second.reshape(nq, nc * n, w)
    core = lax.axis_index("core")
    h = w // 2
    low, high = second[..., :h], second[..., h:]
    keep = jnp.where(core == 0, low, high)
    send = jnp.where(core == 0, high, low).astype(bf16)
    got = lax.ppermute(send, "core", SWAP)
    part = (keep + got.astype(jnp.float32)).astype(bf16)
    second = total(exchange(part, "quarter"))
    tile = lax.dynamic_slice(
        right.reshape(2, nq, nc * n, w), (0, lax.axis_index("quarter"), 0, core * h), (1, 1, nc * n, h)
    )[0, 0]
    mixed = math.sqrt(max(256 * m, k)) * (A1 * tile.astype(jnp.float32) + A3 * second)
    mixed = mixed.reshape(nc, nx, m, h).transpose(1, 0, 2, 3).reshape(nc * n, h)
    return mixed.astype(bf16)[None]


def solution(mesh):
    fine = Mesh(mesh.devices.reshape(-1, 4, 4, 2, 4, 2), AXES)
    return jax.shard_map(
        shards,
        mesh=fine,
        in_specs=(P(("layer", "quarter"), ("y", "half", "x", "core"), None),),
        out_specs=P(("layer", "quarter"), ("y", "half"), ("x", "core")),
        check_vma=False,
    )
```

time: 739 us -> 211 us (0.29)
  the two profiles are of different devices: /device:TPU:4 before, /device:TPU:1 now
where the time goes in v1:
time: 211 us
  blocking collectives  89.7 us (43%)
  waiting for transfers between devices  50.3 us (24%)
  starting transfers between devices  46.9 us (22%)
  between operations  13.6 us (6%)
  matrix products  5.36 us (3%)
  other arithmetic  2.79 us (1%)
    all_gather x1, blocking collectives, shards(): right = lax.all_gather(both, 'quarter', axis=1)  30.8 us
    ppermute x1, starting transfers between devices, shards(): other = lax.ppermute(own, 'half', SWAP)  28.7 us
    all_gather x1, waiting for transfers between devices, shards(): right = lax.all_gather(right, 'core', axis=2).reshape(2 * nq * nc * n, w)  25.7 us
    all_to_all x2, blocking collectives, exchange(): return lax.all_to_all(blocks, axis, 0, 0, tiled=True)  24.1 us
    all_to_all x2, waiting for transfers between devices, exchange(): return lax.all_to_all(blocks, axis, 0, 0, tiled=True)  20.4 us
    all_gather x1, blocking collectives, shards(): firsts = lax.all_gather(first, 'y', axis=0, tiled=True)  12.1 us
    all_gather x1, blocking collectives, shards(): left = lax.all_gather(both, 'y', axis=0).reshape(ny * 2 * n, w)  11.6 us
    all_gather x1, blocking collectives, shards(): gram = lax.all_gather(mine, 'x', axis=0, tiled=True)  11.2 us
  transfers between devices with their start and end apart: 5, of which 5 were waited for; matrix products, arithmetic and copies ran while one was open for 1% of the time, Pallas kernels for 0%

profile of v1, /device:TPU:1, one launch (start us, length us, event | category | flops | bytes accessed | tf_op | source)
XLA Modules:
  0.0 210.7 jit_solution(14324430939731545707)
XLA Ops:
  6.5 1.0 reshape_squeeze.3
  7.6 9.5 %all_to_all.20 = bf16[4,14,1024]{2,1,0:T(8,128)(2,1)S(1)} all-to-all(bf16[4,14,1024]{2,1,0:T(8,128)(2,1)S(1)} %bitcast.25), channel_id=1, replica_groups=mesh['layer'=4,'quarter'=4,'y'=4,'half'=2,'x'=4,'core'=2] {'x'}, dimensions={0} | all-to-all | bytes 229376 | tf_op jit(solution)/shard_map/all_to_all | solution.py:22
  17.1 28.7 %collective-permute-start = (bf16[56,1024]{1,0:T(8,128)(2,1)S(1)}, bf16[56,1024]{1,0:T(8,128)(2,1)S(1)}, u32[]{:S(2)}, u32[]{:S(2)}) collective-permute-start(bf16[56,1024]{1,0:T(8,128)(2,1)S(1)} %reshape.79), channel_id=1, source_target_pairs={{0,8},{8,0},{1,9},{9,1},{2,10},{10,2},{3,11},{11,3},{4,12},{12,4},... | collective-permute-start | bytes 344072 | tf_op jit(solution)/shard_map/ppermute | solution.py:32
  45.8 2.8 %collective-permute-done = bf16[56,1024]{1,0:T(8,128)(2,1)S(1)} collective-permute-done((bf16[56,1024]{1,0:T(8,128)(2,1)S(1)}, bf16[56,1024]{1,0:T(8,128)(2,1)S(1)}, u32[]{:S(2)}, u32[]{:S(2)}) %collective-permute-start) | collective-permute-done | bytes 114720 | tf_op jit(solution)/shard_map/ppermute | solution.py:32
  48.7 30.8 %all-gather = bf16[2,224,1024]{2,1,0:T(8,128)(2,1)} all-gather(bf16[2,56,1024]{2,1,0:T(8,128)(2,1)S(1)} %pad_maximum_fusion), channel_id=2, replica_groups=mesh['layer'=4,'quarter'=4,'y'=4,'half'=2,'x'=4,'core'=2] {'quarter'}, dimensions={1}, use_global_device_ids=true | all-gather | bytes 1146880 | tf_op jit(solution)/shard_map/all_gather | solution.py:35
  79.5 11.6 %all-gather.2 = bf16[8,56,1024]{2,1,0:T(8,128)(2,1)S(1)} all-gather(bf16[2,56,1024]{2,1,0:T(8,128)(2,1)S(1)} %pad_maximum_fusion), channel_id=4, replica_groups=mesh['layer'=4,'quarter'=4,'y'=4,'half'=2,'x'=4,'core'=2] {'y'}, dimensions={0}, use_global_device_ids=true | all-gather | bytes 1146880 | tf_op jit(solution)/shard_map/all_gather | solution.py:34
  91.1 25.7 %all-gather.5.cloned.1.call-done = bf16[2,4,112,1024]{3,2,1,0:T(8,128)(2,1)} async-done(((bf16[2,4,56,1024]{3,2,1,0:T(8,128)(2,1)}), bf16[2,4,112,1024]{3,2,1,0:T(8,128)(2,1)}) %all-gather.5.cloned.1.call-update) | async-done | bytes 1835024 | tf_op jit(solution)/shard_map/all_gather | solution.py:36
  116.7 2.6 %convolution_convert_fusion.1 = bf16[448,896]{1,0:T(8,128)(2,1)S(1)} fusion(bf16[448,1024]{1,0:T(8,128)(2,1)S(1)} %bitcast.23, bf16[896,1024]{1,0:T(8,128)(2,1)} %bitcast.27), kind=kOutput, calls=%fused_computation.2 | convolution fusion | flops 822484992 | bytes 3555328 | tf_op jit(solution)/shard_map/dot_general | solution.py:14
  119.4 14.6 %all_to_all.21 = bf16[4,112,896]{2,1,0:T(8,128)(2,1)S(1)} all-to-all(bf16[4,112,896]{2,1,0:T(8,128)(2,1)S(1)} %bitcast.24), channel_id=1, replica_groups=mesh['layer'=4,'quarter'=4,'y'=4,'half'=2,'x'=4,'core'=2] {'x'}, dimensions={0} | all-to-all | bytes 1605632 | tf_op jit(solution)/shard_map/all_to_all | solution.py:22
  134.1 11.2 %all_gather.30 = bf16[448,896]{1,0:T(8,128)(2,1)S(1)} all-gather(bf16[112,896]{1,0:T(8,128)(2,1)S(1)} %reduce_sum.33), channel_id=1, replica_groups=mesh['layer'=4,'quarter'=4,'y'=4,'half'=2,'x'=4,'core'=2] {'x'}, dimensions={0}, use_global_device_ids=true | all-gather | bytes 1003520 | tf_op jit(solution)/shard_map/all_gather | solution.py:39
  145.3 2.1 convolution_convert_fusion
  147.4 3.5 %all-to-all-start.2 = ((bf16[4,112,1024]{2,1,0:T(8,128)(2,1)}), bf16[4,112,1024]{2,1,0:T(8,128)(2,1)S(1)}, u32[]{:S(2)}, u32[]{:S(2)}) async-start(bf16[4,112,1024]{2,1,0:T(8,128)(2,1)} %bitcast.6), calls=%async_computation.2 | async-start | bytes 1835008 | tf_op jit(solution)/shard_map/all_to_all | solution.py:22
  151.1 8.7 %all-to-all-done.2 = bf16[4,112,1024]{2,1,0:T(8,128)(2,1)S(1)} async-done(((bf16[4,112,1024]{2,1,0:T(8,128)(2,1)}), bf16[4,112,1024]{2,1,0:T(8,128)(2,1)S(1)}, u32[]{:S(2)}, u32[]{:S(2)}) %all-to-all-start.2) | async-done | bytes 917536 | tf_op jit(solution)/shard_map/all_to_all | solution.py:22
  159.9 0.2 reduce_sum.34
  160.1 12.1 %all_gather.31 = bf16[448,1024]{1,0:T(8,128)(2,1)S(1)} all-gather(bf16[112,1024]{1,0:T(8,128)(2,1)S(1)} %reduce_sum.34), channel_id=1, replica_groups=mesh['layer'=4,'quarter'=4,'y'=4,'half'=2,'x'=4,'core'=2] {'y'}, dimensions={0}, use_global_device_ids=true | all-gather | bytes 1146880 | tf_op jit(solution)/shard_map/all_gather | solution.py:42
  172.2 0.7 fusion
  172.9 0.2 multiply_add_fusion
  173.2 10.3 %collective-permute-start.1 = (bf16[4,112,512]{2,1,0:T(8,128)(2,1)S(1)}, bf16[4,112,512]{2,1,0:T(8,128)(2,1)S(1)}, u32[]{:S(2)}, u32[]{:S(2)}) collective-permute-start(bf16[4,112,512]{2,1,0:T(8,128)(2,1)S(1)} %select_convert_fusion), channel_id=1, source_target_pairs={{0,1},{1,0},{2,3},{3,2},{4,5},{5,4},{6,7},{7,6},{8,9},{9,8},{10,11... | collective-permute-start | bytes 1376264 | tf_op jit(solution)/shard_map/ppermute | solution.py:55
  183.5 1.4 collective-permute-done.1
  184.9 1.0 add_convert_fusion
  185.9 4.4 %all-to-all-start.3 = ((bf16[4,112,512]{2,1,0:T(8,128)(2,1)}), bf16[4,112,512]{2,1,0:T(8,128)(2,1)S(1)}, u32[]{:S(2)}, u32[]{:S(2)}) async-start(bf16[4,112,512]{2,1,0:T(8,128)(2,1)} %add_convert_fusion), calls=%async_computation.3 | async-start | bytes 917504 | tf_op jit(solution)/shard_map/all_to_all | solution.py:22
  190.3 0.9 convert_multiply_fusion
  191.3 11.7 %all-to-all-done.3 = bf16[4,112,512]{2,1,0:T(8,128)(2,1)S(1)} async-done(((bf16[4,112,512]{2,1,0:T(8,128)(2,1)}), bf16[4,112,512]{2,1,0:T(8,128)(2,1)S(1)}, u32[]{:S(2)}, u32[]{:S(2)}) %all-to-all-start.3) | async-done | bytes 458784 | tf_op jit(solution)/shard_map/all_to_all | solution.py:22
  203.2 0.7 convert_element_type.56
  (23 shorter events, 0.9 us)
Async XLA Ops:
  6.5 110.2 %all-gather.5.cloned.1.call-start = ((), (), s32[]{:S(2)}) async-start(), calls=%async_computation.4 | async-start | bytes 2752512 | tf_op jit(solution)/shard_map/all_gather | solution.py:36
  17.1 31.6 %collective-permute-start = (bf16[56,1024]{1,0:T(8,128)(2,1)S(1)}, bf16[56,1024]{1,0:T(8,128)(2,1)S(1)}, u32[]{:S(2)}, u32[]{:S(2)}) collective-permute-start(bf16[56,1024]{1,0:T(8,128)(2,1)S(1)} %reshape.79), channel_id=1, source_target_pairs={{0,8},{8,0},{1,9},{9,1},{2,10},{10,2},{3,11},{11,3},{4,12},{12,4},... | collective-permute-start | bytes 344072 | tf_op jit(solution)/shard_map/ppermute | solution.py:32
  119.4 25.9 %copy-start = (bf16[2,4,112,1024]{3,2,1,0:T(8,128)(2,1)S(1)}, bf16[2,4,112,1024]{3,2,1,0:T(8,128)(2,1)}, u32[]{:S(2)}) copy-start(bf16[2,4,112,1024]{3,2,1,0:T(8,128)(2,1)} %all-gather.5.cloned.1.call-done) | copy-start | bytes 5505028
  147.4 12.5 %all-to-all-start.2 = ((bf16[4,112,1024]{2,1,0:T(8,128)(2,1)}), bf16[4,112,1024]{2,1,0:T(8,128)(2,1)S(1)}, u32[]{:S(2)}, u32[]{:S(2)}) async-start(bf16[4,112,1024]{2,1,0:T(8,128)(2,1)} %bitcast.6), calls=%async_computation.2 | async-start | bytes 1835008 | tf_op jit(solution)/shard_map/all_to_all | solution.py:22
  173.2 11.7 %collective-permute-start.1 = (bf16[4,112,512]{2,1,0:T(8,128)(2,1)S(1)}, bf16[4,112,512]{2,1,0:T(8,128)(2,1)S(1)}, u32[]{:S(2)}, u32[]{:S(2)}) collective-permute-start(bf16[4,112,512]{2,1,0:T(8,128)(2,1)S(1)} %select_convert_fusion), channel_id=1, source_target_pairs={{0,1},{1,0},{2,3},{3,2},{4,5},{5,4},{6,7},{7,6},{8,9},{9,8},{10,11... | collective-permute-start | bytes 1376264 | tf_op jit(solution)/shard_map/ppermute | solution.py:55
  185.9 17.1 %all-to-all-start.3 = ((bf16[4,112,512]{2,1,0:T(8,128)(2,1)}), bf16[4,112,512]{2,1,0:T(8,128)(2,1)S(1)}, u32[]{:S(2)}, u32[]{:S(2)}) async-start(bf16[4,112,512]{2,1,0:T(8,128)(2,1)} %add_convert_fusion), calls=%async_computation.3 | async-start | bytes 917504 | tf_op jit(solution)/shard_map/all_to_all | solution.py:22
Sparse Core Ops, SparseCore 0:
  79.6 37.1 all-gather.4

commit v2 on v1

--- a/solution.py
+++ b/solution.py
@@ -30,10 +30,19 @@
     n = nx * m
     own = exchange(momentum[0].reshape(m, nx, w).transpose(1, 0, 2), "x").reshape(n, w)
     other = lax.ppermute(own, "half", SWAP)
-    both = jnp.stack([own, other])
-    left = lax.all_gather(both, "y", axis=0).reshape(ny * 2 * n, w)
-    right = lax.all_gather(both, "quarter", axis=1)
-    right = lax.all_gather(right, "core", axis=2).reshape(2 * nq * nc * n, w)
+    core = lax.axis_index("core")
+
+    def gathered(rows):
+        column = lax.all_gather(rows, "quarter", axis=0)
+        across = lax.ppermute(column, "core", SWAP)
+        line = lax.all_gather(rows, "y", axis=0)
+        pair = [jnp.where(core == 0, column, across), jnp.where(core == 0, across, column)]
+        return line, jnp.stack(pair, 1)
+
+    own_line, own_block = gathered(own)
+    other_line, other_block = gathered(other)
+    left = jnp.stack([own_line, other_line], 1).reshape(ny * 2 * n, w)
+    right = jnp.stack([own_block, other_block]).reshape(2 * nq * nc * n, w)
     term = dot(left, right, ((1,), (1,))).astype(bf16)
     mine = total(exchange(term.reshape(nx, 2 * n, 16 * n), "x")).astype(bf16)
     gram = lax.all_gather(mine, "x", axis=0, tiled=True)
@@ -47,7 +56,6 @@
     pick = jnp.where(here, jnp.float32(A2 / A3), 0.0)[:, :, None, None]
     second = second + pick * first[:n].astype(jnp.float32)[None, None]
     second = second.reshape(nq, nc * n, w)
-    core = lax.axis_index("core")
     h = w // 2
     low, high = second[..., :h], second[..., h:]
     keep = jnp.where(core == 0, low, high)

time: 211 us -> 204 us (0.967)
  waiting for transfers between devices: 50.3 us -> 25.9 us
  starting transfers between devices: 46.9 us -> 65.2 us
  between operations: 13.6 us -> 0.26 us
  blocking collectives: 89.7 us -> 97.8 us
  local copies, waits for them, and re-layouts: 2.06 us -> 4.65 us
    all_gather x1 -> x0, waiting for transfers between devices: 25.7 us -> none  [shards(): right = lax.all_gather(right, 'core', axis=2).reshape(2 * nq * nc * n, w)]
    all_gather x2 -> x4, blocking collectives: 42.4 us -> 61.7 us  [the longest x2 40 us: gathered(): column = lax.all_gather(rows, 'quarter', axis=0)]
    ppermute x0 -> x2, starting transfers between devices: none -> 13.9 us  [gathered(): across = lax.ppermute(column, 'core', SWAP)]
    all_to_all x2 -> x1, blocking collectives: 24.1 us -> 12.9 us  [exchange(): return lax.all_to_all(blocks, axis, 0, 0, tiled=True)]
    all_to_all x2 -> x3, waiting for transfers between devices: 20.4 us -> 24.4 us  [exchange(): return lax.all_to_all(blocks, axis, 0, 0, tiled=True)]
    all_to_all x2 -> x3, starting transfers between devices: 7.92 us -> 11.8 us  [exchange(): return lax.all_to_all(blocks, axis, 0, 0, tiled=True)]
    ppermute x1, waiting for transfers between devices: 2.81 us -> 0.01 us  [shards(): other = lax.ppermute(own, 'half', SWAP)]
  transfers between devices with their start and end apart: 5 -> 7, of which waited for: 5 -> 4; matrix products, arithmetic and copies ran while one was open for 1% -> 1% of each run, Pallas kernels for 0% -> 0%
where the time goes in v2:
time: 204 us; the launch traced here: 203 us
  blocking collectives  97.8 us (48%)
  starting transfers between devices  65.2 us (32%)
  waiting for transfers between devices  25.9 us (13%)
  matrix products  5.37 us (3%)
  local copies, waits for them, and re-layouts  4.65 us (2%)
  other arithmetic  4.11 us (2%)
    all_gather x2, blocking collectives, gathered(): column = lax.all_gather(rows, 'quarter', axis=0)  40 us
    ppermute x1, starting transfers between devices, shards(): other = lax.ppermute(own, 'half', SWAP)  28.7 us
    all_to_all x3, waiting for transfers between devices, exchange(): return lax.all_to_all(blocks, axis, 0, 0, tiled=True)  24.4 us
    all_gather x2, blocking collectives, gathered(): line = lax.all_gather(rows, 'y', axis=0)  21.8 us
    ppermute x2, starting transfers between devices, gathered(): across = lax.ppermute(column, 'core', SWAP)  13.9 us
    all_to_all x1, blocking collectives, exchange(): return lax.all_to_all(blocks, axis, 0, 0, tiled=True)  12.9 us
    all_gather x1, blocking collectives, shards(): gram = lax.all_gather(mine, 'x', axis=0, tiled=True)  11.9 us
    all_to_all x3, starting transfers between devices, exchange(): return lax.all_to_all(blocks, axis, 0, 0, tiled=True)  11.8 us
  transfers between devices with their start and end apart: 7, of which 4 were waited for; matrix products, arithmetic and copies ran while one was open for 1% of the time, Pallas kernels for 0%

profile of v2, /device:TPU:1, one launch (start us, length us, event | category | flops | bytes accessed | tf_op | source)
XLA Modules:
  0.0 203.3 jit_solution(5442874749107214166)
XLA Ops:
  0.0 1.0 reshape_squeeze.3
  1.7 4.8 %all-to-all-start = ((bf16[4,14,1024]{2,1,0:T(8,128)(2,1)}), bf16[4,14,1024]{2,1,0:T(8,128)(2,1)S(1)}, u32[]{:S(2)}, u32[]{:S(2)}) async-start(bf16[4,14,1024]{2,1,0:T(8,128)(2,1)} %bitcast.42), calls=%async_computation | async-start | bytes 262144 | tf_op jit(solution)/shard_map/all_to_all | solution.py:22
  6.5 4.8 %all-to-all-done = bf16[4,14,1024]{2,1,0:T(8,128)(2,1)S(1)} async-done(((bf16[4,14,1024]{2,1,0:T(8,128)(2,1)}), bf16[4,14,1024]{2,1,0:T(8,128)(2,1)S(1)}, u32[]{:S(2)}, u32[]{:S(2)}) %all-to-all-start) | async-done | bytes 114720 | tf_op jit(solution)/shard_map/all_to_all | solution.py:22
  11.4 28.7 %collective-permute-start.1 = (bf16[56,1024]{1,0:T(8,128)(2,1)S(1)}, bf16[56,1024]{1,0:T(8,128)(2,1)S(1)}, u32[]{:S(2)}, u32[]{:S(2)}) collective-permute-start(bf16[56,1024]{1,0:T(8,128)(2,1)S(1)} %reshape.83), channel_id=1, source_target_pairs={{0,8},{8,0},{1,9},{9,1},{2,10},{10,2},{3,11},{11,3},{4,12},{12,4},... | collective-permute-start | bytes 344072 | tf_op jit(solution)/shard_map/ppermute | solution.py:32
  40.1 27.7 %all_gather.22 = bf16[4,56,1024]{2,1,0:T(8,128)(2,1)S(1)} all-gather(bf16[1,56,1024]{2,1,0:T(8,128)(2,1)S(1)} %all_gather_reshape.4), channel_id=1, replica_groups=mesh['layer'=4,'quarter'=4,'y'=4,'half'=2,'x'=4,'core'=2] {'quarter'}, dimensions={0}, use_global_device_ids=true | all-gather | bytes 573440 | tf_op jit(solution)/shard_map/all_gather | solution.py:36
  67.9 7.2 %collective-permute-start = (bf16[4,56,1024]{2,1,0:T(8,128)(2,1)S(1)}, bf16[4,56,1024]{2,1,0:T(8,128)(2,1)S(1)}, u32[]{:S(2)}, u32[]{:S(2)}) collective-permute-start(bf16[4,56,1024]{2,1,0:T(8,128)(2,1)S(1)} %all_gather.22), channel_id=1, source_target_pairs={{0,1},{1,0},{2,3},{3,2},{4,5},{5,4},{6,7},{7,6},{8,9},{9,8},{10,11... | collective-permute-start | bytes 1376264 | tf_op jit(solution)/shard_map/ppermute | solution.py:37
  75.1 10.9 %all_gather.25 = bf16[4,56,1024]{2,1,0:T(8,128)(2,1)S(1)} all-gather(bf16[1,56,1024]{2,1,0:T(8,128)(2,1)S(1)} %all_gather_reshape.4), channel_id=1, replica_groups=mesh['layer'=4,'quarter'=4,'y'=4,'half'=2,'x'=4,'core'=2] {'y'}, dimensions={0}, use_global_device_ids=true | all-gather | bytes 573440 | tf_op jit(solution)/shard_map/all_gather | solution.py:38
  86.0 12.2 %all-gather = bf16[224,1024]{1,0:T(8,128)(2,1)S(1)} all-gather(bf16[56,1024]{1,0:T(8,128)(2,1)S(1)} %collective-permute-done.1), channel_id=2, replica_groups=mesh['layer'=4,'quarter'=4,'y'=4,'half'=2,'x'=4,'core'=2] {'quarter'}, dimensions={0}, use_global_device_ids=true | all-gather | bytes 573440 | tf_op jit(solution)/shard_map/all_gather | solution.py:36
  98.3 6.6 %collective-permute-start.2 = (bf16[4,56,1024]{2,1,0:T(8,128)(2,1)S(1)}, bf16[4,56,1024]{2,1,0:T(8,128)(2,1)S(1)}, u32[]{:S(2)}, u32[]{:S(2)}) collective-permute-start(bf16[4,56,1024]{2,1,0:T(8,128)(2,1)S(1)} %bitcast.51), channel_id=1, source_target_pairs={{0,1},{1,0},{2,3},{3,2},{4,5},{5,4},{6,7},{7,6},{8,9},{9,8},{10,11... | collective-permute-start | bytes 1376264 | tf_op jit(solution)/shard_map/ppermute | solution.py:37
  104.9 10.9 %all-gather.1 = bf16[224,1024]{1,0:T(8,128)(2,1)S(1)} all-gather(bf16[56,1024]{1,0:T(8,128)(2,1)S(1)} %collective-permute-done.1), channel_id=3, replica_groups=mesh['layer'=4,'quarter'=4,'y'=4,'half'=2,'x'=4,'core'=2] {'y'}, dimensions={0}, use_global_device_ids=true | all-gather | bytes 573440 | tf_op jit(solution)/shard_map/all_gather | solution.py:38
  116.5 1.2 convolution_convert_fusion.1
  117.7 12.9 %all_to_all.20 = bf16[4,112,896]{2,1,0:T(8,128)(2,1)S(1)} all-to-all(bf16[4,112,896]{2,1,0:T(8,128)(2,1)S(1)} %bitcast.55), channel_id=1, replica_groups=mesh['layer'=4,'quarter'=4,'y'=4,'half'=2,'x'=4,'core'=2] {'x'}, dimensions={0} | all-to-all | bytes 1605632 | tf_op jit(solution)/shard_map/all_to_all | solution.py:22
  130.8 11.9 %all_gather.27 = bf16[448,896]{1,0:T(8,128)(2,1)S(1)} all-gather(bf16[112,896]{1,0:T(8,128)(2,1)S(1)} %reduce_sum.33), channel_id=1, replica_groups=mesh['layer'=4,'quarter'=4,'y'=4,'half'=2,'x'=4,'core'=2] {'x'}, dimensions={0}, use_global_device_ids=true | all-gather | bytes 1003520 | tf_op jit(solution)/shard_map/all_gather | solution.py:48
  142.7 3.6 %convolution_convert_fusion = bf16[448,1024]{1,0:T(8,128)(2,1)} fusion(bf16[448,896]{1,0:T(8,128)(2,1)S(1)} %all_gather.27, bf16[896,1024]{1,0:T(8,128)(2,1)} %bitcast.48), kind=kOutput, calls=%fused_computation.4 | convolution fusion | flops 822542336 | bytes 3555328 | tf_op jit(solution)/shard_map/dot_general | solution.py:14
  146.2 3.5 %all-to-all-start.2 = ((bf16[4,112,1024]{2,1,0:T(8,128)(2,1)}), bf16[4,112,1024]{2,1,0:T(8,128)(2,1)S(1)}, u32[]{:S(2)}, u32[]{:S(2)}) async-start(bf16[4,112,1024]{2,1,0:T(8,128)(2,1)} %bitcast.54), calls=%async_computation.2 | async-start | bytes 1835008 | tf_op jit(solution)/shard_map/all_to_all | solution.py:22
  150.5 1.4 mul.57
  151.9 6.9 %all-to-all-done.2 = bf16[4,112,1024]{2,1,0:T(8,128)(2,1)S(1)} async-done(((bf16[4,112,1024]{2,1,0:T(8,128)(2,1)}), bf16[4,112,1024]{2,1,0:T(8,128)(2,1)S(1)}, u32[]{:S(2)}, u32[]{:S(2)}) %all-to-all-start.2) | async-done | bytes 917536 | tf_op jit(solution)/shard_map/all_to_all | solution.py:22
  159.6 11.2 %all_gather.28 = bf16[448,1024]{1,0:T(8,128)(2,1)S(1)} all-gather(bf16[112,1024]{1,0:T(8,128)(2,1)} %reduce_sum.34), channel_id=1, replica_groups=mesh['layer'=4,'quarter'=4,'y'=4,'half'=2,'x'=4,'core'=2] {'y'}, dimensions={0}, use_global_device_ids=true | all-gather | bytes 1146880 | tf_op jit(solution)/shard_map/all_gather | solution.py:51
  170.9 0.9 slice_convert_fusion
  172.8 10.8 %collective-permute-start.3 = (bf16[4,112,512]{2,1,0:T(8,128)(2,1)S(1)}, bf16[4,112,512]{2,1,0:T(8,128)(2,1)S(1)}, u32[]{:S(2)}, u32[]{:S(2)}) collective-permute-start(bf16[4,112,512]{2,1,0:T(8,128)(2,1)S(1)} %select_convert_fusion), channel_id=1, source_target_pairs={{0,1},{1,0},{2,3},{3,2},{4,5},{5,4},{6,7},{7,6},{8,9},{9,8},{10,11... | collective-permute-start | bytes 1376264 | tf_op jit(solution)/shard_map/ppermute | solution.py:63
  183.7 1.4 collective-permute-done.3
  185.1 1.0 add_convert_fusion
  186.1 3.5 %all-to-all-start.3 = ((bf16[4,112,512]{2,1,0:T(8,128)(2,1)}), bf16[4,112,512]{2,1,0:T(8,128)(2,1)S(1)}, u32[]{:S(2)}, u32[]{:S(2)}) async-start(bf16[4,112,512]{2,1,0:T(8,128)(2,1)} %add_convert_fusion), calls=%async_computation.3 | async-start | bytes 917504 | tf_op jit(solution)/shard_map/all_to_all | solution.py:22
  189.7 12.7 %all-to-all-done.3 = bf16[4,112,512]{2,1,0:T(8,128)(2,1)S(1)} async-done(((bf16[4,112,512]{2,1,0:T(8,128)(2,1)}), bf16[4,112,512]{2,1,0:T(8,128)(2,1)S(1)}, u32[]{:S(2)}, u32[]{:S(2)}) %all-to-all-start.3) | async-done | bytes 458784 | tf_op jit(solution)/shard_map/all_to_all | solution.py:22
  (33 shorter events, 5.1 us)
Async XLA Ops:
  1.7 9.7 %all-to-all-start = ((bf16[4,14,1024]{2,1,0:T(8,128)(2,1)}), bf16[4,14,1024]{2,1,0:T(8,128)(2,1)S(1)}, u32[]{:S(2)}, u32[]{:S(2)}) async-start(bf16[4,14,1024]{2,1,0:T(8,128)(2,1)} %bitcast.42), calls=%async_computation | async-start | bytes 262144 | tf_op jit(solution)/shard_map/all_to_all | solution.py:22
  11.4 74.6 %collective-permute-start.1 = (bf16[56,1024]{1,0:T(8,128)(2,1)S(1)}, bf16[56,1024]{1,0:T(8,128)(2,1)S(1)}, u32[]{:S(2)}, u32[]{:S(2)}) collective-permute-start(bf16[56,1024]{1,0:T(8,128)(2,1)S(1)} %reshape.83), channel_id=1, source_target_pairs={{0,8},{8,0},{1,9},{9,1},{2,10},{10,2},{3,11},{11,3},{4,12},{12,4},... | collective-permute-start | bytes 344072 | tf_op jit(solution)/shard_map/ppermute | solution.py:32
  67.9 48.0 %collective-permute-start = (bf16[4,56,1024]{2,1,0:T(8,128)(2,1)S(1)}, bf16[4,56,1024]{2,1,0:T(8,128)(2,1)S(1)}, u32[]{:S(2)}, u32[]{:S(2)}) collective-permute-start(bf16[4,56,1024]{2,1,0:T(8,128)(2,1)S(1)} %all_gather.22), channel_id=1, source_target_pairs={{0,1},{1,0},{2,3},{3,2},{4,5},{5,4},{6,7},{7,6},{8,9},{9,8},{10,11... | collective-permute-start | bytes 1376264 | tf_op jit(solution)/shard_map/ppermute | solution.py:37
  98.3 17.7 %collective-permute-start.2 = (bf16[4,56,1024]{2,1,0:T(8,128)(2,1)S(1)}, bf16[4,56,1024]{2,1,0:T(8,128)(2,1)S(1)}, u32[]{:S(2)}, u32[]{:S(2)}) collective-permute-start(bf16[4,56,1024]{2,1,0:T(8,128)(2,1)S(1)} %bitcast.51), channel_id=1, source_target_pairs={{0,1},{1,0},{2,3},{3,2},{4,5},{5,4},{6,7},{7,6},{8,9},{9,8},{10,11... | collective-permute-start | bytes 1376264 | tf_op jit(solution)/shard_map/ppermute | solution.py:37
  116.5 1.2 copy-start
  146.2 12.5 %all-to-all-start.2 = ((bf16[4,112,1024]{2,1,0:T(8,128)(2,1)}), bf16[4,112,1024]{2,1,0:T(8,128)(2,1)S(1)}, u32[]{:S(2)}, u32[]{:S(2)}) async-start(bf16[4,112,1024]{2,1,0:T(8,128)(2,1)} %bitcast.54), calls=%async_computation.2 | async-start | bytes 1835008 | tf_op jit(solution)/shard_map/all_to_all | solution.py:22
  171.8 0.7 copy-start.1
  172.8 12.3 %collective-permute-start.3 = (bf16[4,112,512]{2,1,0:T(8,128)(2,1)S(1)}, bf16[4,112,512]{2,1,0:T(8,128)(2,1)S(1)}, u32[]{:S(2)}, u32[]{:S(2)}) collective-permute-start(bf16[4,112,512]{2,1,0:T(8,128)(2,1)S(1)} %select_convert_fusion), channel_id=1, source_target_pairs={{0,1},{1,0},{2,3},{3,2},{4,5},{5,4},{6,7},{7,6},{8,9},{9,8},{10,11... | collective-permute-start | bytes 1376264 | tf_op jit(solution)/shard_map/ppermute | solution.py:63
  186.1 16.3 %all-to-all-start.3 = ((bf16[4,112,512]{2,1,0:T(8,128)(2,1)}), bf16[4,112,512]{2,1,0:T(8,128)(2,1)S(1)}, u32[]{:S(2)}, u32[]{:S(2)}) async-start(bf16[4,112,512]{2,1,0:T(8,128)(2,1)} %add_convert_fusion), calls=%async_computation.3 | async-start | bytes 917504 | tf_op jit(solution)/shard_map/all_to_all | solution.py:22

commit v3 on v1

v3 whole, which is shorter than its diff:
```python
import math

import jax
import jax.numpy as jnp
from jax import lax
from jax.sharding import Mesh, PartitionSpec as P

AXES = ("layer", "quarter", "y", "half", "x", "core")
SWAP = [(0, 1), (1, 0)]
A1, A2, A3 = 3.4445, -4.775, 2.0315


def dot(lhs, rhs, dims):
    return lax.dot_general(lhs, rhs, (dims, ((), ())), preferred_element_type=jnp.float32)


def total(blocks):
    return jnp.sum(blocks.astype(jnp.float32), 0)


def exchange(blocks, axis):
    return lax.all_to_all(blocks, axis, 0, 0, tiled=True)


def spread(block, axis):
    copies = jnp.broadcast_to(block[None], (4,) + block.shape)
    return exchange(copies, axis)


def ordered(core, mine, other):
    return jnp.where(core == 0, mine, other), jnp.where(core == 0, other, mine)


def shards(momentum):
    bf16 = jnp.bfloat16
    _, m, k = momentum.shape
    nx, ny, nq, nc = 4, 4, 4, 2
    w = k // nx
    h = w // 2
    n = nx * m
    core = lax.axis_index("core")
    own = exchange(momentum[0].reshape(m, nx, w).transpose(1, 0, 2), "x").reshape(n, w)
    other = lax.ppermute(own, "half", SWAP)

    both = jnp.stack([own, other])
    block = spread(both, "quarter")
    left = lax.all_gather(both, "y", axis=0).reshape(ny * 2 * n, w)
    block, left = lax.optimization_barrier((block, left))
    block = jnp.stack(ordered(core, block, lax.ppermute(block, "core", SWAP)), 2)
    right = block.transpose(1, 0, 2, 3, 4).reshape(2 * nq * nc * n, w)

    term = dot(left, right, ((1,), (1,))).astype(bf16)
    mine = total(exchange(term.reshape(nx, 2 * n, 16 * n), "x")).astype(bf16)
    gram = lax.all_gather(mine, "x", axis=0, tiled=True)
    narrow = gram[:, : 8 * n]
    narrow = jnp.concatenate([narrow, lax.ppermute(narrow, "core", SWAP)], 0)

    term = dot(gram, right, ((1,), (0,))).astype(bf16)
    first = total(exchange(term.reshape(ny, 2 * n, w), "y")).astype(bf16)
    keep, send = ordered(core, first[:, :h], first[:, h:])
    first = jnp.stack([keep, lax.ppermute(send, "core", SWAP)])
    firsts = lax.all_gather(first, "y", axis=1).reshape(nc * ny * 2 * n, h)

    term = dot(narrow, firsts, ((0,), (0,))).astype(bf16)
    second = total(exchange(term.reshape(nq, nc * n, h), "quarter"))
    first = jnp.concatenate(ordered(core, first[0, :n], first[1, :n]), 0)
    tile = lax.dynamic_slice(
        right.reshape(2 * nq, nc * n, w), (lax.axis_index("quarter"), 0, core * h), (1, nc * n, h)
    )[0]
    mixed = A1 * tile.astype(jnp.float32) + A2 * first.astype(jnp.float32) + A3 * second
    mixed = math.sqrt(max(256 * m, k)) * mixed
    mixed = mixed.reshape(nc, nx, m, h).transpose(1, 0, 2, 3).reshape(nc * n, h)
    return mixed.astype(bf16)[None]


def solution(mesh):
    fine = Mesh(mesh.devices.reshape(-1, 4, 4, 2, 4, 2), AXES)
    return jax.shard_map(
        shards,
        mesh=fine,
        in_specs=(P(("layer", "quarter"), ("y", "half", "x", "core"), None),),
        out_specs=P(("layer", "quarter"), ("y", "half"), ("x", "core")),
        check_vma=False,
    )
```

time: 211 us -> 169 us (0.80)
  the two profiles are of different devices: /device:TPU:1 before, /device:TPU:8 now
where the time goes in v3:
time: 169 us; the launch traced here: 168 us
  blocking collectives  81.4 us (48%)
  starting transfers between devices  53.2 us (31%)
  waiting for transfers between devices  23.1 us (14%)
  local copies, waits for them, and re-layouts  4.04 us (2%)
  matrix products  3.71 us (2%)
  other arithmetic  2.53 us (1%)
    all_to_all x3, blocking collectives, exchange(): return lax.all_to_all(blocks, axis, 0, 0, tiled=True)  38.9 us
    ppermute x1, starting transfers between devices, shards(): other = lax.ppermute(own, 'half', SWAP)  29 us
    all_to_all x2, starting transfers between devices, exchange(): return lax.all_to_all(blocks, axis, 0, 0, tiled=True)  18 us
    all_to_all x2, waiting for transfers between devices, exchange(): return lax.all_to_all(blocks, axis, 0, 0, tiled=True)  17.2 us
    all_gather x1, blocking collectives, shards(): left = lax.all_gather(both, 'y', axis=0).reshape(ny * 2 * n, w)  14.5 us
    all_gather x1, blocking collectives, shards(): gram = lax.all_gather(mine, 'x', axis=0, tiled=True)  14.4 us
    all_gather x1, blocking collectives, shards(): firsts = lax.all_gather(first, 'y', axis=1).reshape(nc * ny * 2 * n, h)  13.6 us
    dot_general x3, matrix products, dot(): lax.dot_general(lhs, rhs, (dims, ((), ())), preferred_element_type=jnp.fl...  3.71 us
  transfers between devices with their start and end apart: 6, of which 4 were waited for; matrix products, arithmetic and copies ran while one was open for 0% of the time, Pallas kernels for 0%

profile of v3, /device:TPU:8, one launch (start us, length us, event | category | flops | bytes accessed | tf_op | source)
XLA Modules:
  0.0 168.2 jit_solution(8332820298442322784)
XLA Ops:
  0.0 1.0 reshape_squeeze.3
  1.0 10.1 %all_to_all.25 = bf16[4,14,1024]{2,1,0:T(8,128)(2,1)S(1)} all-to-all(bf16[4,14,1024]{2,1,0:T(8,128)(2,1)S(1)} %bitcast.41), channel_id=1, replica_groups=mesh['layer'=4,'quarter'=4,'y'=4,'half'=2,'x'=4,'core'=2] {'x'}, dimensions={0} | all-to-all | bytes 229376 | tf_op jit(solution)/shard_map/all_to_all | solution.py:22
  11.2 29.0 %collective-permute-start = (bf16[56,1024]{1,0:T(8,128)(2,1)S(1)}, bf16[56,1024]{1,0:T(8,128)(2,1)S(1)}, u32[]{:S(2)}, u32[]{:S(2)}) collective-permute-start(bf16[56,1024]{1,0:T(8,128)(2,1)S(1)} %reshape.50), channel_id=1, source_target_pairs={{0,8},{8,0},{1,9},{9,1},{2,10},{10,2},{3,11},{11,3},{4,12},{12,4},... | collective-permute-start | bytes 344072 | tf_op jit(solution)/shard_map/ppermute | solution.py:43
  40.2 3.4 %collective-permute-done = bf16[56,1024]{1,0:T(8,128)(2,1)S(1)} collective-permute-done((bf16[56,1024]{1,0:T(8,128)(2,1)S(1)}, bf16[56,1024]{1,0:T(8,128)(2,1)S(1)}, u32[]{:S(2)}, u32[]{:S(2)}) %collective-permute-start) | collective-permute-done | bytes 114720 | tf_op jit(solution)/shard_map/ppermute | solution.py:43
  43.6 1.1 broadcast_in_dim.4
  44.7 14.5 %all-to-all-start.1 = ((bf16[4,2,56,1024]{3,2,1,0:T(8,128)(2,1)}), bf16[4,2,56,1024]{3,2,1,0:T(8,128)(2,1)S(1)}, u32[]{:S(2)}, u32[]{:S(2)}) async-start(bf16[4,2,56,1024]{3,2,1,0:T(8,128)(2,1)} %broadcast_in_dim.4), calls=%async_computation.1 | async-start | bytes 1835008 | tf_op jit(solution)/shard_map/all_to_all | solution.py:22
  59.2 14.5 %all-gather = bf16[8,56,1024]{2,1,0:T(8,128)(2,1)} all-gather(bf16[2,56,1024]{2,1,0:T(8,128)(2,1)S(1)} %pad_maximum_fusion.1), channel_id=2, replica_groups=mesh['layer'=4,'quarter'=4,'y'=4,'half'=2,'x'=4,'core'=2] {'y'}, dimensions={0}, use_global_device_ids=true | all-gather | bytes 1146880 | tf_op jit(solution)/shard_map/all_gather | solution.py:47
  73.7 5.9 %all-to-all-done.1 = bf16[4,2,56,1024]{3,2,1,0:T(8,128)(2,1)S(1)} async-done(((bf16[4,2,56,1024]{3,2,1,0:T(8,128)(2,1)}), bf16[4,2,56,1024]{3,2,1,0:T(8,128)(2,1)S(1)}, u32[]{:S(2)}, u32[]{:S(2)}) %all-to-all-start.1) | async-done | bytes 917536 | tf_op jit(solution)/shard_map/all_to_all | solution.py:22
  79.7 1.9 %collective-permute-start.1 = (bf16[4,2,56,1024]{3,2,0,1:T(8,128)(2,1)S(1)}, bf16[4,2,56,1024]{3,2,0,1:T(8,128)(2,1)S(1)}, u32[]{:S(2)}, u32[]{:S(2)}) collective-permute-start(bf16[4,2,56,1024]{3,2,0,1:T(8,128)(2,1)S(1)} %copy.7), channel_id=1, source_target_pairs={{0,1},{1,0},{2,3},{3,2},{4,5},{5,4},{6,7},{7,6},{8,9},{9,8},{10,11... | collective-permute-start | bytes 2752520 | tf_op jit(solution)/shard_map/ppermute | solution.py:49
  81.6 2.4 %collective-permute-done.1 = bf16[4,2,56,1024]{3,2,0,1:T(8,128)(2,1)S(1)} collective-permute-done((bf16[4,2,56,1024]{3,2,0,1:T(8,128)(2,1)S(1)}, bf16[4,2,56,1024]{3,2,0,1:T(8,128)(2,1)S(1)}, u32[]{:S(2)}, u32[]{:S(2)}) %collective-permute-start.1) | collective-permute-done | bytes 917536 | tf_op jit(solution)/shard_map/ppermute | solution.py:49
  84.4 1.0 copy-done
  85.4 1.1 convolution_convert_fusion.1
  86.5 15.4 %all_to_all.26 = bf16[4,112,896]{2,1,0:T(8,128)(2,1)S(1)} all-to-all(bf16[4,112,896]{2,1,0:T(8,128)(2,1)S(1)} %bitcast.40), channel_id=1, replica_groups=mesh['layer'=4,'quarter'=4,'y'=4,'half'=2,'x'=4,'core'=2] {'x'}, dimensions={0} | all-to-all | bytes 1605632 | tf_op jit(solution)/shard_map/all_to_all | solution.py:22
  102.1 14.4 %all_gather.14 = bf16[448,896]{1,0:T(8,128)(2,1)S(1)} all-gather(bf16[112,896]{1,0:T(8,128)(2,1)S(1)} %reduce_sum.33), channel_id=1, replica_groups=mesh['layer'=4,'quarter'=4,'y'=4,'half'=2,'x'=4,'core'=2] {'x'}, dimensions={0}, use_global_device_ids=true | all-gather | bytes 1003520 | tf_op jit(solution)/shard_map/all_gather | solution.py:54
  116.4 1.1 convolution_convert_fusion
  117.6 13.4 %all_to_all.27 = bf16[4,112,1024]{2,1,0:T(8,128)(2,1)S(1)} all-to-all(bf16[4,112,1024]{2,1,0:T(8,128)(2,1)S(1)} %bitcast.37), channel_id=1, replica_groups=mesh['layer'=4,'quarter'=4,'y'=4,'half'=2,'x'=4,'core'=2] {'y'}, dimensions={0} | all-to-all | bytes 1835008 | tf_op jit(solution)/shard_map/all_to_all | solution.py:22
  131.0 0.9 reduce_sum.34
  131.9 1.0 select_bitcast_fusion.2
  132.9 1.9 %collective-permute-start.2 = (bf16[112,512]{1,0:T(8,128)(2,1)S(1)}, bf16[112,512]{1,0:T(8,128)(2,1)S(1)}, u32[]{:S(2)}, u32[]{:S(2)}) collective-permute-start(bf16[112,512]{1,0:T(8,128)(2,1)S(1)} %get-tuple-element.14), channel_id=1, source_target_pairs={{0,1},{1,0},{2,3},{3,2},{4,5},{5,4},{6,7},{7,6},{8,9},{9,8},{10,11... | collective-permute-start | bytes 344072 | tf_op jit(solution)/shard_map/ppermute | solution.py:61
  134.8 2.4 %collective-permute-start.3 = (bf16[448,448]{1,0:T(8,128)(2,1)S(1)}, bf16[448,448]{1,0:T(8,128)(2,1)S(1)}, u32[]{:S(2)}, u32[]{:S(2)}) collective-permute-start(bf16[448,448]{1,0:T(8,128)(2,1)S(1)} %slice.24), channel_id=1, source_target_pairs={{0,1},{1,0},{2,3},{3,2},{4,5},{5,4},{6,7},{7,6},{8,9},{9,8},{10,11... | collective-permute-start | bytes 1204232 | tf_op jit(solution)/shard_map/ppermute | solution.py:56
  137.3 13.6 %all-gather.1 = bf16[2,448,512]{2,1,0:T(8,128)(2,1)S(1)} all-gather(bf16[2,112,512]{2,1,0:T(8,128)(2,1)S(1)} %pad_maximum_fusion.2), channel_id=3, replica_groups=mesh['layer'=4,'quarter'=4,'y'=4,'half'=2,'x'=4,'core'=2] {'y'}, dimensions={1}, use_global_device_ids=true | all-gather | bytes 1146880 | tf_op jit(solution)/shard_map/all_gather | solution.py:62
  150.9 1.4 convolution_convert_fusion.2
  152.3 3.5 %all-to-all-start.4 = ((bf16[4,112,512]{2,1,0:T(8,128)(2,1)}), bf16[4,112,512]{2,1,0:T(8,128)(2,1)S(1)}, u32[]{:S(2)}, u32[]{:S(2)}) async-start(bf16[4,112,512]{2,1,0:T(8,128)(2,1)} %bitcast.16), calls=%async_computation.4 | async-start | bytes 917504 | tf_op jit(solution)/shard_map/all_to_all | solution.py:22
  155.9 11.3 %all-to-all-done.4 = bf16[4,112,512]{2,1,0:T(8,128)(2,1)S(1)} async-done(((bf16[4,112,512]{2,1,0:T(8,128)(2,1)}), bf16[4,112,512]{2,1,0:T(8,128)(2,1)S(1)}, u32[]{:S(2)}, u32[]{:S(2)}) %all-to-all-start.4) | async-done | bytes 458784 | tf_op jit(solution)/shard_map/all_to_all | solution.py:22
  (24 shorter events, 1.7 us)
Async XLA Ops:
  11.2 32.4 %collective-permute-start = (bf16[56,1024]{1,0:T(8,128)(2,1)S(1)}, bf16[56,1024]{1,0:T(8,128)(2,1)S(1)}, u32[]{:S(2)}, u32[]{:S(2)}) collective-permute-start(bf16[56,1024]{1,0:T(8,128)(2,1)S(1)} %reshape.50), channel_id=1, source_target_pairs={{0,8},{8,0},{1,9},{9,1},{2,10},{10,2},{3,11},{11,3},{4,12},{12,4},... | collective-permute-start | bytes 344072 | tf_op jit(solution)/shard_map/ppermute | solution.py:43
  44.7 34.9 %all-to-all-start.1 = ((bf16[4,2,56,1024]{3,2,1,0:T(8,128)(2,1)}), bf16[4,2,56,1024]{3,2,1,0:T(8,128)(2,1)S(1)}, u32[]{:S(2)}, u32[]{:S(2)}) async-start(bf16[4,2,56,1024]{3,2,1,0:T(8,128)(2,1)} %broadcast_in_dim.4), calls=%async_computation.1 | async-start | bytes 1835008 | tf_op jit(solution)/shard_map/all_to_all | solution.py:22
  79.7 4.4 %collective-permute-start.1 = (bf16[4,2,56,1024]{3,2,0,1:T(8,128)(2,1)S(1)}, bf16[4,2,56,1024]{3,2,0,1:T(8,128)(2,1)S(1)}, u32[]{:S(2)}, u32[]{:S(2)}) collective-permute-start(bf16[4,2,56,1024]{3,2,0,1:T(8,128)(2,1)S(1)} %copy.7), channel_id=1, source_target_pairs={{0,1},{1,0},{2,3},{3,2},{4,5},{5,4},{6,7},{7,6},{8,9},{9,8},{10,11... | collective-permute-start | bytes 2752520 | tf_op jit(solution)/shard_map/ppermute | solution.py:49
  84.2 1.2 copy-start
  132.9 4.4 %collective-permute-start.2 = (bf16[112,512]{1,0:T(8,128)(2,1)S(1)}, bf16[112,512]{1,0:T(8,128)(2,1)S(1)}, u32[]{:S(2)}, u32[]{:S(2)}) collective-permute-start(bf16[112,512]{1,0:T(8,128)(2,1)S(1)} %get-tuple-element.14), channel_id=1, source_target_pairs={{0,1},{1,0},{2,3},{3,2},{4,5},{5,4},{6,7},{7,6},{8,9},{9,8},{10,11... | collective-permute-start | bytes 344072 | tf_op jit(solution)/shard_map/ppermute | solution.py:61
  134.8 16.0 %collective-permute-start.3 = (bf16[448,448]{1,0:T(8,128)(2,1)S(1)}, bf16[448,448]{1,0:T(8,128)(2,1)S(1)}, u32[]{:S(2)}, u32[]{:S(2)}) collective-permute-start(bf16[448,448]{1,0:T(8,128)(2,1)S(1)} %slice.24), channel_id=1, source_target_pairs={{0,1},{1,0},{2,3},{3,2},{4,5},{5,4},{6,7},{7,6},{8,9},{9,8},{10,11... | collective-permute-start | bytes 1204232 | tf_op jit(solution)/shard_map/ppermute | solution.py:56
  152.3 15.0 %all-to-all-start.4 = ((bf16[4,112,512]{2,1,0:T(8,128)(2,1)}), bf16[4,112,512]{2,1,0:T(8,128)(2,1)S(1)}, u32[]{:S(2)}, u32[]{:S(2)}) async-start(bf16[4,112,512]{2,1,0:T(8,128)(2,1)} %bitcast.16), calls=%async_computation.4 | async-start | bytes 917504 | tf_op jit(solution)/shard_map/all_to_all | solution.py:22

commit v4 on v3

--- a/solution.py
+++ b/solution.py
@@ -39,10 +39,9 @@
     h = w // 2
     n = nx * m
     core = lax.axis_index("core")
-    own = exchange(momentum[0].reshape(m, nx, w).transpose(1, 0, 2), "x").reshape(n, w)
-    other = lax.ppermute(own, "half", SWAP)
-
-    both = jnp.stack([own, other])
+    rows = momentum[0].reshape(m, nx, w).transpose(1, 0, 2)
+    rows = exchange(jnp.concatenate([rows, rows], 0), ("half", "x")).reshape(2, n, w)
+    both = jnp.stack(ordered(lax.axis_index("half"), rows[0], rows[1]))
     block = spread(both, "quarter")
     left = lax.all_gather(both, "y", axis=0).reshape(ny * 2 * n, w)
     block, left = lax.optimization_barrier((block, left))

time: 169 us -> 191 us (1.13)
  waiting for transfers between devices: 23.1 us -> 46.2 us
  blocking collectives: 81.4 us -> 71.5 us
  starting transfers between devices: 53.2 us -> 61.1 us
    all_to_all x2 -> x3, starting transfers between devices: 18 us -> 54.9 us  [exchange(): return lax.all_to_all(blocks, axis, 0, 0, tiled=True)]
    ppermute x1 -> x0, starting transfers between devices: 29 us -> none  [shards(): other = lax.ppermute(own, 'half', SWAP)]
    all_to_all x2 -> x3, waiting for transfers between devices: 17.2 us -> 43.8 us  [exchange(): return lax.all_to_all(blocks, axis, 0, 0, tiled=True)]
    all_to_all x3 -> x2, blocking collectives: 38.9 us -> 29.1 us  [exchange(): return lax.all_to_all(blocks, axis, 0, 0, tiled=True)]
    ppermute x1 -> x0, waiting for transfers between devices: 3.41 us -> none  [shards(): other = lax.ppermute(own, 'half', SWAP)]
where the time goes in v4:
time: 191 us; the launch traced here: 190 us
  blocking collectives  71.5 us (37%)
  starting transfers between devices  61.1 us (32%)
  waiting for transfers between devices  46.2 us (24%)
  local copies, waits for them, and re-layouts  4.06 us (2%)
  matrix products  3.7 us (2%)
  other arithmetic  3.24 us (2%)
    all_to_all x3, starting transfers between devices, exchange(): return lax.all_to_all(blocks, axis, 0, 0, tiled=True)  54.9 us
    all_to_all x3, waiting for transfers between devices, exchange(): return lax.all_to_all(blocks, axis, 0, 0, tiled=True)  43.8 us
    all_to_all x2, blocking collectives, exchange(): return lax.all_to_all(blocks, axis, 0, 0, tiled=True)  29.1 us
    all_gather x1, blocking collectives, shards(): left = lax.all_gather(both, 'y', axis=0).reshape(ny * 2 * n, w)  14.5 us
    all_gather x1, blocking collectives, shards(): gram = lax.all_gather(mine, 'x', axis=0, tiled=True)  14.3 us
    all_gather x1, blocking collectives, shards(): firsts = lax.all_gather(first, 'y', axis=1).reshape(nc * ny * 2 * n, h)  13.6 us
  transfers between devices with their start and end apart: 6, of which 4 were waited for; matrix products, arithmetic and copies ran while one was open for 0% of the time, Pallas kernels for 0%

profile of v4, /device:TPU:8, one launch (start us, length us, event | category | flops | bytes accessed | tf_op | source)
XLA Modules:
  0.0 190.1 jit_solution(12811702787717858423)
XLA Ops:
  0.0 1.0 reshape_squeeze.3
  1.0 0.7 pad_maximum_fusion.1
  1.8 30.8 %all-to-all-start = ((bf16[8,14,1024]{2,1,0:T(8,128)(2,1)}), bf16[8,14,1024]{2,1,0:T(8,128)(2,1)S(1)}, u32[]{:S(2)}, u32[]{:S(2)}) async-start(bf16[8,14,1024]{2,1,0:T(8,128)(2,1)} %pad_maximum_fusion.1), calls=%async_computation | async-start | bytes 524288 | tf_op jit(solution)/shard_map/all_to_all | solution.py:22
  32.6 26.6 %all-to-all-done = bf16[8,14,1024]{2,1,0:T(8,128)(2,1)S(1)} async-done(((bf16[8,14,1024]{2,1,0:T(8,128)(2,1)}), bf16[8,14,1024]{2,1,0:T(8,128)(2,1)S(1)}, u32[]{:S(2)}, u32[]{:S(2)}) %all-to-all-start) | async-done | bytes 229408 | tf_op jit(solution)/shard_map/all_to_all | solution.py:22
  59.3 1.1 broadcast_in_dim.4
  60.4 20.6 %all-to-all-start.1 = ((bf16[4,2,56,1024]{3,2,1,0:T(8,128)(2,1)}), bf16[4,2,56,1024]{3,2,1,0:T(8,128)(2,1)S(1)}, u32[]{:S(2)}, u32[]{:S(2)}) async-start(bf16[4,2,56,1024]{3,2,1,0:T(8,128)(2,1)} %broadcast_in_dim.4), calls=%async_computation.1 | async-start | bytes 1835008 | tf_op jit(solution)/shard_map/all_to_all | solution.py:22
  81.0 14.5 %all-gather = bf16[8,56,1024]{2,1,0:T(8,128)(2,1)} all-gather(bf16[2,56,1024]{2,1,0:T(8,128)(2,1)S(1)} %constant_dynamic-update-slice_fusion), channel_id=2, replica_groups=mesh['layer'=4,'quarter'=4,'y'=4,'half'=2,'x'=4,'core'=2] {'y'}, dimensions={0}, use_global_device_ids=true | all-gather | bytes 1146880 | tf_op jit(solution)/shard_map/all_gather | solution.py:46
  95.5 5.9 %all-to-all-done.1 = bf16[4,2,56,1024]{3,2,1,0:T(8,128)(2,1)S(1)} async-done(((bf16[4,2,56,1024]{3,2,1,0:T(8,128)(2,1)}), bf16[4,2,56,1024]{3,2,1,0:T(8,128)(2,1)S(1)}, u32[]{:S(2)}, u32[]{:S(2)}) %all-to-all-start.1) | async-done | bytes 917536 | tf_op jit(solution)/shard_map/all_to_all | solution.py:22
  101.5 1.9 %collective-permute-start = (bf16[4,2,56,1024]{3,2,0,1:T(8,128)(2,1)S(1)}, bf16[4,2,56,1024]{3,2,0,1:T(8,128)(2,1)S(1)}, u32[]{:S(2)}, u32[]{:S(2)}) collective-permute-start(bf16[4,2,56,1024]{3,2,0,1:T(8,128)(2,1)S(1)} %copy.7), channel_id=1, source_target_pairs={{0,1},{1,0},{2,3},{3,2},{4,5},{5,4},{6,7},{7,6},{8,9},{9,8},{10,11... | collective-permute-start | bytes 2752520 | tf_op jit(solution)/shard_map/ppermute | solution.py:48
  103.4 2.4 %collective-permute-done = bf16[4,2,56,1024]{3,2,0,1:T(8,128)(2,1)S(1)} collective-permute-done((bf16[4,2,56,1024]{3,2,0,1:T(8,128)(2,1)S(1)}, bf16[4,2,56,1024]{3,2,0,1:T(8,128)(2,1)S(1)}, u32[]{:S(2)}, u32[]{:S(2)}) %collective-permute-start) | collective-permute-done | bytes 917536 | tf_op jit(solution)/shard_map/ppermute | solution.py:48
  106.1 1.0 copy-done
  107.1 1.1 convolution_convert_fusion.1
  108.3 15.7 %all_to_all.25 = bf16[4,112,896]{2,1,0:T(8,128)(2,1)S(1)} all-to-all(bf16[4,112,896]{2,1,0:T(8,128)(2,1)S(1)} %bitcast.39), channel_id=1, replica_groups=mesh['layer'=4,'quarter'=4,'y'=4,'half'=2,'x'=4,'core'=2] {'x'}, dimensions={0} | all-to-all | bytes 1605632 | tf_op jit(solution)/shard_map/all_to_all | solution.py:22
  124.1 14.3 %all_gather.14 = bf16[448,896]{1,0:T(8,128)(2,1)S(1)} all-gather(bf16[112,896]{1,0:T(8,128)(2,1)S(1)} %reduce_sum.33), channel_id=1, replica_groups=mesh['layer'=4,'quarter'=4,'y'=4,'half'=2,'x'=4,'core'=2] {'x'}, dimensions={0}, use_global_device_ids=true | all-gather | bytes 1003520 | tf_op jit(solution)/shard_map/all_gather | solution.py:53
  138.4 1.1 convolution_convert_fusion
  139.5 13.4 %all_to_all.26 = bf16[4,112,1024]{2,1,0:T(8,128)(2,1)S(1)} all-to-all(bf16[4,112,1024]{2,1,0:T(8,128)(2,1)S(1)} %bitcast.36), channel_id=1, replica_groups=mesh['layer'=4,'quarter'=4,'y'=4,'half'=2,'x'=4,'core'=2] {'y'}, dimensions={0} | all-to-all | bytes 1835008 | tf_op jit(solution)/shard_map/all_to_all | solution.py:22
  152.9 0.9 reduce_sum.34
  153.8 1.0 select_bitcast_fusion.2
  154.8 1.9 %collective-permute-start.1 = (bf16[112,512]{1,0:T(8,128)(2,1)S(1)}, bf16[112,512]{1,0:T(8,128)(2,1)S(1)}, u32[]{:S(2)}, u32[]{:S(2)}) collective-permute-start(bf16[112,512]{1,0:T(8,128)(2,1)S(1)} %get-tuple-element.16), channel_id=1, source_target_pairs={{0,1},{1,0},{2,3},{3,2},{4,5},{5,4},{6,7},{7,6},{8,9},{9,8},{10,11... | collective-permute-start | bytes 344072 | tf_op jit(solution)/shard_map/ppermute | solution.py:60
  156.8 2.4 %collective-permute-start.2 = (bf16[448,448]{1,0:T(8,128)(2,1)S(1)}, bf16[448,448]{1,0:T(8,128)(2,1)S(1)}, u32[]{:S(2)}, u32[]{:S(2)}) collective-permute-start(bf16[448,448]{1,0:T(8,128)(2,1)S(1)} %slice.36), channel_id=1, source_target_pairs={{0,1},{1,0},{2,3},{3,2},{4,5},{5,4},{6,7},{7,6},{8,9},{9,8},{10,11... | collective-permute-start | bytes 1204232 | tf_op jit(solution)/shard_map/ppermute | solution.py:55
  159.2 13.6 %all-gather.1 = bf16[2,448,512]{2,1,0:T(8,128)(2,1)S(1)} all-gather(bf16[2,112,512]{2,1,0:T(8,128)(2,1)S(1)} %pad_maximum_fusion.2), channel_id=3, replica_groups=mesh['layer'=4,'quarter'=4,'y'=4,'half'=2,'x'=4,'core'=2] {'y'}, dimensions={1}, use_global_device_ids=true | all-gather | bytes 1146880 | tf_op jit(solution)/shard_map/all_gather | solution.py:61
  172.8 1.4 convolution_convert_fusion.2
  174.2 3.5 %all-to-all-start.4 = ((bf16[4,112,512]{2,1,0:T(8,128)(2,1)}), bf16[4,112,512]{2,1,0:T(8,128)(2,1)S(1)}, u32[]{:S(2)}, u32[]{:S(2)}) async-start(bf16[4,112,512]{2,1,0:T(8,128)(2,1)} %bitcast.15), calls=%async_computation.4 | async-start | bytes 917504 | tf_op jit(solution)/shard_map/all_to_all | solution.py:22
  177.9 11.3 %all-to-all-done.4 = bf16[4,112,512]{2,1,0:T(8,128)(2,1)S(1)} async-done(((bf16[4,112,512]{2,1,0:T(8,128)(2,1)}), bf16[4,112,512]{2,1,0:T(8,128)(2,1)S(1)}, u32[]{:S(2)}, u32[]{:S(2)}) %all-to-all-start.4) | async-done | bytes 458784 | tf_op jit(solution)/shard_map/all_to_all | solution.py:22
  (26 shorter events, 1.7 us)
Async XLA Ops:
  1.8 57.4 %all-to-all-start = ((bf16[8,14,1024]{2,1,0:T(8,128)(2,1)}), bf16[8,14,1024]{2,1,0:T(8,128)(2,1)S(1)}, u32[]{:S(2)}, u32[]{:S(2)}) async-start(bf16[8,14,1024]{2,1,0:T(8,128)(2,1)} %pad_maximum_fusion.1), calls=%async_computation | async-start | bytes 524288 | tf_op jit(solution)/shard_map/all_to_all | solution.py:22
  60.4 41.0 %all-to-all-start.1 = ((bf16[4,2,56,1024]{3,2,1,0:T(8,128)(2,1)}), bf16[4,2,56,1024]{3,2,1,0:T(8,128)(2,1)S(1)}, u32[]{:S(2)}, u32[]{:S(2)}) async-start(bf16[4,2,56,1024]{3,2,1,0:T(8,128)(2,1)} %broadcast_in_dim.4), calls=%async_computation.1 | async-start | bytes 1835008 | tf_op jit(solution)/shard_map/all_to_all | solution.py:22
  101.5 4.4 %collective-permute-start = (bf16[4,2,56,1024]{3,2,0,1:T(8,128)(2,1)S(1)}, bf16[4,2,56,1024]{3,2,0,1:T(8,128)(2,1)S(1)}, u32[]{:S(2)}, u32[]{:S(2)}) collective-permute-start(bf16[4,2,56,1024]{3,2,0,1:T(8,128)(2,1)S(1)} %copy.7), channel_id=1, source_target_pairs={{0,1},{1,0},{2,3},{3,2},{4,5},{5,4},{6,7},{7,6},{8,9},{9,8},{10,11... | collective-permute-start | bytes 2752520 | tf_op jit(solution)/shard_map/ppermute | solution.py:48
  105.9 1.2 copy-start
  154.8 4.4 %collective-permute-start.1 = (bf16[112,512]{1,0:T(8,128)(2,1)S(1)}, bf16[112,512]{1,0:T(8,128)(2,1)S(1)}, u32[]{:S(2)}, u32[]{:S(2)}) collective-permute-start(bf16[112,512]{1,0:T(8,128)(2,1)S(1)} %get-tuple-element.16), channel_id=1, source_target_pairs={{0,1},{1,0},{2,3},{3,2},{4,5},{5,4},{6,7},{7,6},{8,9},{9,8},{10,11... | collective-permute-start | bytes 344072 | tf_op jit(solution)/shard_map/ppermute | solution.py:60
  156.8 16.0 %collective-permute-start.2 = (bf16[448,448]{1,0:T(8,128)(2,1)S(1)}, bf16[448,448]{1,0:T(8,128)(2,1)S(1)}, u32[]{:S(2)}, u32[]{:S(2)}) collective-permute-start(bf16[448,448]{1,0:T(8,128)(2,1)S(1)} %slice.36), channel_id=1, source_target_pairs={{0,1},{1,0},{2,3},{3,2},{4,5},{5,4},{6,7},{7,6},{8,9},{9,8},{10,11... | collective-permute-start | bytes 1204232 | tf_op jit(solution)/shard_map/ppermute | solution.py:55
  174.2 15.0 %all-to-all-start.4 = ((bf16[4,112,512]{2,1,0:T(8,128)(2,1)}), bf16[4,112,512]{2,1,0:T(8,128)(2,1)S(1)}, u32[]{:S(2)}, u32[]{:S(2)}) async-start(bf16[4,112,512]{2,1,0:T(8,128)(2,1)} %bitcast.15), calls=%async_computation.4 | async-start | bytes 917504 | tf_op jit(solution)/shard_map/all_to_all | solution.py:22

commit v5 on v3

--- a/solution.py
+++ b/solution.py
@@ -51,15 +51,17 @@
 
     term = dot(left, right, ((1,), (1,))).astype(bf16)
     mine = total(exchange(term.reshape(nx, 2 * n, 16 * n), "x")).astype(bf16)
-    gram = lax.all_gather(mine, "x", axis=0, tiled=True)
+    gram = spread(mine, "x").reshape(nx * 2 * n, 16 * n)
     narrow = gram[:, : 8 * n]
-    narrow = jnp.concatenate([narrow, lax.ppermute(narrow, "core", SWAP)], 0)
+    narrow = jnp.stack([narrow.reshape(ny, 2 * n, 8 * n), lax.ppermute(narrow, "core", SWAP).reshape(ny, 2 * n, 8 * n)], 1)
+    narrow = narrow.reshape(ny * nc * 2 * n, 8 * n)
 
     term = dot(gram, right, ((1,), (0,))).astype(bf16)
-    first = total(exchange(term.reshape(ny, 2 * n, w), "y")).astype(bf16)
-    keep, send = ordered(core, first[:, :h], first[:, h:])
-    first = jnp.stack([keep, lax.ppermute(send, "core", SWAP)])
-    firsts = lax.all_gather(first, "y", axis=1).reshape(nc * ny * 2 * n, h)
+    terms, narrow = lax.optimization_barrier((exchange(term.reshape(ny, 2 * n, w), "y"), narrow))
+    keep, send = ordered(core, terms[..., :h], terms[..., h:])
+    send = lax.ppermute(total(send).astype(bf16), "core", SWAP)
+    first = jnp.stack([total(keep).astype(bf16), send])
+    firsts = spread(first, "y").reshape(nc * ny * 2 * n, h)
 
     term = dot(narrow, firsts, ((0,), (0,))).astype(bf16)
     second = total(exchange(term.reshape(nq, nc * n, h), "quarter"))

time: 169 us -> 175 us (1.036)
  the two profiles are of different devices: /device:TPU:8 before, /device:TPU:1 now
where the time goes in v5:
time: 175 us
  blocking collectives  65.8 us (38%)
  starting transfers between devices  64.1 us (37%)
  waiting for transfers between devices  31.7 us (18%)
  local copies, waits for them, and re-layouts  5.18 us (3%)
  matrix products  4.61 us (3%)
  other arithmetic  3.04 us (2%)
    all_to_all x4, blocking collectives, exchange(): return lax.all_to_all(blocks, axis, 0, 0, tiled=True)  53.6 us
    ppermute x1, starting transfers between devices, shards(): other = lax.ppermute(own, 'half', SWAP)  28.7 us
    all_to_all x3, waiting for transfers between devices, exchange(): return lax.all_to_all(blocks, axis, 0, 0, tiled=True)  24.3 us
    all_to_all x3, starting transfers between devices, exchange(): return lax.all_to_all(blocks, axis, 0, 0, tiled=True)  21.7 us
    all_gather x1, blocking collectives, shards(): left = lax.all_gather(both, 'y', axis=0).reshape(ny * 2 * n, w)  12.2 us
    ppermute x1, starting transfers between devices, shards(): send = lax.ppermute(total(send).astype(bf16), 'core', SWAP)  5.53 us
    dot_general x3, matrix products, dot(): lax.dot_general(lhs, rhs, (dims, ((), ())), preferred_element_type=jnp.fl...  4.61 us
    ppermute x1, starting transfers between devices, shards(): lax.ppermute(narrow, 'core', SWAP).reshape(ny, 2 * n, 8 * n)  4.31 us
  transfers between devices with their start and end apart: 7, of which 7 were waited for; matrix products, arithmetic and copies ran while one was open for 2% of the time, Pallas kernels for 0%

profile of v5, /device:TPU:1, one launch (start us, length us, event | category | flops | bytes accessed | tf_op | source)
XLA Modules:
  0.0 174.6 jit_solution(4398527082543023098)
XLA Ops:
  1.0 9.5 %all_to_all.35 = bf16[4,14,1024]{2,1,0:T(8,128)(2,1)S(1)} all-to-all(bf16[4,14,1024]{2,1,0:T(8,128)(2,1)S(1)} %bitcast.50), channel_id=1, replica_groups=mesh['layer'=4,'quarter'=4,'y'=4,'half'=2,'x'=4,'core'=2] {'x'}, dimensions={0} | all-to-all | bytes 229376 | tf_op jit(solution)/shard_map/all_to_all | solution.py:22
  10.6 28.7 %collective-permute-start = (bf16[56,1024]{1,0:T(8,128)(2,1)S(1)}, bf16[56,1024]{1,0:T(8,128)(2,1)S(1)}, u32[]{:S(2)}, u32[]{:S(2)}) collective-permute-start(bf16[56,1024]{1,0:T(8,128)(2,1)S(1)} %reshape.58), channel_id=1, source_target_pairs={{0,8},{8,0},{1,9},{9,1},{2,10},{10,2},{3,11},{11,3},{4,12},{12,4},... | collective-permute-start | bytes 344072 | tf_op jit(solution)/shard_map/ppermute | solution.py:43
  39.3 2.8 %collective-permute-done = bf16[56,1024]{1,0:T(8,128)(2,1)S(1)} collective-permute-done((bf16[56,1024]{1,0:T(8,128)(2,1)S(1)}, bf16[56,1024]{1,0:T(8,128)(2,1)S(1)}, u32[]{:S(2)}, u32[]{:S(2)}) %collective-permute-start) | collective-permute-done | bytes 114720 | tf_op jit(solution)/shard_map/ppermute | solution.py:43
  42.1 1.0 broadcast_in_dim.8
  43.2 14.1 %all-to-all-start.1 = ((bf16[4,2,56,1024]{3,2,1,0:T(8,128)(2,1)}), bf16[4,2,56,1024]{3,2,1,0:T(8,128)(2,1)S(1)}, u32[]{:S(2)}, u32[]{:S(2)}) async-start(bf16[4,2,56,1024]{3,2,1,0:T(8,128)(2,1)} %broadcast_in_dim.8), calls=%async_computation.1 | async-start | bytes 1835008 | tf_op jit(solution)/shard_map/all_to_all | solution.py:22
  57.2 12.2 %all-gather = bf16[8,56,1024]{2,1,0:T(8,128)(2,1)S(1)} all-gather(bf16[2,56,1024]{2,1,0:T(8,128)(2,1)S(1)} %pad_maximum_fusion.2), channel_id=2, replica_groups=mesh['layer'=4,'quarter'=4,'y'=4,'half'=2,'x'=4,'core'=2] {'y'}, dimensions={0}, use_global_device_ids=true | all-gather | bytes 1146880 | tf_op jit(solution)/shard_map/all_gather | solution.py:47
  69.4 9.7 %all-to-all-done.1 = bf16[4,2,56,1024]{3,2,1,0:T(8,128)(2,1)S(1)} async-done(((bf16[4,2,56,1024]{3,2,1,0:T(8,128)(2,1)}), bf16[4,2,56,1024]{3,2,1,0:T(8,128)(2,1)S(1)}, u32[]{:S(2)}, u32[]{:S(2)}) %all-to-all-start.1) | async-done | bytes 917536 | tf_op jit(solution)/shard_map/all_to_all | solution.py:22
  79.3 3.8 %collective-permute-start.1 = (bf16[4,2,56,1024]{3,2,0,1:T(8,128)(2,1)S(1)}, bf16[4,2,56,1024]{3,2,0,1:T(8,128)(2,1)}, u32[]{:S(2)}, u32[]{:S(2)}) collective-permute-start(bf16[4,2,56,1024]{3,2,0,1:T(8,128)(2,1)S(1)} %copy.11), channel_id=1, source_target_pairs={{0,1},{1,0},{2,3},{3,2},{4,5},{5,4},{6,7},{7,6},{8,9},{9,8},{10,11... | collective-permute-start | bytes 2752520 | tf_op jit(solution)/shard_map/ppermute | solution.py:49
  83.1 2.2 %collective-permute-done.1 = bf16[4,2,56,1024]{3,2,0,1:T(8,128)(2,1)} collective-permute-done((bf16[4,2,56,1024]{3,2,0,1:T(8,128)(2,1)S(1)}, bf16[4,2,56,1024]{3,2,0,1:T(8,128)(2,1)}, u32[]{:S(2)}, u32[]{:S(2)}) %collective-permute-start.1) | collective-permute-done | bytes 917536 | tf_op jit(solution)/shard_map/ppermute | solution.py:49
  85.3 1.3 select_bitcast_fusion.1
  86.8 1.1 convolution_convert_fusion.1
  87.9 14.6 %all_to_all.36 = bf16[4,112,896]{2,1,0:T(8,128)(2,1)S(1)} all-to-all(bf16[4,112,896]{2,1,0:T(8,128)(2,1)S(1)} %bitcast.47), channel_id=1, replica_groups=mesh['layer'=4,'quarter'=4,'y'=4,'half'=2,'x'=4,'core'=2] {'x'}, dimensions={0} | all-to-all | bytes 1605632 | tf_op jit(solution)/shard_map/all_to_all | solution.py:22
  102.7 13.7 %all_to_all.37 = bf16[4,112,896]{2,1,0:T(8,128)(2,1)S(1)} all-to-all(bf16[4,112,896]{2,1,0:T(8,128)(2,1)S(1)} %broadcast_in_dim.10), channel_id=1, replica_groups=mesh['layer'=4,'quarter'=4,'y'=4,'half'=2,'x'=4,'core'=2] {'x'}, dimensions={0} | all-to-all | bytes 1605632 | tf_op jit(solution)/shard_map/all_to_all | solution.py:22
  116.4 2.0 %convolution_convert_fusion = bf16[448,1024]{1,0:T(8,128)(2,1)} fusion(bf16[448,896]{1,0:T(8,128)(2,1)S(1)} %bitcast.42, bf16[896,1024]{1,0:T(8,128)(2,1)S(1)} %bitcast.40), kind=kOutput, calls=%fused_computation.1 | convolution fusion | flops 822542336 | bytes 3555328 | tf_op jit(solution)/shard_map/dot_general | solution.py:14
  118.4 4.2 %all-to-all-start.4 = ((bf16[4,112,1024]{2,1,0:T(8,128)(2,1)}), bf16[4,112,1024]{2,1,0:T(8,128)(2,1)S(1)}, u32[]{:S(2)}, u32[]{:S(2)}) async-start(bf16[4,112,1024]{2,1,0:T(8,128)(2,1)} %bitcast.11), calls=%async_computation.4 | async-start | bytes 1835008 | tf_op jit(solution)/shard_map/all_to_all | solution.py:22
  122.7 4.3 %collective-permute-start.2 = (bf16[448,448]{1,0:T(8,128)(2,1)S(1)}, bf16[448,448]{1,0:T(8,128)(2,1)S(1)}, u32[]{:S(2)}, u32[]{:S(2)}) collective-permute-start(bf16[448,448]{1,0:T(8,128)(2,1)S(1)} %slice.20), channel_id=1, source_target_pairs={{0,1},{1,0},{2,3},{3,2},{4,5},{5,4},{6,7},{7,6},{8,9},{9,8},{10,11... | collective-permute-start | bytes 1204232 | tf_op jit(solution)/shard_map/ppermute | solution.py:56
  127.0 1.4 collective-permute-done.2
  128.5 1.3 copy.14
  130.6 3.1 %all-to-all-done.4 = bf16[4,112,1024]{2,1,0:T(8,128)(2,1)S(1)} async-done(((bf16[4,112,1024]{2,1,0:T(8,128)(2,1)}), bf16[4,112,1024]{2,1,0:T(8,128)(2,1)S(1)}, u32[]{:S(2)}, u32[]{:S(2)}) %all-to-all-start.4) | async-done | bytes 917536 | tf_op jit(solution)/shard_map/all_to_all | solution.py:22
  133.9 5.5 %collective-permute-start.3 = (bf16[112,512]{1,0:T(8,128)(2,1)S(1)}, bf16[112,512]{1,0:T(8,128)(2,1)S(1)}, u32[]{:S(2)}, u32[]{:S(2)}) collective-permute-start(bf16[112,512]{1,0:T(8,128)(2,1)S(1)} %get-tuple-element.14), channel_id=1, source_target_pairs={{0,1},{1,0},{2,3},{3,2},{4,5},{5,4},{6,7},{7,6},{8,9},{9,8},{10,11... | collective-permute-start | bytes 344072 | tf_op jit(solution)/shard_map/ppermute | solution.py:62
  140.4 15.9 %all_to_all.38 = bf16[4,2,112,512]{3,2,1,0:T(8,128)(2,1)S(1)} all-to-all(bf16[4,2,112,512]{3,2,1,0:T(8,128)(2,1)S(1)} %broadcast_in_dim.11), channel_id=1, replica_groups=mesh['layer'=4,'quarter'=4,'y'=4,'half'=2,'x'=4,'core'=2] {'y'}, dimensions={0} | all-to-all | bytes 1835008 | tf_op jit(solution)/shard_map/all_to_all | solution.py:22
  156.3 1.4 convolution_convert_fusion.2
  157.7 3.5 %all-to-all-start.6 = ((bf16[4,112,512]{2,1,0:T(8,128)(2,1)}), bf16[4,112,512]{2,1,0:T(8,128)(2,1)S(1)}, u32[]{:S(2)}, u32[]{:S(2)}) async-start(bf16[4,112,512]{2,1,0:T(8,128)(2,1)} %bitcast.19), calls=%async_computation.6 | async-start | bytes 917504 | tf_op jit(solution)/shard_map/all_to_all | solution.py:22
  162.3 11.5 %all-to-all-done.6 = bf16[4,112,512]{2,1,0:T(8,128)(2,1)S(1)} async-done(((bf16[4,112,512]{2,1,0:T(8,128)(2,1)}), bf16[4,112,512]{2,1,0:T(8,128)(2,1)S(1)}, u32[]{:S(2)}, u32[]{:S(2)}) %all-to-all-start.6) | async-done | bytes 458784 | tf_op jit(solution)/shard_map/all_to_all | solution.py:22
  (29 shorter events, 5.5 us)
Async XLA Ops:
  10.6 31.6 %collective-permute-start = (bf16[56,1024]{1,0:T(8,128)(2,1)S(1)}, bf16[56,1024]{1,0:T(8,128)(2,1)S(1)}, u32[]{:S(2)}, u32[]{:S(2)}) collective-permute-start(bf16[56,1024]{1,0:T(8,128)(2,1)S(1)} %reshape.58), channel_id=1, source_target_pairs={{0,8},{8,0},{1,9},{9,1},{2,10},{10,2},{3,11},{11,3},{4,12},{12,4},... | collective-permute-start | bytes 344072 | tf_op jit(solution)/shard_map/ppermute | solution.py:43
  43.2 36.0 %all-to-all-start.1 = ((bf16[4,2,56,1024]{3,2,1,0:T(8,128)(2,1)}), bf16[4,2,56,1024]{3,2,1,0:T(8,128)(2,1)S(1)}, u32[]{:S(2)}, u32[]{:S(2)}) async-start(bf16[4,2,56,1024]{3,2,1,0:T(8,128)(2,1)} %broadcast_in_dim.8), calls=%async_computation.1 | async-start | bytes 1835008 | tf_op jit(solution)/shard_map/all_to_all | solution.py:22
  79.3 6.0 %collective-permute-start.1 = (bf16[4,2,56,1024]{3,2,0,1:T(8,128)(2,1)S(1)}, bf16[4,2,56,1024]{3,2,0,1:T(8,128)(2,1)}, u32[]{:S(2)}, u32[]{:S(2)}) collective-permute-start(bf16[4,2,56,1024]{3,2,0,1:T(8,128)(2,1)S(1)} %copy.11), channel_id=1, source_target_pairs={{0,1},{1,0},{2,3},{3,2},{4,5},{5,4},{6,7},{7,6},{8,9},{9,8},{10,11... | collective-permute-start | bytes 2752520 | tf_op jit(solution)/shard_map/ppermute | solution.py:49
  86.8 29.6 %copy-start = (bf16[4,2,2,56,1024]{4,3,2,0,1:T(8,128)(2,1)}, bf16[4,2,2,56,1024]{4,3,2,0,1:T(8,128)(2,1)S(1)}, u32[]{:S(2)}) copy-start(bf16[4,2,2,56,1024]{4,3,2,0,1:T(8,128)(2,1)S(1)} %pad_maximum_fusion) | copy-start | bytes 5505028
  118.4 15.2 %all-to-all-start.4 = ((bf16[4,112,1024]{2,1,0:T(8,128)(2,1)}), bf16[4,112,1024]{2,1,0:T(8,128)(2,1)S(1)}, u32[]{:S(2)}, u32[]{:S(2)}) async-start(bf16[4,112,1024]{2,1,0:T(8,128)(2,1)} %bitcast.11), calls=%async_computation.4 | async-start | bytes 1835008 | tf_op jit(solution)/shard_map/all_to_all | solution.py:22
  122.7 5.7 %collective-permute-start.2 = (bf16[448,448]{1,0:T(8,128)(2,1)S(1)}, bf16[448,448]{1,0:T(8,128)(2,1)S(1)}, u32[]{:S(2)}, u32[]{:S(2)}) collective-permute-start(bf16[448,448]{1,0:T(8,128)(2,1)S(1)} %slice.20), channel_id=1, source_target_pairs={{0,1},{1,0},{2,3},{3,2},{4,5},{5,4},{6,7},{7,6},{8,9},{9,8},{10,11... | collective-permute-start | bytes 1204232 | tf_op jit(solution)/shard_map/ppermute | solution.py:56
  133.9 6.5 %collective-permute-start.3 = (bf16[112,512]{1,0:T(8,128)(2,1)S(1)}, bf16[112,512]{1,0:T(8,128)(2,1)S(1)}, u32[]{:S(2)}, u32[]{:S(2)}) collective-permute-start(bf16[112,512]{1,0:T(8,128)(2,1)S(1)} %get-tuple-element.14), channel_id=1, source_target_pairs={{0,1},{1,0},{2,3},{3,2},{4,5},{5,4},{6,7},{7,6},{8,9},{9,8},{10,11... | collective-permute-start | bytes 344072 | tf_op jit(solution)/shard_map/ppermute | solution.py:62
  157.7 16.0 %all-to-all-start.6 = ((bf16[4,112,512]{2,1,0:T(8,128)(2,1)}), bf16[4,112,512]{2,1,0:T(8,128)(2,1)S(1)}, u32[]{:S(2)}, u32[]{:S(2)}) async-start(bf16[4,112,512]{2,1,0:T(8,128)(2,1)} %bitcast.19), calls=%async_computation.6 | async-start | bytes 917504 | tf_op jit(solution)/shard_map/all_to_all | solution.py:22

commit v6 on v3

--- a/solution.py
+++ b/solution.py
@@ -43,30 +43,34 @@
     other = lax.ppermute(own, "half", SWAP)
 
     both = jnp.stack([own, other])
-    block = spread(both, "quarter")
-    left = lax.all_gather(both, "y", axis=0).reshape(ny * 2 * n, w)
-    block, left = lax.optimization_barrier((block, left))
-    block = jnp.stack(ordered(core, block, lax.ppermute(block, "core", SWAP)), 2)
-    right = block.transpose(1, 0, 2, 3, 4).reshape(2 * nq * nc * n, w)
 
-    term = dot(left, right, ((1,), (1,))).astype(bf16)
+    right = spread(both, "quarter").transpose(1, 0, 2, 3).reshape(2 * nq * n, w)
+    line = lax.all_gather(both.reshape(2 * n, w), "y", axis=0)
+    left = jnp.stack(ordered(core, line, lax.ppermute(line, "core", SWAP)), 1)
+    left = left.reshape(ny * nc * 2 * n, w)
+
+    term = dot(right, left, ((1,), (1,))).astype(bf16)
     mine = total(exchange(term.reshape(nx, 2 * n, 16 * n), "x")).astype(bf16)
     gram = lax.all_gather(mine, "x", axis=0, tiled=True)
-    narrow = gram[:, : 8 * n]
-    narrow = jnp.concatenate([narrow, lax.ppermute(narrow, "core", SWAP)], 0)
+    narrow = gram[: nq * n].reshape(nq, n, 16 * n)
+    narrow = jnp.stack(ordered(core, narrow, lax.ppermute(narrow, "core", SWAP)), 1)
+    narrow = narrow.reshape(nq * nc * n, 16 * n)
 
-    term = dot(gram, right, ((1,), (0,))).astype(bf16)
-    first = total(exchange(term.reshape(ny, 2 * n, w), "y")).astype(bf16)
-    keep, send = ordered(core, first[:, :h], first[:, h:])
-    first = jnp.stack([keep, lax.ppermute(send, "core", SWAP)])
-    firsts = lax.all_gather(first, "y", axis=1).reshape(nc * ny * 2 * n, h)
+    keep, send = ordered(core, right[:, :h], right[:, h:])
+    send = dot(gram, send, ((0,), (0,))).astype(bf16)
+    got = lax.ppermute(send, "core", SWAP)
+    keep = dot(gram, keep, ((0,), (0,)))
+    term = (keep + got.astype(jnp.float32)).astype(bf16)
+    term, narrow = lax.optimization_barrier((exchange(term.reshape(ny, 4 * n, h), "y"), narrow))
+    first = total(term).astype(bf16)
+    firsts = lax.all_gather(first, "y", axis=0, tiled=True)
 
-    term = dot(narrow, firsts, ((0,), (0,))).astype(bf16)
+    term = dot(narrow, firsts, ((1,), (0,))).astype(bf16)
     second = total(exchange(term.reshape(nq, nc * n, h), "quarter"))
-    first = jnp.concatenate(ordered(core, first[0, :n], first[1, :n]), 0)
-    tile = lax.dynamic_slice(
-        right.reshape(2 * nq, nc * n, w), (lax.axis_index("quarter"), 0, core * h), (1, nc * n, h)
-    )[0]
+    first = first.reshape(nc, 2, n, h)[:, 0].reshape(nc * n, h)
+    tile = lax.dynamic_index_in_dim(left.reshape(ny, nc, 2, n, w), lax.axis_index("y"), 0, False)
+    tile = tile[:, 0].reshape(nc * n, w)
+    tile = jnp.where(core == 0, tile[:, :h], tile[:, h:])
     mixed = A1 * tile.astype(jnp.float32) + A2 * first.astype(jnp.float32) + A3 * second
     mixed = math.sqrt(max(256 * m, k)) * mixed
     mixed = mixed.reshape(nc, nx, m, h).transpose(1, 0, 2, 3).reshape(nc * n, h)

time: 169 us -> 173 us (1.024)
  blocking collectives: 81.4 us -> 67.7 us
  starting transfers between devices: 53.2 us -> 60.3 us
  waiting for transfers between devices: 23.1 us -> 28.4 us
  other arithmetic: 2.53 us -> 5.3 us
  matrix products: 3.71 us -> 6 us
    all_to_all x3 -> x2, blocking collectives: 38.9 us -> 25.6 us  [exchange(): return lax.all_to_all(blocks, axis, 0, 0, tiled=True)]
    all_to_all x2 -> x3, starting transfers between devices: 18 us -> 25 us  [exchange(): return lax.all_to_all(blocks, axis, 0, 0, tiled=True)]
    all_to_all x2 -> x3, waiting for transfers between devices: 17.2 us -> 22.4 us  [exchange(): return lax.all_to_all(blocks, axis, 0, 0, tiled=True)]
    dot_general x3 -> x4, matrix products: 3.71 us -> 6 us  [dot(): lax.dot_general(lhs, rhs, (dims, ((), ())), preferred_element_type=jnp.fl...]
  transfers between devices with their start and end apart: 6 -> 7, of which waited for: 4 -> 4; matrix products, arithmetic and copies ran while one was open for 0% -> 3% of each run, Pallas kernels for 0% -> 0%
where the time goes in v6:
time: 173 us
  blocking collectives  67.7 us (39%)
  starting transfers between devices  60.3 us (35%)
  waiting for transfers between devices  28.4 us (16%)
  matrix products  6 us (3%)
  other arithmetic  5.3 us (3%)
  local copies, waits for them, and re-layouts  4.79 us (3%)
    ppermute x1, starting transfers between devices, shards(): other = lax.ppermute(own, 'half', SWAP)  29 us
    all_to_all x2, blocking collectives, exchange(): return lax.all_to_all(blocks, axis, 0, 0, tiled=True)  25.6 us
    all_to_all x3, starting transfers between devices, exchange(): return lax.all_to_all(blocks, axis, 0, 0, tiled=True)  25 us
    all_to_all x3, waiting for transfers between devices, exchange(): return lax.all_to_all(blocks, axis, 0, 0, tiled=True)  22.4 us
    all_gather x1, blocking collectives, shards(): gram = lax.all_gather(mine, 'x', axis=0, tiled=True)  14.6 us
    all_gather x1, blocking collectives, shards(): line = lax.all_gather(both.reshape(2 * n, w), 'y', axis=0)  13.8 us
    all_gather x1, blocking collectives, shards(): firsts = lax.all_gather(first, 'y', axis=0, tiled=True)  13.7 us
    dot_general x4, matrix products, dot(): lax.dot_general(lhs, rhs, (dims, ((), ())), preferred_element_type=jnp.fl...  6 us
  transfers between devices with their start and end apart: 7, of which 4 were waited for; matrix products, arithmetic and copies ran while one was open for 3% of the time, Pallas kernels for 0%

profile of v6, /device:TPU:8, one launch (start us, length us, event | category | flops | bytes accessed | tf_op | source)
XLA Modules:
  0.0 172.6 jit_solution(15461836148631983787)
XLA Ops:
  1.0 10.1 %all_to_all.25 = bf16[4,14,1024]{2,1,0:T(8,128)(2,1)S(1)} all-to-all(bf16[4,14,1024]{2,1,0:T(8,128)(2,1)S(1)} %bitcast.61), channel_id=1, replica_groups=mesh['layer'=4,'quarter'=4,'y'=4,'half'=2,'x'=4,'core'=2] {'x'}, dimensions={0} | all-to-all | bytes 229376 | tf_op jit(solution)/shard_map/all_to_all | solution.py:22
  11.2 29.0 %collective-permute-start = (bf16[56,1024]{1,0:T(8,128)(2,1)S(1)}, bf16[56,1024]{1,0:T(8,128)(2,1)S(1)}, u32[]{:S(2)}, u32[]{:S(2)}) collective-permute-start(bf16[56,1024]{1,0:T(8,128)(2,1)S(1)} %reshape.49), channel_id=1, source_target_pairs={{0,8},{8,0},{1,9},{9,1},{2,10},{10,2},{3,11},{11,3},{4,12},{12,4},... | collective-permute-start | bytes 344072 | tf_op jit(solution)/shard_map/ppermute | solution.py:43
  40.2 3.4 %collective-permute-done = bf16[56,1024]{1,0:T(8,128)(2,1)S(1)} collective-permute-done((bf16[56,1024]{1,0:T(8,128)(2,1)S(1)}, bf16[56,1024]{1,0:T(8,128)(2,1)S(1)}, u32[]{:S(2)}, u32[]{:S(2)}) %collective-permute-start) | collective-permute-done | bytes 114720 | tf_op jit(solution)/shard_map/ppermute | solution.py:43
  43.6 1.1 broadcast_in_dim.2
  44.7 14.5 %all-to-all-start.1 = ((bf16[4,2,56,1024]{3,2,1,0:T(8,128)(2,1)}), bf16[4,2,56,1024]{3,2,1,0:T(8,128)(2,1)S(1)}, u32[]{:S(2)}, u32[]{:S(2)}) async-start(bf16[4,2,56,1024]{3,2,1,0:T(8,128)(2,1)} %broadcast_in_dim.2), calls=%async_computation.1 | async-start | bytes 1835008 | tf_op jit(solution)/shard_map/all_to_all | solution.py:22
  59.2 13.8 %all_gather.9 = bf16[4,112,1024]{2,1,0:T(8,128)(2,1)S(1)} all-gather(bf16[1,112,1024]{2,1,0:T(8,128)(2,1)S(1)} %bitcast.49), channel_id=1, replica_groups=mesh['layer'=4,'quarter'=4,'y'=4,'half'=2,'x'=4,'core'=2] {'y'}, dimensions={0}, use_global_device_ids=true | all-gather | bytes 1146880 | tf_op jit(solution)/shard_map/all_gather | solution.py:48
  73.0 1.9 %collective-permute-start.1 = (bf16[4,112,1024]{2,1,0:T(8,128)(2,1)S(1)}, bf16[4,112,1024]{2,1,0:T(8,128)(2,1)}, u32[]{:S(2)}, u32[]{:S(2)}) collective-permute-start(bf16[4,112,1024]{2,1,0:T(8,128)(2,1)S(1)} %all_gather.9), channel_id=1, source_target_pairs={{0,1},{1,0},{2,3},{3,2},{4,5},{5,4},{6,7},{7,6},{8,9},{9,8},{10,11... | collective-permute-start | bytes 2752520 | tf_op jit(solution)/shard_map/ppermute | solution.py:49
  74.9 2.6 %collective-permute-done.1 = bf16[4,112,1024]{2,1,0:T(8,128)(2,1)} collective-permute-done((bf16[4,112,1024]{2,1,0:T(8,128)(2,1)S(1)}, bf16[4,112,1024]{2,1,0:T(8,128)(2,1)}, u32[]{:S(2)}, u32[]{:S(2)}) %collective-permute-start.1) | collective-permute-done | bytes 917536 | tf_op jit(solution)/shard_map/ppermute | solution.py:49
  77.5 1.6 broadcast_select_fusion.1
  79.1 1.4 pad_maximum_fusion
  80.5 1.7 %copy-done.1 = bf16[4,2,112,1024]{3,2,1,0:T(8,128)(2,1)S(1)} copy-done((bf16[4,2,112,1024]{3,2,1,0:T(8,128)(2,1)S(1)}, bf16[4,2,112,1024]{3,2,1,0:T(8,128)(2,1)}, u32[]{:S(2)}) %copy-start.1) | copy-done | bytes 1835032
  82.3 1.1 convolution_convert_fusion.1
  83.5 15.6 %all_to_all.26 = bf16[4,112,896]{2,1,0:T(8,128)(2,1)S(1)} all-to-all(bf16[4,112,896]{2,1,0:T(8,128)(2,1)S(1)} %bitcast.60), channel_id=1, replica_groups=mesh['layer'=4,'quarter'=4,'y'=4,'half'=2,'x'=4,'core'=2] {'x'}, dimensions={0} | all-to-all | bytes 1605632 | tf_op jit(solution)/shard_map/all_to_all | solution.py:22
  99.8 14.6 %all_gather.10 = bf16[448,896]{1,0:T(8,128)(2,1)S(1)} all-gather(bf16[112,896]{1,0:T(8,128)(2,1)} %reduce_sum.33), channel_id=1, replica_groups=mesh['layer'=4,'quarter'=4,'y'=4,'half'=2,'x'=4,'core'=2] {'x'}, dimensions={0}, use_global_device_ids=true | all-gather | bytes 1003520 | tf_op jit(solution)/shard_map/all_gather | solution.py:54
  115.1 1.9 %collective-permute-start.2 = (bf16[896,512]{1,0:T(8,128)(2,1)S(1)}, bf16[896,512]{1,0:T(8,128)(2,1)S(1)}, u32[]{:S(2)}, u32[]{:S(2)}) collective-permute-start(bf16[896,512]{1,0:T(8,128)(2,1)S(1)} %convolution_convert_fusion), channel_id=1, source_target_pairs={{0,1},{1,0},{2,3},{3,2},{4,5},{5,4},{6,7},{7,6},{8,9},{9,8},{10,11... | collective-permute-start | bytes 2752520 | tf_op jit(solution)/shard_map/ppermute | solution.py:61
  117.1 2.4 %collective-permute-start.3 = (bf16[4,56,896]{2,1,0:T(8,128)(2,1)S(1)}, bf16[4,56,896]{2,1,0:T(8,128)(2,1)S(1)}, u32[]{:S(2)}, u32[]{:S(2)}) collective-permute-start(bf16[4,56,896]{2,1,0:T(8,128)(2,1)S(1)} %bitcast.51), channel_id=1, source_target_pairs={{0,1},{1,0},{2,3},{3,2},{4,5},{5,4},{6,7},{7,6},{8,9},{9,8},{10,11... | collective-permute-start | bytes 1204232 | tf_op jit(solution)/shard_map/ppermute | solution.py:56
  119.5 1.6 add_convert_fusion
  121.1 5.4 %all-to-all-start.3 = ((bf16[4,224,512]{2,1,0:T(8,128)(2,1)}), bf16[4,224,512]{2,1,0:T(8,128)(2,1)S(1)}, u32[]{:S(2)}, u32[]{:S(2)}) async-start(bf16[4,224,512]{2,1,0:T(8,128)(2,1)} %bitcast.57), calls=%async_computation.3 | async-start | bytes 1835008 | tf_op jit(solution)/shard_map/all_to_all | solution.py:22
  126.7 1.0 pad_maximum_fusion.1
  127.7 11.7 %all-to-all-done.3 = bf16[4,224,512]{2,1,0:T(8,128)(2,1)S(1)} async-done(((bf16[4,224,512]{2,1,0:T(8,128)(2,1)}), bf16[4,224,512]{2,1,0:T(8,128)(2,1)S(1)}, u32[]{:S(2)}, u32[]{:S(2)}) %all-to-all-start.3) | async-done | bytes 917536 | tf_op jit(solution)/shard_map/all_to_all | solution.py:22
  139.6 13.7 %all_gather.11 = bf16[896,512]{1,0:T(8,128)(2,1)S(1)} all-gather(bf16[224,512]{1,0:T(8,128)(2,1)S(1)} %reduce_sum.34), channel_id=1, replica_groups=mesh['layer'=4,'quarter'=4,'y'=4,'half'=2,'x'=4,'core'=2] {'y'}, dimensions={0}, use_global_device_ids=true | all-gather | bytes 1146880 | tf_op jit(solution)/shard_map/all_gather | solution.py:66
  153.3 2.6 %convolution_convert_fusion.2 = bf16[448,512]{1,0:T(8,128)(2,1)} fusion(bf16[448,896]{1,0:T(8,128)(2,1)} %bitcast.59, bf16[896,512]{1,0:T(8,128)(2,1)S(1)} %all_gather.11), kind=kOutput, calls=%fused_computation.6 | convolution fusion | flops 411271168 | bytes 2179072 | tf_op jit(solution)/shard_map/dot_general | solution.py:14
  155.8 5.1 %all-to-all-start.4 = ((bf16[4,112,512]{2,1,0:T(8,128)(2,1)}), bf16[4,112,512]{2,1,0:T(8,128)(2,1)S(1)}, u32[]{:S(2)}, u32[]{:S(2)}) async-start(bf16[4,112,512]{2,1,0:T(8,128)(2,1)} %bitcast.23), calls=%async_computation.4 | async-start | bytes 917504 | tf_op jit(solution)/shard_map/all_to_all | solution.py:22
  161.0 10.7 %all-to-all-done.4 = bf16[4,112,512]{2,1,0:T(8,128)(2,1)S(1)} async-done(((bf16[4,112,512]{2,1,0:T(8,128)(2,1)}), bf16[4,112,512]{2,1,0:T(8,128)(2,1)S(1)}, u32[]{:S(2)}, u32[]{:S(2)}) %all-to-all-start.4) | async-done | bytes 458784 | tf_op jit(solution)/shard_map/all_to_all | solution.py:22
  (31 shorter events, 4.0 us)
Async XLA Ops:
  11.2 32.4 %collective-permute-start = (bf16[56,1024]{1,0:T(8,128)(2,1)S(1)}, bf16[56,1024]{1,0:T(8,128)(2,1)S(1)}, u32[]{:S(2)}, u32[]{:S(2)}) collective-permute-start(bf16[56,1024]{1,0:T(8,128)(2,1)S(1)} %reshape.49), channel_id=1, source_target_pairs={{0,8},{8,0},{1,9},{9,1},{2,10},{10,2},{3,11},{11,3},{4,12},{12,4},... | collective-permute-start | bytes 344072 | tf_op jit(solution)/shard_map/ppermute | solution.py:43
  44.7 35.8 %all-to-all-start.1 = ((bf16[4,2,56,1024]{3,2,1,0:T(8,128)(2,1)}), bf16[4,2,56,1024]{3,2,1,0:T(8,128)(2,1)S(1)}, u32[]{:S(2)}, u32[]{:S(2)}) async-start(bf16[4,2,56,1024]{3,2,1,0:T(8,128)(2,1)} %broadcast_in_dim.2), calls=%async_computation.1 | async-start | bytes 1835008 | tf_op jit(solution)/shard_map/all_to_all | solution.py:22
  73.0 1.9 %copy-start = (bf16[4,112,1024]{2,1,0:T(8,128)(2,1)}, bf16[4,112,1024]{2,1,0:T(8,128)(2,1)S(1)}, u32[]{:S(2)}) copy-start(bf16[4,112,1024]{2,1,0:T(8,128)(2,1)S(1)} %all_gather.9) | copy-start | bytes 2752516
  73.0 4.5 %collective-permute-start.1 = (bf16[4,112,1024]{2,1,0:T(8,128)(2,1)S(1)}, bf16[4,112,1024]{2,1,0:T(8,128)(2,1)}, u32[]{:S(2)}, u32[]{:S(2)}) collective-permute-start(bf16[4,112,1024]{2,1,0:T(8,128)(2,1)S(1)} %all_gather.9), channel_id=1, source_target_pairs={{0,1},{1,0},{2,3},{3,2},{4,5},{5,4},{6,7},{7,6},{8,9},{9,8},{10,11... | collective-permute-start | bytes 2752520 | tf_op jit(solution)/shard_map/ppermute | solution.py:49
  80.5 1.8 %copy-start.1 = (bf16[4,2,112,1024]{3,2,1,0:T(8,128)(2,1)S(1)}, bf16[4,2,112,1024]{3,2,1,0:T(8,128)(2,1)}, u32[]{:S(2)}) copy-start(bf16[4,2,112,1024]{3,2,1,0:T(8,128)(2,1)} %pad_maximum_fusion) | copy-start | bytes 5505028
  80.5 2.9 %copy-start.2 = (bf16[4,2,56,1024]{3,2,0,1:T(8,128)(2,1)}, bf16[4,2,56,1024]{3,2,0,1:T(8,128)(2,1)S(1)}, u32[]{:S(2)}) copy-start(bf16[4,2,56,1024]{3,2,0,1:T(8,128)(2,1)S(1)} %copy.11) | copy-start | bytes 2752516
  83.5 31.0 %copy-start.3 = (bf16[4,2,56,1024]{3,2,0,1:T(8,128)(2,1)S(1)}, bf16[4,2,56,1024]{3,2,0,1:T(8,128)(2,1)}, u32[]{:S(2)}) copy-start(bf16[4,2,56,1024]{3,2,0,1:T(8,128)(2,1)} %copy-done.2) | copy-start | bytes 2752516
  114.4 5.1 %copy-start.4 = (bf16[4,2,56,1024]{3,2,0,1:T(8,128)(2,1)S(1)}, bf16[4,2,56,1024]{3,2,0,1:T(8,128)(2,1)}, u32[]{:S(2)}) copy-start(bf16[4,2,56,1024]{3,2,0,1:T(8,128)(2,1)} %copy-done.2) | copy-start | bytes 2752516
  115.1 4.4 %collective-permute-start.2 = (bf16[896,512]{1,0:T(8,128)(2,1)S(1)}, bf16[896,512]{1,0:T(8,128)(2,1)S(1)}, u32[]{:S(2)}, u32[]{:S(2)}) collective-permute-start(bf16[896,512]{1,0:T(8,128)(2,1)S(1)} %convolution_convert_fusion), channel_id=1, source_target_pairs={{0,1},{1,0},{2,3},{3,2},{4,5},{5,4},{6,7},{7,6},{8,9},{9,8},{10,11... | collective-permute-start | bytes 2752520 | tf_op jit(solution)/shard_map/ppermute | solution.py:61
  117.1 9.5 %collective-permute-start.3 = (bf16[4,56,896]{2,1,0:T(8,128)(2,1)S(1)}, bf16[4,56,896]{2,1,0:T(8,128)(2,1)S(1)}, u32[]{:S(2)}, u32[]{:S(2)}) collective-permute-start(bf16[4,56,896]{2,1,0:T(8,128)(2,1)S(1)} %bitcast.51), channel_id=1, source_target_pairs={{0,1},{1,0},{2,3},{3,2},{4,5},{5,4},{6,7},{7,6},{8,9},{9,8},{10,11... | collective-permute-start | bytes 1204232 | tf_op jit(solution)/shard_map/ppermute | solution.py:56
  121.1 18.2 %all-to-all-start.3 = ((bf16[4,224,512]{2,1,0:T(8,128)(2,1)}), bf16[4,224,512]{2,1,0:T(8,128)(2,1)S(1)}, u32[]{:S(2)}, u32[]{:S(2)}) async-start(bf16[4,224,512]{2,1,0:T(8,128)(2,1)} %bitcast.57), calls=%async_computation.3 | async-start | bytes 1835008 | tf_op jit(solution)/shard_map/all_to_all | solution.py:22
  155.8 15.9 %all-to-all-start.4 = ((bf16[4,112,512]{2,1,0:T(8,128)(2,1)}), bf16[4,112,512]{2,1,0:T(8,128)(2,1)S(1)}, u32[]{:S(2)}, u32[]{:S(2)}) async-start(bf16[4,112,512]{2,1,0:T(8,128)(2,1)} %bitcast.23), calls=%async_computation.4 | async-start | bytes 917504 | tf_op jit(solution)/shard_map/all_to_all | solution.py:22

commit v7 on v5

--- a/solution.py
+++ b/solution.py
@@ -51,7 +51,7 @@
 
     term = dot(left, right, ((1,), (1,))).astype(bf16)
     mine = total(exchange(term.reshape(nx, 2 * n, 16 * n), "x")).astype(bf16)
-    gram = spread(mine, "x").reshape(nx * 2 * n, 16 * n)
+    gram = lax.all_gather(mine, "x", axis=0, tiled=True)
     narrow = gram[:, : 8 * n]
     narrow = jnp.stack([narrow.reshape(ny, 2 * n, 8 * n), lax.ppermute(narrow, "core", SWAP).reshape(ny, 2 * n, 8 * n)], 1)
     narrow = narrow.reshape(ny * nc * 2 * n, 8 * n)
@@ -61,7 +61,7 @@
     keep, send = ordered(core, terms[..., :h], terms[..., h:])
     send = lax.ppermute(total(send).astype(bf16), "core", SWAP)
     first = jnp.stack([total(keep).astype(bf16), send])
-    firsts = spread(first, "y").reshape(nc * ny * 2 * n, h)
+    firsts = lax.all_gather(first, "y", axis=0).reshape(ny * nc * 2 * n, h)
 
     term = dot(narrow, firsts, ((0,), (0,))).astype(bf16)
     second = total(exchange(term.reshape(nq, nc * n, h), "quarter"))

time: 175 us -> 168 us (0.960)
  the two profiles are of different devices: /device:TPU:1 before, /device:TPU:8 now
where the time goes in v7:
time: 168 us; the launch traced here: 167 us
  blocking collectives  67.4 us (40%)
  starting transfers between devices  57.6 us (34%)
  waiting for transfers between devices  29 us (17%)
  local copies, waits for them, and re-layouts  5.05 us (3%)
  matrix products  4.61 us (3%)
  other arithmetic  3.04 us (2%)
    ppermute x1, starting transfers between devices, shards(): other = lax.ppermute(own, 'half', SWAP)  29 us
    all_to_all x2, blocking collectives, exchange(): return lax.all_to_all(blocks, axis, 0, 0, tiled=True)  25.5 us
    all_to_all x3, starting transfers between devices, exchange(): return lax.all_to_all(blocks, axis, 0, 0, tiled=True)  22.9 us
    all_to_all x3, waiting for transfers between devices, exchange(): return lax.all_to_all(blocks, axis, 0, 0, tiled=True)  19.9 us
    all_gather x1, blocking collectives, shards(): gram = lax.all_gather(mine, 'x', axis=0, tiled=True)  14.4 us
    all_gather x1, blocking collectives, shards(): left = lax.all_gather(both, 'y', axis=0).reshape(ny * 2 * n, w)  13.8 us
    all_gather x1, blocking collectives, shards(): firsts = lax.all_gather(first, 'y', axis=0).reshape(ny * nc * 2 * n, h)  13.7 us
    dot_general x3, matrix products, dot(): lax.dot_general(lhs, rhs, (dims, ((), ())), preferred_element_type=jnp.fl...  4.61 us
  transfers between devices with their start and end apart: 7, of which 7 were waited for; matrix products, arithmetic and copies ran while one was open for 2% of the time, Pallas kernels for 0%

profile of v7, /device:TPU:8, one launch (start us, length us, event | category | flops | bytes accessed | tf_op | source)
XLA Modules:
  0.0 166.9 jit_solution(14499776150738573739)
XLA Ops:
  1.0 10.1 %all_to_all.25 = bf16[4,14,1024]{2,1,0:T(8,128)(2,1)S(1)} all-to-all(bf16[4,14,1024]{2,1,0:T(8,128)(2,1)S(1)} %bitcast.47), channel_id=1, replica_groups=mesh['layer'=4,'quarter'=4,'y'=4,'half'=2,'x'=4,'core'=2] {'x'}, dimensions={0} | all-to-all | bytes 229376 | tf_op jit(solution)/shard_map/all_to_all | solution.py:22
  11.2 29.0 %collective-permute-start = (bf16[56,1024]{1,0:T(8,128)(2,1)S(1)}, bf16[56,1024]{1,0:T(8,128)(2,1)S(1)}, u32[]{:S(2)}, u32[]{:S(2)}) collective-permute-start(bf16[56,1024]{1,0:T(8,128)(2,1)S(1)} %reshape.53), channel_id=1, source_target_pairs={{0,8},{8,0},{1,9},{9,1},{2,10},{10,2},{3,11},{11,3},{4,12},{12,4},... | collective-permute-start | bytes 344072 | tf_op jit(solution)/shard_map/ppermute | solution.py:43
  40.2 3.4 %collective-permute-done = bf16[56,1024]{1,0:T(8,128)(2,1)S(1)} collective-permute-done((bf16[56,1024]{1,0:T(8,128)(2,1)S(1)}, bf16[56,1024]{1,0:T(8,128)(2,1)S(1)}, u32[]{:S(2)}, u32[]{:S(2)}) %collective-permute-start) | collective-permute-done | bytes 114720 | tf_op jit(solution)/shard_map/ppermute | solution.py:43
  44.6 14.5 %all-to-all-start.1 = ((bf16[4,2,56,1024]{3,2,1,0:T(8,128)(2,1)}), bf16[4,2,56,1024]{3,2,1,0:T(8,128)(2,1)S(1)}, u32[]{:S(2)}, u32[]{:S(2)}) async-start(bf16[4,2,56,1024]{3,2,1,0:T(8,128)(2,1)} %broadcast_in_dim.4), calls=%async_computation.1 | async-start | bytes 1835008 | tf_op jit(solution)/shard_map/all_to_all | solution.py:22
  59.2 13.8 %all-gather = bf16[8,56,1024]{2,1,0:T(8,128)(2,1)S(1)} all-gather(bf16[2,56,1024]{2,1,0:T(8,128)(2,1)S(1)} %pad_maximum_fusion.2), channel_id=2, replica_groups=mesh['layer'=4,'quarter'=4,'y'=4,'half'=2,'x'=4,'core'=2] {'y'}, dimensions={0}, use_global_device_ids=true | all-gather | bytes 1146880 | tf_op jit(solution)/shard_map/all_gather | solution.py:47
  72.9 6.6 %all-to-all-done.1 = bf16[4,2,56,1024]{3,2,1,0:T(8,128)(2,1)S(1)} async-done(((bf16[4,2,56,1024]{3,2,1,0:T(8,128)(2,1)}), bf16[4,2,56,1024]{3,2,1,0:T(8,128)(2,1)S(1)}, u32[]{:S(2)}, u32[]{:S(2)}) %all-to-all-start.1) | async-done | bytes 917536 | tf_op jit(solution)/shard_map/all_to_all | solution.py:22
  79.7 1.9 %collective-permute-start.1 = (bf16[4,2,56,1024]{3,2,0,1:T(8,128)(2,1)S(1)}, bf16[4,2,56,1024]{3,2,0,1:T(8,128)(2,1)}, u32[]{:S(2)}, u32[]{:S(2)}) collective-permute-start(bf16[4,2,56,1024]{3,2,0,1:T(8,128)(2,1)S(1)} %copy.11), channel_id=1, source_target_pairs={{0,1},{1,0},{2,3},{3,2},{4,5},{5,4},{6,7},{7,6},{8,9},{9,8},{10,11... | collective-permute-start | bytes 2752520 | tf_op jit(solution)/shard_map/ppermute | solution.py:49
  81.6 2.6 %collective-permute-done.1 = bf16[4,2,56,1024]{3,2,0,1:T(8,128)(2,1)} collective-permute-done((bf16[4,2,56,1024]{3,2,0,1:T(8,128)(2,1)S(1)}, bf16[4,2,56,1024]{3,2,0,1:T(8,128)(2,1)}, u32[]{:S(2)}, u32[]{:S(2)}) %collective-permute-start.1) | collective-permute-done | bytes 917536 | tf_op jit(solution)/shard_map/ppermute | solution.py:49
  84.2 1.3 select_bitcast_fusion.1
  85.7 1.1 convolution_convert_fusion.1
  86.8 15.4 %all_to_all.26 = bf16[4,112,896]{2,1,0:T(8,128)(2,1)S(1)} all-to-all(bf16[4,112,896]{2,1,0:T(8,128)(2,1)S(1)} %bitcast.44), channel_id=1, replica_groups=mesh['layer'=4,'quarter'=4,'y'=4,'half'=2,'x'=4,'core'=2] {'x'}, dimensions={0} | all-to-all | bytes 1605632 | tf_op jit(solution)/shard_map/all_to_all | solution.py:22
  102.4 14.4 %all_gather.14 = bf16[448,896]{1,0:T(8,128)(2,1)S(1)} all-gather(bf16[112,896]{1,0:T(8,128)(2,1)S(1)} %reduce_sum.45), channel_id=1, replica_groups=mesh['layer'=4,'quarter'=4,'y'=4,'half'=2,'x'=4,'core'=2] {'x'}, dimensions={0}, use_global_device_ids=true | all-gather | bytes 1003520 | tf_op jit(solution)/shard_map/all_gather | solution.py:54
  116.7 2.0 %convolution_convert_fusion = bf16[448,1024]{1,0:T(8,128)(2,1)} fusion(bf16[448,896]{1,0:T(8,128)(2,1)S(1)} %all_gather.14, bf16[896,1024]{1,0:T(8,128)(2,1)S(1)} %bitcast.39), kind=kOutput, calls=%fused_computation.1 | convolution fusion | flops 822542336 | bytes 3555328 | tf_op jit(solution)/shard_map/dot_general | solution.py:14
  118.8 4.9 %all-to-all-start.3 = ((bf16[4,112,1024]{2,1,0:T(8,128)(2,1)}), bf16[4,112,1024]{2,1,0:T(8,128)(2,1)S(1)}, u32[]{:S(2)}, u32[]{:S(2)}) async-start(bf16[4,112,1024]{2,1,0:T(8,128)(2,1)} %bitcast.10), calls=%async_computation.3 | async-start | bytes 1835008 | tf_op jit(solution)/shard_map/all_to_all | solution.py:22
  123.7 1.9 %collective-permute-start.2 = (bf16[448,448]{1,0:T(8,128)(2,1)S(1)}, bf16[448,448]{1,0:T(8,128)(2,1)S(1)}, u32[]{:S(2)}, u32[]{:S(2)}) collective-permute-start(bf16[448,448]{1,0:T(8,128)(2,1)S(1)} %slice.20), channel_id=1, source_target_pairs={{0,1},{1,0},{2,3},{3,2},{4,5},{5,4},{6,7},{7,6},{8,9},{9,8},{10,11... | collective-permute-start | bytes 1204232 | tf_op jit(solution)/shard_map/ppermute | solution.py:56
  125.6 1.8 %collective-permute-done.2 = bf16[448,448]{1,0:T(8,128)(2,1)S(1)} collective-permute-done((bf16[448,448]{1,0:T(8,128)(2,1)S(1)}, bf16[448,448]{1,0:T(8,128)(2,1)S(1)}, u32[]{:S(2)}, u32[]{:S(2)}) %collective-permute-start.2) | collective-permute-done | bytes 401440 | tf_op jit(solution)/shard_map/ppermute | solution.py:56
  127.5 1.3 copy.14
  129.6 2.8 %all-to-all-done.3 = bf16[4,112,1024]{2,1,0:T(8,128)(2,1)S(1)} async-done(((bf16[4,112,1024]{2,1,0:T(8,128)(2,1)}), bf16[4,112,1024]{2,1,0:T(8,128)(2,1)S(1)}, u32[]{:S(2)}, u32[]{:S(2)}) %all-to-all-start.3) | async-done | bytes 917536 | tf_op jit(solution)/shard_map/all_to_all | solution.py:22
  132.6 1.9 %collective-permute-start.3 = (bf16[112,512]{1,0:T(8,128)(2,1)S(1)}, bf16[112,512]{1,0:T(8,128)(2,1)S(1)}, u32[]{:S(2)}, u32[]{:S(2)}) collective-permute-start(bf16[112,512]{1,0:T(8,128)(2,1)S(1)} %get-tuple-element.14), channel_id=1, source_target_pairs={{0,1},{1,0},{2,3},{3,2},{4,5},{5,4},{6,7},{7,6},{8,9},{9,8},{10,11... | collective-permute-start | bytes 344072 | tf_op jit(solution)/shard_map/ppermute | solution.py:62
  134.5 1.3 collective-permute-done.3
  135.8 13.7 %all-gather.1 = bf16[8,112,512]{2,1,0:T(8,128)(2,1)S(1)} all-gather(bf16[2,112,512]{2,1,0:T(8,128)(2,1)S(1)} %pad_maximum_fusion.3), channel_id=3, replica_groups=mesh['layer'=4,'quarter'=4,'y'=4,'half'=2,'x'=4,'core'=2] {'y'}, dimensions={0}, use_global_device_ids=true | all-gather | bytes 1146880 | tf_op jit(solution)/shard_map/all_gather | solution.py:64
  149.6 1.4 convolution_convert_fusion.2
  151.0 3.5 %all-to-all-start.4 = ((bf16[4,112,512]{2,1,0:T(8,128)(2,1)}), bf16[4,112,512]{2,1,0:T(8,128)(2,1)S(1)}, u32[]{:S(2)}, u32[]{:S(2)}) async-start(bf16[4,112,512]{2,1,0:T(8,128)(2,1)} %bitcast.18), calls=%async_computation.4 | async-start | bytes 917504 | tf_op jit(solution)/shard_map/all_to_all | solution.py:22
  155.5 10.4 %all-to-all-done.4 = bf16[4,112,512]{2,1,0:T(8,128)(2,1)S(1)} async-done(((bf16[4,112,512]{2,1,0:T(8,128)(2,1)}), bf16[4,112,512]{2,1,0:T(8,128)(2,1)S(1)}, u32[]{:S(2)}, u32[]{:S(2)}) %all-to-all-start.4) | async-done | bytes 458784 | tf_op jit(solution)/shard_map/all_to_all | solution.py:22
  (27 shorter events, 5.5 us)
Async XLA Ops:
  11.2 32.4 %collective-permute-start = (bf16[56,1024]{1,0:T(8,128)(2,1)S(1)}, bf16[56,1024]{1,0:T(8,128)(2,1)S(1)}, u32[]{:S(2)}, u32[]{:S(2)}) collective-permute-start(bf16[56,1024]{1,0:T(8,128)(2,1)S(1)} %reshape.53), channel_id=1, source_target_pairs={{0,8},{8,0},{1,9},{9,1},{2,10},{10,2},{3,11},{11,3},{4,12},{12,4},... | collective-permute-start | bytes 344072 | tf_op jit(solution)/shard_map/ppermute | solution.py:43
  44.6 34.9 %all-to-all-start.1 = ((bf16[4,2,56,1024]{3,2,1,0:T(8,128)(2,1)}), bf16[4,2,56,1024]{3,2,1,0:T(8,128)(2,1)S(1)}, u32[]{:S(2)}, u32[]{:S(2)}) async-start(bf16[4,2,56,1024]{3,2,1,0:T(8,128)(2,1)} %broadcast_in_dim.4), calls=%async_computation.1 | async-start | bytes 1835008 | tf_op jit(solution)/shard_map/all_to_all | solution.py:22
  79.7 4.5 %collective-permute-start.1 = (bf16[4,2,56,1024]{3,2,0,1:T(8,128)(2,1)S(1)}, bf16[4,2,56,1024]{3,2,0,1:T(8,128)(2,1)}, u32[]{:S(2)}, u32[]{:S(2)}) collective-permute-start(bf16[4,2,56,1024]{3,2,0,1:T(8,128)(2,1)S(1)} %copy.11), channel_id=1, source_target_pairs={{0,1},{1,0},{2,3},{3,2},{4,5},{5,4},{6,7},{7,6},{8,9},{9,8},{10,11... | collective-permute-start | bytes 2752520 | tf_op jit(solution)/shard_map/ppermute | solution.py:49
  85.6 31.1 %copy-start = (bf16[4,2,2,56,1024]{4,3,2,0,1:T(8,128)(2,1)}, bf16[4,2,2,56,1024]{4,3,2,0,1:T(8,128)(2,1)S(1)}, u32[]{:S(2)}) copy-start(bf16[4,2,2,56,1024]{4,3,2,0,1:T(8,128)(2,1)S(1)} %pad_maximum_fusion) | copy-start | bytes 5505028
  118.8 13.6 %all-to-all-start.3 = ((bf16[4,112,1024]{2,1,0:T(8,128)(2,1)}), bf16[4,112,1024]{2,1,0:T(8,128)(2,1)S(1)}, u32[]{:S(2)}, u32[]{:S(2)}) async-start(bf16[4,112,1024]{2,1,0:T(8,128)(2,1)} %bitcast.10), calls=%async_computation.3 | async-start | bytes 1835008 | tf_op jit(solution)/shard_map/all_to_all | solution.py:22
  123.7 3.7 %collective-permute-start.2 = (bf16[448,448]{1,0:T(8,128)(2,1)S(1)}, bf16[448,448]{1,0:T(8,128)(2,1)S(1)}, u32[]{:S(2)}, u32[]{:S(2)}) collective-permute-start(bf16[448,448]{1,0:T(8,128)(2,1)S(1)} %slice.20), channel_id=1, source_target_pairs={{0,1},{1,0},{2,3},{3,2},{4,5},{5,4},{6,7},{7,6},{8,9},{9,8},{10,11... | collective-permute-start | bytes 1204232 | tf_op jit(solution)/shard_map/ppermute | solution.py:56
  132.6 3.2 %collective-permute-start.3 = (bf16[112,512]{1,0:T(8,128)(2,1)S(1)}, bf16[112,512]{1,0:T(8,128)(2,1)S(1)}, u32[]{:S(2)}, u32[]{:S(2)}) collective-permute-start(bf16[112,512]{1,0:T(8,128)(2,1)S(1)} %get-tuple-element.14), channel_id=1, source_target_pairs={{0,1},{1,0},{2,3},{3,2},{4,5},{5,4},{6,7},{7,6},{8,9},{9,8},{10,11... | collective-permute-start | bytes 344072 | tf_op jit(solution)/shard_map/ppermute | solution.py:62
  151.0 15.0 %all-to-all-start.4 = ((bf16[4,112,512]{2,1,0:T(8,128)(2,1)}), bf16[4,112,512]{2,1,0:T(8,128)(2,1)S(1)}, u32[]{:S(2)}, u32[]{:S(2)}) async-start(bf16[4,112,512]{2,1,0:T(8,128)(2,1)} %bitcast.18), calls=%async_computation.4 | async-start | bytes 917504 | tf_op jit(solution)/shard_map/all_to_all | solution.py:22

commit v8 on v7

--- a/solution.py
+++ b/solution.py
@@ -40,7 +40,9 @@
     n = nx * m
     core = lax.axis_index("core")
     own = exchange(momentum[0].reshape(m, nx, w).transpose(1, 0, 2), "x").reshape(n, w)
-    other = lax.ppermute(own, "half", SWAP)
+    up = lax.ppermute(own, "half", [(0, 1)])
+    down = lax.ppermute(own, "half", [(1, 0)])
+    other = jnp.where(lax.axis_index("half") == 1, up, down)
 
     both = jnp.stack([own, other])
     block = spread(both, "quarter")

time: 168 us -> 174 us (1.036)
  the two profiles are of different devices: /device:TPU:8 before, /device:TPU:896 now
where the time goes in v8:
time: 174 us; the launch traced here: 173 us
  blocking collectives  69.1 us (40%)
  waiting for transfers between devices  59.9 us (34%)
  starting transfers between devices  31.1 us (18%)
  local copies, waits for them, and re-layouts  5.06 us (3%)
  matrix products  4.64 us (3%)
  other arithmetic  3.06 us (2%)
    all_to_all x2, blocking collectives, exchange(): return lax.all_to_all(blocks, axis, 0, 0, tiled=True)  25.5 us
    all_to_all x3, waiting for transfers between devices, exchange(): return lax.all_to_all(blocks, axis, 0, 0, tiled=True)  21.9 us
    ppermute x1, waiting for transfers between devices, shards(): up = lax.ppermute(own, 'half', [(0, 1)])  20.7 us
    all_gather x1, blocking collectives, shards(): left = lax.all_gather(both, 'y', axis=0).reshape(ny * 2 * n, w)  14.6 us
    all_gather x1, blocking collectives, shards(): firsts = lax.all_gather(first, 'y', axis=0).reshape(ny * nc * 2 * n, h)  14.6 us
    all_to_all x3, starting transfers between devices, exchange(): return lax.all_to_all(blocks, axis, 0, 0, tiled=True)  14.4 us
    all_gather x1, blocking collectives, shards(): gram = lax.all_gather(mine, 'x', axis=0, tiled=True)  14.4 us
    ppermute x1, waiting for transfers between devices, shards(): down = lax.ppermute(own, 'half', [(1, 0)])  11.6 us
  transfers between devices with their start and end apart: 8, of which 8 were waited for; matrix products, arithmetic and copies ran while one was open for 2% of the time, Pallas kernels for 0%

profile of v8, /device:TPU:896, one launch (start us, length us, event | category | flops | bytes accessed | tf_op | source)
XLA Modules:
  0.0 173.0 jit_solution(13108109159818381481)
XLA Ops:
  1.0 10.1 %all_to_all.25 = bf16[4,14,1024]{2,1,0:T(8,128)(2,1)S(1)} all-to-all(bf16[4,14,1024]{2,1,0:T(8,128)(2,1)S(1)} %bitcast.48), channel_id=1, replica_groups=mesh['layer'=4,'quarter'=4,'y'=4,'half'=2,'x'=4,'core'=2] {'x'}, dimensions={0} | all-to-all | bytes 229376 | tf_op jit(solution)/shard_map/all_to_all | solution.py:22
  11.2 9.6 %collective-permute-start.1 = (bf16[56,1024]{1,0:T(8,128)(2,1)S(1)}, bf16[56,1024]{1,0:T(8,128)(2,1)S(1)}, u32[]{:S(2)}, u32[]{:S(2)}) collective-permute-start(bf16[56,1024]{1,0:T(8,128)(2,1)S(1)} %reshape.53), channel_id=1, source_target_pairs={{8,0},{9,1},{10,2},{11,3},{12,4},{13,5},{14,6},{15,7},{24,16},{25,... | collective-permute-start | bytes 344072 | tf_op jit(solution)/shard_map/ppermute | solution.py:44
  20.8 1.3 collective-permute-start
  22.1 11.6 %collective-permute-done.1 = bf16[56,1024]{1,0:T(8,128)(2,1)S(1)} collective-permute-done((bf16[56,1024]{1,0:T(8,128)(2,1)S(1)}, bf16[56,1024]{1,0:T(8,128)(2,1)S(1)}, u32[]{:S(2)}, u32[]{:S(2)}) %collective-permute-start.1) | collective-permute-done | bytes 114720 | tf_op jit(solution)/shard_map/ppermute | solution.py:44
  33.7 20.7 %collective-permute-done = bf16[56,1024]{1,0:T(8,128)(2,1)S(1)} collective-permute-done((bf16[56,1024]{1,0:T(8,128)(2,1)S(1)}, bf16[56,1024]{1,0:T(8,128)(2,1)S(1)}, u32[]{:S(2)}, u32[]{:S(2)}) %collective-permute-start) | collective-permute-done | bytes 114720 | tf_op jit(solution)/shard_map/ppermute | solution.py:43
  55.6 6.1 %all-to-all-start.1 = ((bf16[4,2,56,1024]{3,2,1,0:T(8,128)(2,1)}), bf16[4,2,56,1024]{3,2,1,0:T(8,128)(2,1)S(1)}, u32[]{:S(2)}, u32[]{:S(2)}) async-start(bf16[4,2,56,1024]{3,2,1,0:T(8,128)(2,1)} %broadcast_in_dim.4), calls=%async_computation.1 | async-start | bytes 1835008 | tf_op jit(solution)/shard_map/all_to_all | solution.py:22
  61.6 14.6 %all-gather = bf16[8,56,1024]{2,1,0:T(8,128)(2,1)S(1)} all-gather(bf16[2,56,1024]{2,1,0:T(8,128)(2,1)S(1)} %pad_maximum_fusion.2), channel_id=2, replica_groups=mesh['layer'=4,'quarter'=4,'y'=4,'half'=2,'x'=4,'core'=2] {'y'}, dimensions={0}, use_global_device_ids=true | all-gather | bytes 1146880 | tf_op jit(solution)/shard_map/all_gather | solution.py:49
  76.3 8.2 %all-to-all-done.1 = bf16[4,2,56,1024]{3,2,1,0:T(8,128)(2,1)S(1)} async-done(((bf16[4,2,56,1024]{3,2,1,0:T(8,128)(2,1)}), bf16[4,2,56,1024]{3,2,1,0:T(8,128)(2,1)S(1)}, u32[]{:S(2)}, u32[]{:S(2)}) %all-to-all-start.1) | async-done | bytes 917536 | tf_op jit(solution)/shard_map/all_to_all | solution.py:22
  84.6 1.9 %collective-permute-start.2 = (bf16[4,2,56,1024]{3,2,0,1:T(8,128)(2,1)S(1)}, bf16[4,2,56,1024]{3,2,0,1:T(8,128)(2,1)}, u32[]{:S(2)}, u32[]{:S(2)}) collective-permute-start(bf16[4,2,56,1024]{3,2,0,1:T(8,128)(2,1)S(1)} %copy.11), channel_id=1, source_target_pairs={{0,1},{1,0},{2,3},{3,2},{4,5},{5,4},{6,7},{7,6},{8,9},{9,8},{10,11... | collective-permute-start | bytes 2752520 | tf_op jit(solution)/shard_map/ppermute | solution.py:51
  86.5 2.6 %collective-permute-done.2 = bf16[4,2,56,1024]{3,2,0,1:T(8,128)(2,1)} collective-permute-done((bf16[4,2,56,1024]{3,2,0,1:T(8,128)(2,1)S(1)}, bf16[4,2,56,1024]{3,2,0,1:T(8,128)(2,1)}, u32[]{:S(2)}, u32[]{:S(2)}) %collective-permute-start.2) | collective-permute-done | bytes 917536 | tf_op jit(solution)/shard_map/ppermute | solution.py:51
  89.1 1.3 select_bitcast_fusion.1
  91.7 15.4 %all_to_all.26 = bf16[4,112,896]{2,1,0:T(8,128)(2,1)S(1)} all-to-all(bf16[4,112,896]{2,1,0:T(8,128)(2,1)S(1)} %bitcast.45), channel_id=1, replica_groups=mesh['layer'=4,'quarter'=4,'y'=4,'half'=2,'x'=4,'core'=2] {'x'}, dimensions={0} | all-to-all | bytes 1605632 | tf_op jit(solution)/shard_map/all_to_all | solution.py:22
  107.3 14.4 %all_gather.14 = bf16[448,896]{1,0:T(8,128)(2,1)S(1)} all-gather(bf16[112,896]{1,0:T(8,128)(2,1)S(1)} %reduce_sum.45), channel_id=1, replica_groups=mesh['layer'=4,'quarter'=4,'y'=4,'half'=2,'x'=4,'core'=2] {'x'}, dimensions={0}, use_global_device_ids=true | all-gather | bytes 1003520 | tf_op jit(solution)/shard_map/all_gather | solution.py:56
  121.6 2.1 %convolution_convert_fusion = bf16[448,1024]{1,0:T(8,128)(2,1)} fusion(bf16[448,896]{1,0:T(8,128)(2,1)S(1)} %all_gather.14, bf16[896,1024]{1,0:T(8,128)(2,1)S(1)} %bitcast.40), kind=kOutput, calls=%fused_computation.1 | convolution fusion | flops 822542336 | bytes 3555328 | tf_op jit(solution)/shard_map/dot_general | solution.py:14
  123.7 4.8 %all-to-all-start.3 = ((bf16[4,112,1024]{2,1,0:T(8,128)(2,1)}), bf16[4,112,1024]{2,1,0:T(8,128)(2,1)S(1)}, u32[]{:S(2)}, u32[]{:S(2)}) async-start(bf16[4,112,1024]{2,1,0:T(8,128)(2,1)} %bitcast.10), calls=%async_computation.3 | async-start | bytes 1835008 | tf_op jit(solution)/shard_map/all_to_all | solution.py:22
  128.6 1.9 %collective-permute-start.3 = (bf16[448,448]{1,0:T(8,128)(2,1)S(1)}, bf16[448,448]{1,0:T(8,128)(2,1)S(1)}, u32[]{:S(2)}, u32[]{:S(2)}) collective-permute-start(bf16[448,448]{1,0:T(8,128)(2,1)S(1)} %slice.20), channel_id=1, source_target_pairs={{0,1},{1,0},{2,3},{3,2},{4,5},{5,4},{6,7},{7,6},{8,9},{9,8},{10,11... | collective-permute-start | bytes 1204232 | tf_op jit(solution)/shard_map/ppermute | solution.py:58
  130.5 1.8 %collective-permute-done.3 = bf16[448,448]{1,0:T(8,128)(2,1)S(1)} collective-permute-done((bf16[448,448]{1,0:T(8,128)(2,1)S(1)}, bf16[448,448]{1,0:T(8,128)(2,1)S(1)}, u32[]{:S(2)}, u32[]{:S(2)}) %collective-permute-start.3) | collective-permute-done | bytes 401440 | tf_op jit(solution)/shard_map/ppermute | solution.py:58
  132.4 1.3 copy.14
  134.4 4.3 %all-to-all-done.3 = bf16[4,112,1024]{2,1,0:T(8,128)(2,1)S(1)} async-done(((bf16[4,112,1024]{2,1,0:T(8,128)(2,1)}), bf16[4,112,1024]{2,1,0:T(8,128)(2,1)S(1)}, u32[]{:S(2)}, u32[]{:S(2)}) %all-to-all-start.3) | async-done | bytes 917536 | tf_op jit(solution)/shard_map/all_to_all | solution.py:22
  138.9 1.9 %collective-permute-start.4 = (bf16[112,512]{1,0:T(8,128)(2,1)S(1)}, bf16[112,512]{1,0:T(8,128)(2,1)S(1)}, u32[]{:S(2)}, u32[]{:S(2)}) collective-permute-start(bf16[112,512]{1,0:T(8,128)(2,1)S(1)} %get-tuple-element.14), channel_id=1, source_target_pairs={{0,1},{1,0},{2,3},{3,2},{4,5},{5,4},{6,7},{7,6},{8,9},{9,8},{10,11... | collective-permute-start | bytes 344072 | tf_op jit(solution)/shard_map/ppermute | solution.py:64
  142.1 14.6 %all-gather.1 = bf16[8,112,512]{2,1,0:T(8,128)(2,1)S(1)} all-gather(bf16[2,112,512]{2,1,0:T(8,128)(2,1)S(1)} %pad_maximum_fusion.3), channel_id=3, replica_groups=mesh['layer'=4,'quarter'=4,'y'=4,'half'=2,'x'=4,'core'=2] {'y'}, dimensions={0}, use_global_device_ids=true | all-gather | bytes 1146880 | tf_op jit(solution)/shard_map/all_gather | solution.py:66
  156.7 1.4 convolution_convert_fusion.2
  158.2 3.5 %all-to-all-start.4 = ((bf16[4,112,512]{2,1,0:T(8,128)(2,1)}), bf16[4,112,512]{2,1,0:T(8,128)(2,1)S(1)}, u32[]{:S(2)}, u32[]{:S(2)}) async-start(bf16[4,112,512]{2,1,0:T(8,128)(2,1)} %bitcast.18), calls=%async_computation.4 | async-start | bytes 917504 | tf_op jit(solution)/shard_map/all_to_all | solution.py:22
  162.7 9.4 %all-to-all-done.4 = bf16[4,112,512]{2,1,0:T(8,128)(2,1)S(1)} async-done(((bf16[4,112,512]{2,1,0:T(8,128)(2,1)}), bf16[4,112,512]{2,1,0:T(8,128)(2,1)S(1)}, u32[]{:S(2)}, u32[]{:S(2)}) %all-to-all-start.4) | async-done | bytes 458784 | tf_op jit(solution)/shard_map/all_to_all | solution.py:22
  (30 shorter events, 8.0 us)
Async XLA Ops:
  11.2 22.6 %collective-permute-start.1 = (bf16[56,1024]{1,0:T(8,128)(2,1)S(1)}, bf16[56,1024]{1,0:T(8,128)(2,1)S(1)}, u32[]{:S(2)}, u32[]{:S(2)}) collective-permute-start(bf16[56,1024]{1,0:T(8,128)(2,1)S(1)} %reshape.53), channel_id=1, source_target_pairs={{8,0},{9,1},{10,2},{11,3},{12,4},{13,5},{14,6},{15,7},{24,16},{25,... | collective-permute-start | bytes 344072 | tf_op jit(solution)/shard_map/ppermute | solution.py:44
  20.8 33.7 %collective-permute-start = (bf16[56,1024]{1,0:T(8,128)(2,1)S(1)}, bf16[56,1024]{1,0:T(8,128)(2,1)S(1)}, u32[]{:S(2)}, u32[]{:S(2)}) collective-permute-start(bf16[56,1024]{1,0:T(8,128)(2,1)S(1)} %reshape.53), channel_id=1, source_target_pairs={{0,8},{1,9},{2,10},{3,11},{4,12},{5,13},{6,14},{7,15},{16,24},{17,... | collective-permute-start | bytes 344072 | tf_op jit(solution)/shard_map/ppermute | solution.py:43
  55.6 28.9 %all-to-all-start.1 = ((bf16[4,2,56,1024]{3,2,1,0:T(8,128)(2,1)}), bf16[4,2,56,1024]{3,2,1,0:T(8,128)(2,1)S(1)}, u32[]{:S(2)}, u32[]{:S(2)}) async-start(bf16[4,2,56,1024]{3,2,1,0:T(8,128)(2,1)} %broadcast_in_dim.4), calls=%async_computation.1 | async-start | bytes 1835008 | tf_op jit(solution)/shard_map/all_to_all | solution.py:22
  84.6 4.5 %collective-permute-start.2 = (bf16[4,2,56,1024]{3,2,0,1:T(8,128)(2,1)S(1)}, bf16[4,2,56,1024]{3,2,0,1:T(8,128)(2,1)}, u32[]{:S(2)}, u32[]{:S(2)}) collective-permute-start(bf16[4,2,56,1024]{3,2,0,1:T(8,128)(2,1)S(1)} %copy.11), channel_id=1, source_target_pairs={{0,1},{1,0},{2,3},{3,2},{4,5},{5,4},{6,7},{7,6},{8,9},{9,8},{10,11... | collective-permute-start | bytes 2752520 | tf_op jit(solution)/shard_map/ppermute | solution.py:51
  90.5 31.1 %copy-start = (bf16[4,2,2,56,1024]{4,3,2,0,1:T(8,128)(2,1)}, bf16[4,2,2,56,1024]{4,3,2,0,1:T(8,128)(2,1)S(1)}, u32[]{:S(2)}) copy-start(bf16[4,2,2,56,1024]{4,3,2,0,1:T(8,128)(2,1)S(1)} %pad_maximum_fusion) | copy-start | bytes 5505028
  123.7 15.0 %all-to-all-start.3 = ((bf16[4,112,1024]{2,1,0:T(8,128)(2,1)}), bf16[4,112,1024]{2,1,0:T(8,128)(2,1)S(1)}, u32[]{:S(2)}, u32[]{:S(2)}) async-start(bf16[4,112,1024]{2,1,0:T(8,128)(2,1)} %bitcast.10), calls=%async_computation.3 | async-start | bytes 1835008 | tf_op jit(solution)/shard_map/all_to_all | solution.py:22
  128.6 3.7 %collective-permute-start.3 = (bf16[448,448]{1,0:T(8,128)(2,1)S(1)}, bf16[448,448]{1,0:T(8,128)(2,1)S(1)}, u32[]{:S(2)}, u32[]{:S(2)}) collective-permute-start(bf16[448,448]{1,0:T(8,128)(2,1)S(1)} %slice.20), channel_id=1, source_target_pairs={{0,1},{1,0},{2,3},{3,2},{4,5},{5,4},{6,7},{7,6},{8,9},{9,8},{10,11... | collective-permute-start | bytes 1204232 | tf_op jit(solution)/shard_map/ppermute | solution.py:58
  138.9 3.2 %collective-permute-start.4 = (bf16[112,512]{1,0:T(8,128)(2,1)S(1)}, bf16[112,512]{1,0:T(8,128)(2,1)S(1)}, u32[]{:S(2)}, u32[]{:S(2)}) collective-permute-start(bf16[112,512]{1,0:T(8,128)(2,1)S(1)} %get-tuple-element.14), channel_id=1, source_target_pairs={{0,1},{1,0},{2,3},{3,2},{4,5},{5,4},{6,7},{7,6},{8,9},{9,8},{10,11... | collective-permute-start | bytes 344072 | tf_op jit(solution)/shard_map/ppermute | solution.py:64
  158.2 13.9 %all-to-all-start.4 = ((bf16[4,112,512]{2,1,0:T(8,128)(2,1)}), bf16[4,112,512]{2,1,0:T(8,128)(2,1)S(1)}, u32[]{:S(2)}, u32[]{:S(2)}) async-start(bf16[4,112,512]{2,1,0:T(8,128)(2,1)} %bitcast.18), calls=%async_computation.4 | async-start | bytes 917504 | tf_op jit(solution)/shard_map/all_to_all | solution.py:22

commit v9 on v7

--- a/solution.py
+++ b/solution.py
@@ -39,7 +39,8 @@
     h = w // 2
     n = nx * m
     core = lax.axis_index("core")
-    own = exchange(momentum[0].reshape(m, nx, w).transpose(1, 0, 2), "x").reshape(n, w)
+    rows = jnp.stack([momentum[0, :, i * w : (i + 1) * w] for i in range(nx)])
+    own = exchange(rows, "x").reshape(n, w)
     other = lax.ppermute(own, "half", SWAP)
 
     both = jnp.stack([own, other])
@@ -53,15 +54,14 @@
     mine = total(exchange(term.reshape(nx, 2 * n, 16 * n), "x")).astype(bf16)
     gram = lax.all_gather(mine, "x", axis=0, tiled=True)
     narrow = gram[:, : 8 * n]
-    narrow = jnp.stack([narrow.reshape(ny, 2 * n, 8 * n), lax.ppermute(narrow, "core", SWAP).reshape(ny, 2 * n, 8 * n)], 1)
-    narrow = narrow.reshape(ny * nc * 2 * n, 8 * n)
+    narrow = jnp.concatenate([narrow, lax.ppermute(narrow, "core", SWAP)], 0)
 
     term = dot(gram, right, ((1,), (0,))).astype(bf16)
-    terms, narrow = lax.optimization_barrier((exchange(term.reshape(ny, 2 * n, w), "y"), narrow))
+    terms = exchange(term.reshape(ny, 2 * n, w), "y")
     keep, send = ordered(core, terms[..., :h], terms[..., h:])
     send = lax.ppermute(total(send).astype(bf16), "core", SWAP)
     first = jnp.stack([total(keep).astype(bf16), send])
-    firsts = lax.all_gather(first, "y", axis=0).reshape(ny * nc * 2 * n, h)
+    firsts = lax.all_gather(first, "y", axis=1).reshape(nc * ny * 2 * n, h)
 
     term = dot(narrow, firsts, ((0,), (0,))).astype(bf16)
     second = total(exchange(term.reshape(nq, nc * n, h), "quarter"))

time: 168 us -> 167 us (level)
  blocking collectives: 67.4 us -> 80.7 us
  waiting for transfers between devices: 29 us -> 23.9 us
  starting transfers between devices: 57.6 us -> 53.2 us
  local copies, waits for them, and re-layouts: 5.05 us -> 2.82 us
    all_to_all x2 -> x3, blocking collectives: 25.5 us -> 38.9 us  [exchange(): return lax.all_to_all(blocks, axis, 0, 0, tiled=True)]
    all_to_all x3 -> x2, starting transfers between devices: 22.9 us -> 18 us  [exchange(): return lax.all_to_all(blocks, axis, 0, 0, tiled=True)]
    another operation x3 -> x0, local copies, waits for them, and re-layouts: 2.32 us -> none  [the longest x1 1.3 us: shards(): jnp.stack([narrow.reshape(ny, 2 * n, 8 * n), lax.ppermute(narrow, 'core',...]
    all_to_all x3 -> x2, waiting for transfers between devices: 19.9 us -> 18 us  [exchange(): return lax.all_to_all(blocks, axis, 0, 0, tiled=True)]
    ppermute x1, waiting for transfers between devices: 1.78 us -> 0.01 us  [shards(): narrow = jnp.concatenate([narrow, lax.ppermute(narrow, 'core', SWAP)], 0)]
  transfers between devices with their start and end apart: 7 -> 6, of which waited for: 7 -> 4; matrix products, arithmetic and copies ran while one was open for 2% -> 0% of each run, Pallas kernels for 0% -> 0%
where the time goes in v9:
time: 167 us
  blocking collectives  80.7 us (48%)
  starting transfers between devices  53.2 us (32%)
  waiting for transfers between devices  23.9 us (14%)
  matrix products  3.71 us (2%)
  local copies, waits for them, and re-layouts  2.82 us (2%)
  other arithmetic  2.06 us (1%)
    all_to_all x3, blocking collectives, exchange(): return lax.all_to_all(blocks, axis, 0, 0, tiled=True)  38.9 us
    ppermute x1, starting transfers between devices, shards(): other = lax.ppermute(own, 'half', SWAP)  29 us
    all_to_all x2, starting transfers between devices, exchange(): return lax.all_to_all(blocks, axis, 0, 0, tiled=True)  18 us
    all_to_all x2, waiting for transfers between devices, exchange(): return lax.all_to_all(blocks, axis, 0, 0, tiled=True)  18 us
    all_gather x1, blocking collectives, shards(): gram = lax.all_gather(mine, 'x', axis=0, tiled=True)  14.4 us
    all_gather x1, blocking collectives, shards(): left = lax.all_gather(both, 'y', axis=0).reshape(ny * 2 * n, w)  13.8 us
    all_gather x1, blocking collectives, shards(): firsts = lax.all_gather(first, 'y', axis=1).reshape(nc * ny * 2 * n, h)  13.6 us
    dot_general x3, matrix products, dot(): lax.dot_general(lhs, rhs, (dims, ((), ())), preferred_element_type=jnp.fl...  3.71 us
  transfers between devices with their start and end apart: 6, of which 4 were waited for; matrix products, arithmetic and copies ran while one was open for 0% of the time, Pallas kernels for 0%

profile of v9, /device:TPU:8, one launch (start us, length us, event | category | flops | bytes accessed | tf_op | source)
XLA Modules:
  0.0 166.6 jit_solution(7546201186475185899)
XLA Ops:
  0.0 0.8 fusion.5
  0.9 10.1 %all_to_all.25 = bf16[4,14,1024]{2,1,0:T(8,128)(2,1)S(1)} all-to-all(bf16[4,14,1024]{2,1,0:T(8,128)(2,1)S(1)} %pad_maximum_fusion.3), channel_id=1, replica_groups=mesh['layer'=4,'quarter'=4,'y'=4,'half'=2,'x'=4,'core'=2] {'x'}, dimensions={0} | all-to-all | bytes 229376 | tf_op jit(solution)/shard_map/all_to_all | solution.py:22
  11.0 29.0 %collective-permute-start = (bf16[56,1024]{1,0:T(8,128)(2,1)S(1)}, bf16[56,1024]{1,0:T(8,128)(2,1)S(1)}, u32[]{:S(2)}, u32[]{:S(2)}) collective-permute-start(bf16[56,1024]{1,0:T(8,128)(2,1)S(1)} %reshape.50), channel_id=1, source_target_pairs={{0,8},{8,0},{1,9},{9,1},{2,10},{10,2},{3,11},{11,3},{4,12},{12,4},... | collective-permute-start | bytes 344072 | tf_op jit(solution)/shard_map/ppermute | solution.py:44
  40.0 3.4 %collective-permute-done = bf16[56,1024]{1,0:T(8,128)(2,1)S(1)} collective-permute-done((bf16[56,1024]{1,0:T(8,128)(2,1)S(1)}, bf16[56,1024]{1,0:T(8,128)(2,1)S(1)}, u32[]{:S(2)}, u32[]{:S(2)}) %collective-permute-start) | collective-permute-done | bytes 114720 | tf_op jit(solution)/shard_map/ppermute | solution.py:44
  43.4 1.0 broadcast_in_dim.4
  44.5 14.5 %all-to-all-start.1 = ((bf16[4,2,56,1024]{3,2,1,0:T(8,128)(2,1)}), bf16[4,2,56,1024]{3,2,1,0:T(8,128)(2,1)S(1)}, u32[]{:S(2)}, u32[]{:S(2)}) async-start(bf16[4,2,56,1024]{3,2,1,0:T(8,128)(2,1)} %broadcast_in_dim.4), calls=%async_computation.1 | async-start | bytes 1835008 | tf_op jit(solution)/shard_map/all_to_all | solution.py:22
  59.0 13.8 %all-gather = bf16[8,56,1024]{2,1,0:T(8,128)(2,1)S(1)} all-gather(bf16[2,56,1024]{2,1,0:T(8,128)(2,1)S(1)} %pad_maximum_fusion.1), channel_id=2, replica_groups=mesh['layer'=4,'quarter'=4,'y'=4,'half'=2,'x'=4,'core'=2] {'y'}, dimensions={0}, use_global_device_ids=true | all-gather | bytes 1146880 | tf_op jit(solution)/shard_map/all_gather | solution.py:48
  72.8 6.6 %all-to-all-done.1 = bf16[4,2,56,1024]{3,2,1,0:T(8,128)(2,1)S(1)} async-done(((bf16[4,2,56,1024]{3,2,1,0:T(8,128)(2,1)}), bf16[4,2,56,1024]{3,2,1,0:T(8,128)(2,1)S(1)}, u32[]{:S(2)}, u32[]{:S(2)}) %all-to-all-start.1) | async-done | bytes 917536 | tf_op jit(solution)/shard_map/all_to_all | solution.py:22
  79.5 1.9 %collective-permute-start.1 = (bf16[4,2,56,1024]{3,2,0,1:T(8,128)(2,1)S(1)}, bf16[4,2,56,1024]{3,2,0,1:T(8,128)(2,1)}, u32[]{:S(2)}, u32[]{:S(2)}) collective-permute-start(bf16[4,2,56,1024]{3,2,0,1:T(8,128)(2,1)S(1)} %copy.5), channel_id=1, source_target_pairs={{0,1},{1,0},{2,3},{3,2},{4,5},{5,4},{6,7},{7,6},{8,9},{9,8},{10,11... | collective-permute-start | bytes 2752520 | tf_op jit(solution)/shard_map/ppermute | solution.py:50
  81.4 2.6 %collective-permute-done.1 = bf16[4,2,56,1024]{3,2,0,1:T(8,128)(2,1)} collective-permute-done((bf16[4,2,56,1024]{3,2,0,1:T(8,128)(2,1)S(1)}, bf16[4,2,56,1024]{3,2,0,1:T(8,128)(2,1)}, u32[]{:S(2)}, u32[]{:S(2)}) %collective-permute-start.1) | collective-permute-done | bytes 917536 | tf_op jit(solution)/shard_map/ppermute | solution.py:50
  84.0 1.3 select_bitcast_fusion.1
  85.5 1.2 convolution_convert_fusion.1
  86.6 15.4 %all_to_all.26 = bf16[4,112,896]{2,1,0:T(8,128)(2,1)S(1)} all-to-all(bf16[4,112,896]{2,1,0:T(8,128)(2,1)S(1)} %bitcast.36), channel_id=1, replica_groups=mesh['layer'=4,'quarter'=4,'y'=4,'half'=2,'x'=4,'core'=2] {'x'}, dimensions={0} | all-to-all | bytes 1605632 | tf_op jit(solution)/shard_map/all_to_all | solution.py:22
  102.2 14.4 %all_gather.14 = bf16[448,896]{1,0:T(8,128)(2,1)S(1)} all-gather(bf16[112,896]{1,0:T(8,128)(2,1)S(1)} %reduce_sum.45), channel_id=1, replica_groups=mesh['layer'=4,'quarter'=4,'y'=4,'half'=2,'x'=4,'core'=2] {'x'}, dimensions={0}, use_global_device_ids=true | all-gather | bytes 1003520 | tf_op jit(solution)/shard_map/all_gather | solution.py:55
  116.6 1.1 convolution_convert_fusion
  117.7 13.4 %all_to_all.27 = bf16[4,112,1024]{2,1,0:T(8,128)(2,1)S(1)} all-to-all(bf16[4,112,1024]{2,1,0:T(8,128)(2,1)S(1)} %bitcast.33), channel_id=1, replica_groups=mesh['layer'=4,'quarter'=4,'y'=4,'half'=2,'x'=4,'core'=2] {'y'}, dimensions={0} | all-to-all | bytes 1835008 | tf_op jit(solution)/shard_map/all_to_all | solution.py:22
  131.1 0.2 select_reduce_fusion.1
  131.3 1.9 %collective-permute-start.2 = (bf16[112,512]{1,0:T(8,128)(2,1)S(1)}, bf16[112,512]{1,0:T(8,128)(2,1)S(1)}, u32[]{:S(2)}, u32[]{:S(2)}) collective-permute-start(bf16[112,512]{1,0:T(8,128)(2,1)S(1)} %get-tuple-element.10), channel_id=1, source_target_pairs={{0,1},{1,0},{2,3},{3,2},{4,5},{5,4},{6,7},{7,6},{8,9},{9,8},{10,11... | collective-permute-start | bytes 344072 | tf_op jit(solution)/shard_map/ppermute | solution.py:62
  133.3 2.4 %collective-permute-start.3 = (bf16[448,448]{1,0:T(8,128)(2,1)S(1)}, bf16[448,448]{1,0:T(8,128)(2,1)S(1)}, u32[]{:S(2)}, u32[]{:S(2)}) collective-permute-start(bf16[448,448]{1,0:T(8,128)(2,1)S(1)} %slice.40), channel_id=1, source_target_pairs={{0,1},{1,0},{2,3},{3,2},{4,5},{5,4},{6,7},{7,6},{8,9},{9,8},{10,11... | collective-permute-start | bytes 1204232 | tf_op jit(solution)/shard_map/ppermute | solution.py:57
  135.7 13.6 %all-gather.1 = bf16[2,448,512]{2,1,0:T(8,128)(2,1)S(1)} all-gather(bf16[2,112,512]{2,1,0:T(8,128)(2,1)S(1)} %pad_maximum_fusion.2), channel_id=3, replica_groups=mesh['layer'=4,'quarter'=4,'y'=4,'half'=2,'x'=4,'core'=2] {'y'}, dimensions={1}, use_global_device_ids=true | all-gather | bytes 1146880 | tf_op jit(solution)/shard_map/all_gather | solution.py:64
  149.3 1.4 convolution_convert_fusion.2
  150.7 3.5 %all-to-all-start.4 = ((bf16[4,112,512]{2,1,0:T(8,128)(2,1)}), bf16[4,112,512]{2,1,0:T(8,128)(2,1)S(1)}, u32[]{:S(2)}, u32[]{:S(2)}) async-start(bf16[4,112,512]{2,1,0:T(8,128)(2,1)} %bitcast.15), calls=%async_computation.4 | async-start | bytes 917504 | tf_op jit(solution)/shard_map/all_to_all | solution.py:22
  154.4 11.3 %all-to-all-done.4 = bf16[4,112,512]{2,1,0:T(8,128)(2,1)S(1)} async-done(((bf16[4,112,512]{2,1,0:T(8,128)(2,1)}), bf16[4,112,512]{2,1,0:T(8,128)(2,1)S(1)}, u32[]{:S(2)}, u32[]{:S(2)}) %all-to-all-start.4) | async-done | bytes 458784 | tf_op jit(solution)/shard_map/all_to_all | solution.py:22
  165.9 0.7 convert_element_type.52
  (21 shorter events, 0.9 us)
Async XLA Ops:
  11.0 32.4 %collective-permute-start = (bf16[56,1024]{1,0:T(8,128)(2,1)S(1)}, bf16[56,1024]{1,0:T(8,128)(2,1)S(1)}, u32[]{:S(2)}, u32[]{:S(2)}) collective-permute-start(bf16[56,1024]{1,0:T(8,128)(2,1)S(1)} %reshape.50), channel_id=1, source_target_pairs={{0,8},{8,0},{1,9},{9,1},{2,10},{10,2},{3,11},{11,3},{4,12},{12,4},... | collective-permute-start | bytes 344072 | tf_op jit(solution)/shard_map/ppermute | solution.py:44
  44.5 34.9 %all-to-all-start.1 = ((bf16[4,2,56,1024]{3,2,1,0:T(8,128)(2,1)}), bf16[4,2,56,1024]{3,2,1,0:T(8,128)(2,1)S(1)}, u32[]{:S(2)}, u32[]{:S(2)}) async-start(bf16[4,2,56,1024]{3,2,1,0:T(8,128)(2,1)} %broadcast_in_dim.4), calls=%async_computation.1 | async-start | bytes 1835008 | tf_op jit(solution)/shard_map/all_to_all | solution.py:22
  79.5 4.5 %collective-permute-start.1 = (bf16[4,2,56,1024]{3,2,0,1:T(8,128)(2,1)S(1)}, bf16[4,2,56,1024]{3,2,0,1:T(8,128)(2,1)}, u32[]{:S(2)}, u32[]{:S(2)}) collective-permute-start(bf16[4,2,56,1024]{3,2,0,1:T(8,128)(2,1)S(1)} %copy.5), channel_id=1, source_target_pairs={{0,1},{1,0},{2,3},{3,2},{4,5},{5,4},{6,7},{7,6},{8,9},{9,8},{10,11... | collective-permute-start | bytes 2752520 | tf_op jit(solution)/shard_map/ppermute | solution.py:50
  131.3 4.4 %collective-permute-start.2 = (bf16[112,512]{1,0:T(8,128)(2,1)S(1)}, bf16[112,512]{1,0:T(8,128)(2,1)S(1)}, u32[]{:S(2)}, u32[]{:S(2)}) collective-permute-start(bf16[112,512]{1,0:T(8,128)(2,1)S(1)} %get-tuple-element.10), channel_id=1, source_target_pairs={{0,1},{1,0},{2,3},{3,2},{4,5},{5,4},{6,7},{7,6},{8,9},{9,8},{10,11... | collective-permute-start | bytes 344072 | tf_op jit(solution)/shard_map/ppermute | solution.py:62
  133.3 16.0 %collective-permute-start.3 = (bf16[448,448]{1,0:T(8,128)(2,1)S(1)}, bf16[448,448]{1,0:T(8,128)(2,1)S(1)}, u32[]{:S(2)}, u32[]{:S(2)}) collective-permute-start(bf16[448,448]{1,0:T(8,128)(2,1)S(1)} %slice.40), channel_id=1, source_target_pairs={{0,1},{1,0},{2,3},{3,2},{4,5},{5,4},{6,7},{7,6},{8,9},{9,8},{10,11... | collective-permute-start | bytes 1204232 | tf_op jit(solution)/shard_map/ppermute | solution.py:57
  150.7 15.0 %all-to-all-start.4 = ((bf16[4,112,512]{2,1,0:T(8,128)(2,1)}), bf16[4,112,512]{2,1,0:T(8,128)(2,1)S(1)}, u32[]{:S(2)}, u32[]{:S(2)}) async-start(bf16[4,112,512]{2,1,0:T(8,128)(2,1)} %bitcast.15), calls=%async_computation.4 | async-start | bytes 917504 | tf_op jit(solution)/shard_map/all_to_all | solution.py:22

commit v10 on v9

--- a/solution.py
+++ b/solution.py
@@ -40,9 +40,15 @@
     n = nx * m
     core = lax.axis_index("core")
     rows = jnp.stack([momentum[0, :, i * w : (i + 1) * w] for i in range(nx)])
+    x = lax.axis_index("x")
+    got = []
+    for step in range(nx):
+        block = lax.dynamic_index_in_dim(rows, (x + step) % nx, 0, False)
+        pairs = [(g * nx + i, (1 - g) * nx + (i + step) % nx) for g in range(2) for i in range(nx)]
+        got.append(lax.ppermute(block, ("half", "x"), pairs))
+    got = jnp.stack(got)
+    other = jnp.concatenate([lax.dynamic_index_in_dim(got, (x - i) % nx, 0, False) for i in range(nx)], 0)
     own = exchange(rows, "x").reshape(n, w)
-    other = lax.ppermute(own, "half", SWAP)
-
     both = jnp.stack([own, other])
     block = spread(both, "quarter")
     left = lax.all_gather(both, "y", axis=0).reshape(ny * 2 * n, w)

time: 167 us -> 198 us (1.19)
  starting transfers between devices: 53.2 us -> 74.7 us
  waiting for transfers between devices: 23.9 us -> 41.3 us
  blocking collectives: 80.7 us -> 71.3 us
    ppermute x1 -> x4, starting transfers between devices: 29 us -> 57.8 us  [shards(): got.append(lax.ppermute(block, ('half', 'x'), pairs))]
    ppermute x1 -> x4, waiting for transfers between devices: 3.41 us -> 23.3 us  [shards(): got.append(lax.ppermute(block, ('half', 'x'), pairs))]
    all_to_all x3 -> x2, blocking collectives: 38.9 us -> 28.9 us  [exchange(): return lax.all_to_all(blocks, axis, 0, 0, tiled=True)]
    all_to_all x2 -> x3, starting transfers between devices: 18 us -> 10.7 us  [exchange(): return lax.all_to_all(blocks, axis, 0, 0, tiled=True)]
    all_to_all x2 -> x3, waiting for transfers between devices: 18 us -> 15.4 us  [exchange(): return lax.all_to_all(blocks, axis, 0, 0, tiled=True)]
  transfers between devices with their start and end apart: 6 -> 10, of which waited for: 4 -> 4; matrix products, arithmetic and copies ran while one was open for 0% -> 0% of each run, Pallas kernels for 0% -> 0%
where the time goes in v10:
time: 198 us
  starting transfers between devices  74.7 us (38%)
  blocking collectives  71.3 us (36%)
  waiting for transfers between devices  41.3 us (21%)
  matrix products  3.7 us (2%)
  local copies, waits for them, and re-layouts  3.63 us (2%)
  other arithmetic  2.79 us (1%)
    ppermute x4, starting transfers between devices, shards(): got.append(lax.ppermute(block, ('half', 'x'), pairs))  57.8 us
    all_to_all x2, blocking collectives, exchange(): return lax.all_to_all(blocks, axis, 0, 0, tiled=True)  28.9 us
    ppermute x4, waiting for transfers between devices, shards(): got.append(lax.ppermute(block, ('half', 'x'), pairs))  23.3 us
    all_to_all x3, waiting for transfers between devices, exchange(): return lax.all_to_all(blocks, axis, 0, 0, tiled=True)  15.4 us
    all_gather x1, blocking collectives, shards(): left = lax.all_gather(both, 'y', axis=0).reshape(ny * 2 * n, w)  14.4 us
    all_gather x1, blocking collectives, shards(): gram = lax.all_gather(mine, 'x', axis=0, tiled=True)  14.4 us
    all_gather x1, blocking collectives, shards(): firsts = lax.all_gather(first, 'y', axis=1).reshape(nc * ny * 2 * n, h)  13.6 us
    all_to_all x3, starting transfers between devices, exchange(): return lax.all_to_all(blocks, axis, 0, 0, tiled=True)  10.7 us
  transfers between devices with their start and end apart: 10, of which 4 were waited for; matrix products, arithmetic and copies ran while one was open for 0% of the time, Pallas kernels for 0%

profile of v10, /device:TPU:8, one launch (start us, length us, event | category | flops | bytes accessed | tf_op | source)
XLA Modules:
  0.0 197.7 jit_solution(16504119600220996887)
XLA Ops:
  2.3 29.0 %collective-permute-start = (bf16[14,1024]{1,0:T(8,128)(2,1)S(1)}, bf16[14,1024]{1,0:T(8,128)(2,1)S(1)}, u32[]{:S(2)}, u32[]{:S(2)}) collective-permute-start(bf16[14,1024]{1,0:T(8,128)(2,1)S(1)} %get-tuple-element.19), channel_id=1, source_target_pairs={{0,8},{2,10},{4,12},{6,14},{8,0},{10,2},{12,4},{14,6},{1,9},{3,11}... | collective-permute-start | bytes 86024 | tf_op jit(solution)/shard_map/ppermute | solution.py:48
  31.3 4.1 %collective-permute-start.3 = (bf16[14,1024]{1,0:T(8,128)(2,1)S(1)}, bf16[14,1024]{1,0:T(8,128)(2,1)S(1)}, u32[]{:S(2)}, u32[]{:S(2)}) collective-permute-start(bf16[14,1024]{1,0:T(8,128)(2,1)S(1)} %get-tuple-element.20), channel_id=1, source_target_pairs={{0,14},{2,8},{4,10},{6,12},{8,6},{10,0},{12,2},{14,4},{1,15},{3,9}... | collective-permute-start | bytes 86024 | tf_op jit(solution)/shard_map/ppermute | solution.py:48
  35.4 22.5 %collective-permute-start.2 = (bf16[14,1024]{1,0:T(8,128)(2,1)S(1)}, bf16[14,1024]{1,0:T(8,128)(2,1)S(1)}, u32[]{:S(2)}, u32[]{:S(2)}) collective-permute-start(bf16[14,1024]{1,0:T(8,128)(2,1)S(1)} %get-tuple-element.21), channel_id=1, source_target_pairs={{0,12},{2,14},{4,8},{6,10},{8,4},{10,6},{12,0},{14,2},{1,13},{3,15... | collective-permute-start | bytes 86024 | tf_op jit(solution)/shard_map/ppermute | solution.py:48
  57.9 2.2 %collective-permute-start.1 = (bf16[14,1024]{1,0:T(8,128)(2,1)S(1)}, bf16[14,1024]{1,0:T(8,128)(2,1)S(1)}, u32[]{:S(2)}, u32[]{:S(2)}) collective-permute-start(bf16[14,1024]{1,0:T(8,128)(2,1)S(1)} %get-tuple-element.22), channel_id=1, source_target_pairs={{0,10},{2,12},{4,14},{6,8},{8,2},{10,4},{12,6},{14,0},{1,11},{3,13... | collective-permute-start | bytes 86024 | tf_op jit(solution)/shard_map/ppermute | solution.py:48
  60.2 3.7 %all-to-all-start = ((bf16[4,14,1024]{2,1,0:T(8,128)(2,1)}), bf16[4,14,1024]{2,1,0:T(8,128)(2,1)S(1)}, u32[]{:S(2)}, u32[]{:S(2)}) async-start(bf16[4,14,1024]{2,1,0:T(8,128)(2,1)} %pad_maximum_fusion.3), calls=%async_computation | async-start | bytes 262144 | tf_op jit(solution)/shard_map/all_to_all | solution.py:22
  63.9 23.3 %collective-permute-done.1 = bf16[14,1024]{1,0:T(8,128)(2,1)S(1)} collective-permute-done((bf16[14,1024]{1,0:T(8,128)(2,1)S(1)}, bf16[14,1024]{1,0:T(8,128)(2,1)S(1)}, u32[]{:S(2)}, u32[]{:S(2)}) %collective-permute-start.1) | collective-permute-done | bytes 28704 | tf_op jit(solution)/shard_map/ppermute | solution.py:48
  87.4 1.1 broadcast_in_dim.4
  88.4 3.5 %all-to-all-start.1 = ((bf16[4,2,56,1024]{3,2,1,0:T(8,128)(2,1)}), bf16[4,2,56,1024]{3,2,1,0:T(8,128)(2,1)S(1)}, u32[]{:S(2)}, u32[]{:S(2)}) async-start(bf16[4,2,56,1024]{3,2,1,0:T(8,128)(2,1)} %broadcast_in_dim.4), calls=%async_computation.1 | async-start | bytes 1835008 | tf_op jit(solution)/shard_map/all_to_all | solution.py:22
  91.9 14.4 %all-gather = bf16[8,56,1024]{2,1,0:T(8,128)(2,1)S(1)} all-gather(bf16[2,56,1024]{2,1,0:T(8,128)(2,1)S(1)} %pad_maximum_fusion.1), channel_id=2, replica_groups=mesh['layer'=4,'quarter'=4,'y'=4,'half'=2,'x'=4,'core'=2] {'y'}, dimensions={0}, use_global_device_ids=true | all-gather | bytes 1146880 | tf_op jit(solution)/shard_map/all_gather | solution.py:54
  106.4 4.1 %all-to-all-done.1 = bf16[4,2,56,1024]{3,2,1,0:T(8,128)(2,1)S(1)} async-done(((bf16[4,2,56,1024]{3,2,1,0:T(8,128)(2,1)}), bf16[4,2,56,1024]{3,2,1,0:T(8,128)(2,1)S(1)}, u32[]{:S(2)}, u32[]{:S(2)}) %all-to-all-start.1) | async-done | bytes 917536 | tf_op jit(solution)/shard_map/all_to_all | solution.py:22
  110.5 1.9 collective-permute-start.4
  112.5 2.6 %collective-permute-done.4 = bf16[4,2,56,1024]{3,2,0,1:T(8,128)(2,1)} collective-permute-done((bf16[4,2,56,1024]{3,2,0,1:T(8,128)(2,1)S(1)}, bf16[4,2,56,1024]{3,2,0,1:T(8,128)(2,1)}, u32[]{:S(2)}, u32[]{:S(2)}) %collective-permute-start.4) | collective-permute-done | bytes 917536 | tf_op jit(solution)/shard_map/ppermute | solution.py:56
  115.0 1.3 select_bitcast_fusion.1
  116.5 1.1 convolution_convert_fusion.1
  117.7 15.4 %all_to_all.25 = bf16[4,112,896]{2,1,0:T(8,128)(2,1)S(1)} all-to-all(bf16[4,112,896]{2,1,0:T(8,128)(2,1)S(1)} %bitcast.57), channel_id=1, replica_groups=mesh['layer'=4,'quarter'=4,'y'=4,'half'=2,'x'=4,'core'=2] {'x'}, dimensions={0} | all-to-all | bytes 1605632 | tf_op jit(solution)/shard_map/all_to_all | solution.py:22
  133.2 14.4 %all_gather.14 = bf16[448,896]{1,0:T(8,128)(2,1)S(1)} all-gather(bf16[112,896]{1,0:T(8,128)(2,1)S(1)} %reduce_sum.45), channel_id=1, replica_groups=mesh['layer'=4,'quarter'=4,'y'=4,'half'=2,'x'=4,'core'=2] {'x'}, dimensions={0}, use_global_device_ids=true | all-gather | bytes 1003520 | tf_op jit(solution)/shard_map/all_gather | solution.py:61
  147.6 1.1 convolution_convert_fusion
  148.7 13.4 %all_to_all.26 = bf16[4,112,1024]{2,1,0:T(8,128)(2,1)S(1)} all-to-all(bf16[4,112,1024]{2,1,0:T(8,128)(2,1)S(1)} %bitcast.54), channel_id=1, replica_groups=mesh['layer'=4,'quarter'=4,'y'=4,'half'=2,'x'=4,'core'=2] {'y'}, dimensions={0} | all-to-all | bytes 1835008 | tf_op jit(solution)/shard_map/all_to_all | solution.py:22
  162.4 1.9 collective-permute-start.5
  164.3 2.4 %collective-permute-start.6 = (bf16[448,448]{1,0:T(8,128)(2,1)S(1)}, bf16[448,448]{1,0:T(8,128)(2,1)S(1)}, u32[]{:S(2)}, u32[]{:S(2)}) collective-permute-start(bf16[448,448]{1,0:T(8,128)(2,1)S(1)} %slice.40), channel_id=1, source_target_pairs={{0,1},{1,0},{2,3},{3,2},{4,5},{5,4},{6,7},{7,6},{8,9},{9,8},{10,11... | collective-permute-start | bytes 1204232 | tf_op jit(solution)/shard_map/ppermute | solution.py:63
  166.8 13.6 %all-gather.1 = bf16[2,448,512]{2,1,0:T(8,128)(2,1)S(1)} all-gather(bf16[2,112,512]{2,1,0:T(8,128)(2,1)S(1)} %pad_maximum_fusion.2), channel_id=3, replica_groups=mesh['layer'=4,'quarter'=4,'y'=4,'half'=2,'x'=4,'core'=2] {'y'}, dimensions={1}, use_global_device_ids=true | all-gather | bytes 1146880 | tf_op jit(solution)/shard_map/all_gather | solution.py:70
  180.4 1.4 convolution_convert_fusion.2
  181.8 3.5 %all-to-all-start.4 = ((bf16[4,112,512]{2,1,0:T(8,128)(2,1)}), bf16[4,112,512]{2,1,0:T(8,128)(2,1)S(1)}, u32[]{:S(2)}, u32[]{:S(2)}) async-start(bf16[4,112,512]{2,1,0:T(8,128)(2,1)} %bitcast.27), calls=%async_computation.4 | async-start | bytes 917504 | tf_op jit(solution)/shard_map/all_to_all | solution.py:22
  185.4 11.3 %all-to-all-done.4 = bf16[4,112,512]{2,1,0:T(8,128)(2,1)S(1)} async-done(((bf16[4,112,512]{2,1,0:T(8,128)(2,1)}), bf16[4,112,512]{2,1,0:T(8,128)(2,1)S(1)}, u32[]{:S(2)}, u32[]{:S(2)}) %all-to-all-start.4) | async-done | bytes 458784 | tf_op jit(solution)/shard_map/all_to_all | solution.py:22
  (31 shorter events, 4.1 us)
Async XLA Ops:
  2.3 61.5 %collective-permute-start = (bf16[14,1024]{1,0:T(8,128)(2,1)S(1)}, bf16[14,1024]{1,0:T(8,128)(2,1)S(1)}, u32[]{:S(2)}, u32[]{:S(2)}) collective-permute-start(bf16[14,1024]{1,0:T(8,128)(2,1)S(1)} %get-tuple-element.19), channel_id=1, source_target_pairs={{0,8},{2,10},{4,12},{6,14},{8,0},{10,2},{12,4},{14,6},{1,9},{3,11}... | collective-permute-start | bytes 86024 | tf_op jit(solution)/shard_map/ppermute | solution.py:48
  31.3 32.6 %collective-permute-start.3 = (bf16[14,1024]{1,0:T(8,128)(2,1)S(1)}, bf16[14,1024]{1,0:T(8,128)(2,1)S(1)}, u32[]{:S(2)}, u32[]{:S(2)}) collective-permute-start(bf16[14,1024]{1,0:T(8,128)(2,1)S(1)} %get-tuple-element.20), channel_id=1, source_target_pairs={{0,14},{2,8},{4,10},{6,12},{8,6},{10,0},{12,2},{14,4},{1,15},{3,9}... | collective-permute-start | bytes 86024 | tf_op jit(solution)/shard_map/ppermute | solution.py:48
  35.4 28.4 %collective-permute-start.2 = (bf16[14,1024]{1,0:T(8,128)(2,1)S(1)}, bf16[14,1024]{1,0:T(8,128)(2,1)S(1)}, u32[]{:S(2)}, u32[]{:S(2)}) collective-permute-start(bf16[14,1024]{1,0:T(8,128)(2,1)S(1)} %get-tuple-element.21), channel_id=1, source_target_pairs={{0,12},{2,14},{4,8},{6,10},{8,4},{10,6},{12,0},{14,2},{1,13},{3,15... | collective-permute-start | bytes 86024 | tf_op jit(solution)/shard_map/ppermute | solution.py:48
  57.9 29.2 %collective-permute-start.1 = (bf16[14,1024]{1,0:T(8,128)(2,1)S(1)}, bf16[14,1024]{1,0:T(8,128)(2,1)S(1)}, u32[]{:S(2)}, u32[]{:S(2)}) collective-permute-start(bf16[14,1024]{1,0:T(8,128)(2,1)S(1)} %get-tuple-element.22), channel_id=1, source_target_pairs={{0,10},{2,12},{4,14},{6,8},{8,2},{10,4},{12,6},{14,0},{1,11},{3,13... | collective-permute-start | bytes 86024 | tf_op jit(solution)/shard_map/ppermute | solution.py:48
  60.2 27.1 %all-to-all-start = ((bf16[4,14,1024]{2,1,0:T(8,128)(2,1)}), bf16[4,14,1024]{2,1,0:T(8,128)(2,1)S(1)}, u32[]{:S(2)}, u32[]{:S(2)}) async-start(bf16[4,14,1024]{2,1,0:T(8,128)(2,1)} %pad_maximum_fusion.3), calls=%async_computation | async-start | bytes 262144 | tf_op jit(solution)/shard_map/all_to_all | solution.py:22
  88.4 22.0 %all-to-all-start.1 = ((bf16[4,2,56,1024]{3,2,1,0:T(8,128)(2,1)}), bf16[4,2,56,1024]{3,2,1,0:T(8,128)(2,1)S(1)}, u32[]{:S(2)}, u32[]{:S(2)}) async-start(bf16[4,2,56,1024]{3,2,1,0:T(8,128)(2,1)} %broadcast_in_dim.4), calls=%async_computation.1 | async-start | bytes 1835008 | tf_op jit(solution)/shard_map/all_to_all | solution.py:22
  110.5 4.5 %collective-permute-start.4 = (bf16[4,2,56,1024]{3,2,0,1:T(8,128)(2,1)S(1)}, bf16[4,2,56,1024]{3,2,0,1:T(8,128)(2,1)}, u32[]{:S(2)}, u32[]{:S(2)}) collective-permute-start(bf16[4,2,56,1024]{3,2,0,1:T(8,128)(2,1)S(1)} %copy.5), channel_id=1, source_target_pairs={{0,1},{1,0},{2,3},{3,2},{4,5},{5,4},{6,7},{7,6},{8,9},{9,8},{10,11... | collective-permute-start | bytes 2752520 | tf_op jit(solution)/shard_map/ppermute | solution.py:56
  162.4 4.4 %collective-permute-start.5 = (bf16[112,512]{1,0:T(8,128)(2,1)S(1)}, bf16[112,512]{1,0:T(8,128)(2,1)S(1)}, u32[]{:S(2)}, u32[]{:S(2)}) collective-permute-start(bf16[112,512]{1,0:T(8,128)(2,1)S(1)} %get-tuple-element.10), channel_id=1, source_target_pairs={{0,1},{1,0},{2,3},{3,2},{4,5},{5,4},{6,7},{7,6},{8,9},{9,8},{10,11... | collective-permute-start | bytes 344072 | tf_op jit(solution)/shard_map/ppermute | solution.py:68
  164.3 16.0 %collective-permute-start.6 = (bf16[448,448]{1,0:T(8,128)(2,1)S(1)}, bf16[448,448]{1,0:T(8,128)(2,1)S(1)}, u32[]{:S(2)}, u32[]{:S(2)}) collective-permute-start(bf16[448,448]{1,0:T(8,128)(2,1)S(1)} %slice.40), channel_id=1, source_target_pairs={{0,1},{1,0},{2,3},{3,2},{4,5},{5,4},{6,7},{7,6},{8,9},{9,8},{10,11... | collective-permute-start | bytes 1204232 | tf_op jit(solution)/shard_map/ppermute | solution.py:63
  181.8 15.0 %all-to-all-start.4 = ((bf16[4,112,512]{2,1,0:T(8,128)(2,1)}), bf16[4,112,512]{2,1,0:T(8,128)(2,1)S(1)}, u32[]{:S(2)}, u32[]{:S(2)}) async-start(bf16[4,112,512]{2,1,0:T(8,128)(2,1)} %bitcast.27), calls=%async_computation.4 | async-start | bytes 917504 | tf_op jit(solution)/shard_map/all_to_all | solution.py:22

commit v11 on v9

--- a/solution.py
+++ b/solution.py
@@ -44,7 +44,7 @@
     other = lax.ppermute(own, "half", SWAP)
 
     both = jnp.stack([own, other])
-    block = spread(both, "quarter")
+    block = spread(both.reshape(2 * n, w), "quarter").reshape(nq, 2, n, w)
     left = lax.all_gather(both, "y", axis=0).reshape(ny * 2 * n, w)
     block, left = lax.optimization_barrier((block, left))
     block = jnp.stack(ordered(core, block, lax.ppermute(block, "core", SWAP)), 2)
@@ -52,7 +52,7 @@
 
     term = dot(left, right, ((1,), (1,))).astype(bf16)
     mine = total(exchange(term.reshape(nx, 2 * n, 16 * n), "x")).astype(bf16)
-    gram = lax.all_gather(mine, "x", axis=0, tiled=True)
+    gram = spread(mine, "x").reshape(nx * 2 * n, 16 * n)
     narrow = gram[:, : 8 * n]
     narrow = jnp.concatenate([narrow, lax.ppermute(narrow, "core", SWAP)], 0)
 
@@ -61,7 +61,8 @@
     keep, send = ordered(core, terms[..., :h], terms[..., h:])
     send = lax.ppermute(total(send).astype(bf16), "core", SWAP)
     first = jnp.stack([total(keep).astype(bf16), send])
-    firsts = lax.all_gather(first, "y", axis=1).reshape(nc * ny * 2 * n, h)
+    firsts = spread(first.reshape(nc * 2 * n, h), "y").reshape(ny, nc, 2 * n, h)
+    firsts = firsts.transpose(1, 0, 2, 3).reshape(nc * ny * 2 * n, h)
 
     term = dot(narrow, firsts, ((0,), (0,))).astype(bf16)
     second = total(exchange(term.reshape(nq, nc * n, h), "quarter"))

time: 167 us -> 178 us (1.066)
  the two profiles are of different devices: /device:TPU:8 before, /device:TPU:1 now
where the time goes in v11:
time: 178 us; the launch traced here: 177 us
  blocking collectives  65.6 us (37%)
  starting transfers between devices  61 us (34%)
  waiting for transfers between devices  37.9 us (21%)
  local copies, waits for them, and re-layouts  6.51 us (4%)
  matrix products  4.76 us (3%)
    all_to_all x4, blocking collectives, exchange(): return lax.all_to_all(blocks, axis, 0, 0, tiled=True)  53 us
    all_to_all x3, waiting for transfers between devices, exchange(): return lax.all_to_all(blocks, axis, 0, 0, tiled=True)  32.1 us
    ppermute x1, starting transfers between devices, shards(): other = lax.ppermute(own, 'half', SWAP)  28.7 us
    all_to_all x3, starting transfers between devices, exchange(): return lax.all_to_all(blocks, axis, 0, 0, tiled=True)  21 us
    all_gather x1, blocking collectives, shards(): left = lax.all_gather(both, 'y', axis=0).reshape(ny * 2 * n, w)  12.5 us
    ppermute x1, starting transfers between devices, shards(): send = lax.ppermute(total(send).astype(bf16), 'core', SWAP)  5.24 us
    dot_general x3, matrix products, dot(): lax.dot_general(lhs, rhs, (dims, ((), ())), preferred_element_type=jnp.fl...  4.76 us
    ppermute x1, starting transfers between devices, shards(): lax.ppermute(block, 'core', SWAP)  3.8 us
  transfers between devices with their start and end apart: 7, of which 6 were waited for; matrix products, arithmetic and copies ran while one was open for 1% of the time, Pallas kernels for 0%

profile of v11, /device:TPU:1, one launch (start us, length us, event | category | flops | bytes accessed | tf_op | source)
XLA Modules:
  0.0 177.0 jit_solution(8082862510733516563)
XLA Ops:
  0.9 9.5 %all_to_all.35 = bf16[4,14,1024]{2,1,0:T(8,128)(2,1)S(1)} all-to-all(bf16[4,14,1024]{2,1,0:T(8,128)(2,1)S(1)} %pad_maximum_fusion.2), channel_id=1, replica_groups=mesh['layer'=4,'quarter'=4,'y'=4,'half'=2,'x'=4,'core'=2] {'x'}, dimensions={0} | all-to-all | bytes 229376 | tf_op jit(solution)/shard_map/all_to_all | solution.py:22
  10.4 28.7 %collective-permute-start = (bf16[56,1024]{1,0:T(8,128)(2,1)S(1)}, bf16[56,1024]{1,0:T(8,128)(2,1)S(1)}, u32[]{:S(2)}, u32[]{:S(2)}) collective-permute-start(bf16[56,1024]{1,0:T(8,128)(2,1)S(1)} %reshape.61), channel_id=1, source_target_pairs={{0,8},{8,0},{1,9},{9,1},{2,10},{10,2},{3,11},{11,3},{4,12},{12,4},... | collective-permute-start | bytes 344072 | tf_op jit(solution)/shard_map/ppermute | solution.py:44
  39.1 2.8 %collective-permute-done = bf16[56,1024]{1,0:T(8,128)(2,1)S(1)} collective-permute-done((bf16[56,1024]{1,0:T(8,128)(2,1)S(1)}, bf16[56,1024]{1,0:T(8,128)(2,1)S(1)}, u32[]{:S(2)}, u32[]{:S(2)}) %collective-permute-start) | collective-permute-done | bytes 114720 | tf_op jit(solution)/shard_map/ppermute | solution.py:44
  42.0 1.1 broadcast_in_dim.22
  43.0 14.1 %all-to-all-start.1 = ((bf16[4,112,1024]{2,1,0:T(8,128)(2,1)}), bf16[4,112,1024]{2,1,0:T(8,128)(2,1)S(1)}, u32[]{:S(2)}, u32[]{:S(2)}) async-start(bf16[4,112,1024]{2,1,0:T(8,128)(2,1)} %broadcast_in_dim.22), calls=%async_computation.1 | async-start | bytes 1835008 | tf_op jit(solution)/shard_map/all_to_all | solution.py:22
  57.1 12.5 %all-gather = bf16[8,56,1024]{2,1,0:T(8,128)(2,1)} all-gather(bf16[2,56,1024]{2,1,0:T(8,128)(2,1)S(1)} %pad_maximum_fusion), channel_id=2, replica_groups=mesh['layer'=4,'quarter'=4,'y'=4,'half'=2,'x'=4,'core'=2] {'y'}, dimensions={0}, use_global_device_ids=true | all-gather | bytes 1146880 | tf_op jit(solution)/shard_map/all_gather | solution.py:48
  69.6 9.4 %all-to-all-done.1 = bf16[4,112,1024]{2,1,0:T(8,128)(2,1)S(1)} async-done(((bf16[4,112,1024]{2,1,0:T(8,128)(2,1)}), bf16[4,112,1024]{2,1,0:T(8,128)(2,1)S(1)}, u32[]{:S(2)}, u32[]{:S(2)}) %all-to-all-start.1) | async-done | bytes 917536 | tf_op jit(solution)/shard_map/all_to_all | solution.py:22
  79.1 3.8 %collective-permute-start.1 = (bf16[4,2,56,1024]{3,2,1,0:T(8,128)(2,1)S(1)}, bf16[4,2,56,1024]{3,2,1,0:T(8,128)(2,1)S(1)}, u32[]{:S(2)}, u32[]{:S(2)}) collective-permute-start(bf16[4,2,56,1024]{3,2,1,0:T(8,128)(2,1)S(1)} %bitcast.35), channel_id=1, source_target_pairs={{0,1},{1,0},{2,3},{3,2},{4,5},{5,4},{6,7},{7,6},{8,9},{9,8},{10,11... | collective-permute-start | bytes 2752520 | tf_op jit(solution)/shard_map/ppermute | solution.py:50
  82.9 2.1 %collective-permute-done.1 = bf16[4,2,56,1024]{3,2,1,0:T(8,128)(2,1)S(1)} collective-permute-done((bf16[4,2,56,1024]{3,2,1,0:T(8,128)(2,1)S(1)}, bf16[4,2,56,1024]{3,2,1,0:T(8,128)(2,1)S(1)}, u32[]{:S(2)}, u32[]{:S(2)}) %collective-permute-start.1) | collective-permute-done | bytes 917536 | tf_op jit(solution)/shard_map/ppermute | solution.py:50
  85.4 1.0 copy-done
  86.4 1.2 convolution_convert_fusion.1
  87.6 14.6 %all_to_all.36 = bf16[4,112,896]{2,1,0:T(8,128)(2,1)S(1)} all-to-all(bf16[4,112,896]{2,1,0:T(8,128)(2,1)S(1)} %bitcast.47), channel_id=1, replica_groups=mesh['layer'=4,'quarter'=4,'y'=4,'half'=2,'x'=4,'core'=2] {'x'}, dimensions={0} | all-to-all | bytes 1605632 | tf_op jit(solution)/shard_map/all_to_all | solution.py:22
  102.4 13.7 %all_to_all.37 = bf16[4,112,896]{2,1,0:T(8,128)(2,1)S(1)} all-to-all(bf16[4,112,896]{2,1,0:T(8,128)(2,1)S(1)} %broadcast_in_dim.23), channel_id=1, replica_groups=mesh['layer'=4,'quarter'=4,'y'=4,'half'=2,'x'=4,'core'=2] {'x'}, dimensions={0} | all-to-all | bytes 1605632 | tf_op jit(solution)/shard_map/all_to_all | solution.py:22
  116.0 1.1 convolution_convert_fusion
  117.2 15.3 %all_to_all.38 = bf16[4,112,1024]{2,1,0:T(8,128)(2,1)S(1)} all-to-all(bf16[4,112,1024]{2,1,0:T(8,128)(2,1)S(1)} %bitcast.44), channel_id=1, replica_groups=mesh['layer'=4,'quarter'=4,'y'=4,'half'=2,'x'=4,'core'=2] {'y'}, dimensions={0} | all-to-all | bytes 1835008 | tf_op jit(solution)/shard_map/all_to_all | solution.py:22
  132.6 5.2 %collective-permute-start.2 = (bf16[112,512]{1,0:T(8,128)(2,1)S(1)}, bf16[112,512]{1,0:T(8,128)(2,1)S(1)}, u32[]{:S(2)}, u32[]{:S(2)}) collective-permute-start(bf16[112,512]{1,0:T(8,128)(2,1)S(1)} %get-tuple-element.10), channel_id=1, source_target_pairs={{0,1},{1,0},{2,3},{3,2},{4,5},{5,4},{6,7},{7,6},{8,9},{9,8},{10,11... | collective-permute-start | bytes 344072 | tf_op jit(solution)/shard_map/ppermute | solution.py:62
  137.9 0.9 collective-permute-done.2
  139.5 1.0 broadcast_in_dim.25
  140.5 3.5 %all-to-all-start.5 = ((bf16[4,224,512]{2,1,0:T(8,128)(2,1)}), bf16[4,224,512]{2,1,0:T(8,128)(2,1)S(1)}, u32[]{:S(2)}, u32[]{:S(2)}) async-start(bf16[4,224,512]{2,1,0:T(8,128)(2,1)} %broadcast_in_dim.25), calls=%async_computation.5 | async-start | bytes 1835008 | tf_op jit(solution)/shard_map/all_to_all | solution.py:22
  144.8 2.3 %collective-permute-start.3 = (bf16[448,448]{1,0:T(8,128)(2,1)}, bf16[448,448]{1,0:T(8,128)(2,1)S(1)}, u32[]{:S(2)}, u32[]{:S(2)}) collective-permute-start(bf16[448,448]{1,0:T(8,128)(2,1)} %slice.40), channel_id=1, source_target_pairs={{0,1},{1,0},{2,3},{3,2},{4,5},{5,4},{6,7},{7,6},{8,9},{9,8},{10,11... | collective-permute-start | bytes 1204232 | tf_op jit(solution)/shard_map/ppermute | solution.py:57
  147.1 10.3 %all-to-all-done.5 = bf16[4,224,512]{2,1,0:T(8,128)(2,1)S(1)} async-done(((bf16[4,224,512]{2,1,0:T(8,128)(2,1)}), bf16[4,224,512]{2,1,0:T(8,128)(2,1)S(1)}, u32[]{:S(2)}, u32[]{:S(2)}) %all-to-all-start.5) | async-done | bytes 917536 | tf_op jit(solution)/shard_map/all_to_all | solution.py:22
  157.5 2.5 %convolution_convert_fusion.2 = bf16[448,512]{1,0:T(8,128)(2,1)} fusion(bf16[896,512]{1,0:T(8,128)(2,1)S(1)} %bitcast.43, bf16[448,448]{1,0:T(8,128)(2,1)S(1)} %collective-permute-done.3, bf16[448,448]{1,0:T(8,128)(2,1)} %slice.40), kind=kOutput, calls=%fused_computation.3 | convolution fusion | flops 412876800 | bytes 2179072 | tf_op jit(solution)/shard_map/dot_general | solution.py:14
  160.0 3.5 %all-to-all-start.6 = ((bf16[4,112,512]{2,1,0:T(8,128)(2,1)}), bf16[4,112,512]{2,1,0:T(8,128)(2,1)S(1)}, u32[]{:S(2)}, u32[]{:S(2)}) async-start(bf16[4,112,512]{2,1,0:T(8,128)(2,1)} %bitcast.20), calls=%async_computation.6 | async-start | bytes 917504 | tf_op jit(solution)/shard_map/all_to_all | solution.py:22
  163.7 12.4 %all-to-all-done.6 = bf16[4,112,512]{2,1,0:T(8,128)(2,1)S(1)} async-done(((bf16[4,112,512]{2,1,0:T(8,128)(2,1)}), bf16[4,112,512]{2,1,0:T(8,128)(2,1)S(1)}, u32[]{:S(2)}, u32[]{:S(2)}) %all-to-all-start.6) | async-done | bytes 458784 | tf_op jit(solution)/shard_map/all_to_all | solution.py:22
  (35 shorter events, 4.3 us)
Async XLA Ops:
  10.4 31.6 %collective-permute-start = (bf16[56,1024]{1,0:T(8,128)(2,1)S(1)}, bf16[56,1024]{1,0:T(8,128)(2,1)S(1)}, u32[]{:S(2)}, u32[]{:S(2)}) collective-permute-start(bf16[56,1024]{1,0:T(8,128)(2,1)S(1)} %reshape.61), channel_id=1, source_target_pairs={{0,8},{8,0},{1,9},{9,1},{2,10},{10,2},{3,11},{11,3},{4,12},{12,4},... | collective-permute-start | bytes 344072 | tf_op jit(solution)/shard_map/ppermute | solution.py:44
  43.0 36.0 %all-to-all-start.1 = ((bf16[4,112,1024]{2,1,0:T(8,128)(2,1)}), bf16[4,112,1024]{2,1,0:T(8,128)(2,1)S(1)}, u32[]{:S(2)}, u32[]{:S(2)}) async-start(bf16[4,112,1024]{2,1,0:T(8,128)(2,1)} %broadcast_in_dim.22), calls=%async_computation.1 | async-start | bytes 1835008 | tf_op jit(solution)/shard_map/all_to_all | solution.py:22
  79.1 5.9 %collective-permute-start.1 = (bf16[4,2,56,1024]{3,2,1,0:T(8,128)(2,1)S(1)}, bf16[4,2,56,1024]{3,2,1,0:T(8,128)(2,1)S(1)}, u32[]{:S(2)}, u32[]{:S(2)}) collective-permute-start(bf16[4,2,56,1024]{3,2,1,0:T(8,128)(2,1)S(1)} %bitcast.35), channel_id=1, source_target_pairs={{0,1},{1,0},{2,3},{3,2},{4,5},{5,4},{6,7},{7,6},{8,9},{9,8},{10,11... | collective-permute-start | bytes 2752520 | tf_op jit(solution)/shard_map/ppermute | solution.py:50
  85.2 1.2 copy-start
  132.6 6.2 %copy-start.1 = (bf16[112,512]{1,0:T(8,128)(2,1)}, bf16[112,512]{1,0:T(8,128)(2,1)S(1)}, u32[]{:S(2)}) copy-start(bf16[112,512]{1,0:T(8,128)(2,1)S(1)} %get-tuple-element.9) | copy-start | bytes 344068
  132.6 6.2 %collective-permute-start.2 = (bf16[112,512]{1,0:T(8,128)(2,1)S(1)}, bf16[112,512]{1,0:T(8,128)(2,1)S(1)}, u32[]{:S(2)}, u32[]{:S(2)}) collective-permute-start(bf16[112,512]{1,0:T(8,128)(2,1)S(1)} %get-tuple-element.10), channel_id=1, source_target_pairs={{0,1},{1,0},{2,3},{3,2},{4,5},{5,4},{6,7},{7,6},{8,9},{9,8},{10,11... | collective-permute-start | bytes 344072 | tf_op jit(solution)/shard_map/ppermute | solution.py:62
  138.8 0.6 copy-start.3
  140.5 16.9 %all-to-all-start.5 = ((bf16[4,224,512]{2,1,0:T(8,128)(2,1)}), bf16[4,224,512]{2,1,0:T(8,128)(2,1)S(1)}, u32[]{:S(2)}, u32[]{:S(2)}) async-start(bf16[4,224,512]{2,1,0:T(8,128)(2,1)} %broadcast_in_dim.25), calls=%async_computation.5 | async-start | bytes 1835008 | tf_op jit(solution)/shard_map/all_to_all | solution.py:22
  144.8 12.7 %collective-permute-start.3 = (bf16[448,448]{1,0:T(8,128)(2,1)}, bf16[448,448]{1,0:T(8,128)(2,1)S(1)}, u32[]{:S(2)}, u32[]{:S(2)}) collective-permute-start(bf16[448,448]{1,0:T(8,128)(2,1)} %slice.40), channel_id=1, source_target_pairs={{0,1},{1,0},{2,3},{3,2},{4,5},{5,4},{6,7},{7,6},{8,9},{9,8},{10,11... | collective-permute-start | bytes 1204232 | tf_op jit(solution)/shard_map/ppermute | solution.py:57
  157.5 6.1 %copy-start.2 = (bf16[112,512]{1,0:T(8,128)(2,1)S(1)}, bf16[112,512]{1,0:T(8,128)(2,1)}, u32[]{:S(2)}) copy-start(bf16[112,512]{1,0:T(8,128)(2,1)} %copy-done.1) | copy-start | bytes 344068
  157.5 6.1 %copy-start.4 = (bf16[112,512]{1,0:T(8,128)(2,1)S(1)}, bf16[112,512]{1,0:T(8,128)(2,1)}, u32[]{:S(2)}) copy-start(bf16[112,512]{1,0:T(8,128)(2,1)} %copy-done.3) | copy-start | bytes 344068
  160.0 16.0 %all-to-all-start.6 = ((bf16[4,112,512]{2,1,0:T(8,128)(2,1)}), bf16[4,112,512]{2,1,0:T(8,128)(2,1)S(1)}, u32[]{:S(2)}, u32[]{:S(2)}) async-start(bf16[4,112,512]{2,1,0:T(8,128)(2,1)} %bitcast.20), calls=%async_computation.6 | async-start | bytes 917504 | tf_op jit(solution)/shard_map/all_to_all | solution.py:22

commit v12 on v6

--- a/solution.py
+++ b/solution.py
@@ -39,15 +39,19 @@
     h = w // 2
     n = nx * m
     core = lax.axis_index("core")
-    own = exchange(momentum[0].reshape(m, nx, w).transpose(1, 0, 2), "x").reshape(n, w)
+    rows = jnp.stack([momentum[0, :, i * w : (i + 1) * w] for i in range(nx)])
+    own = exchange(rows, "x").reshape(n, w)
     other = lax.ppermute(own, "half", SWAP)
 
-    both = jnp.stack([own, other])
 
-    right = spread(both, "quarter").transpose(1, 0, 2, 3).reshape(2 * nq * n, w)
-    line = lax.all_gather(both.reshape(2 * n, w), "y", axis=0)
+    early = lax.all_gather(own, "y", axis=0)
+    early, other = lax.optimization_barrier((early, other))
+    line = jnp.stack([early, lax.all_gather(other, "y", axis=0)])
     left = jnp.stack(ordered(core, line, lax.ppermute(line, "core", SWAP)), 1)
-    left = left.reshape(ny * nc * 2 * n, w)
+    tile = lax.dynamic_index_in_dim(left[0], lax.axis_index("y"), 1, False).reshape(nc * n, w)
+    left = left.reshape(2 * nc * ny * n, w)
+    right = spread(jnp.concatenate([own, other], 0), "quarter").reshape(nq, 2, n, w)
+    right = right.transpose(1, 0, 2, 3).reshape(2 * nq * n, w)
 
     term = dot(right, left, ((1,), (1,))).astype(bf16)
     mine = total(exchange(term.reshape(nx, 2 * n, 16 * n), "x")).astype(bf16)
@@ -61,15 +65,14 @@
     got = lax.ppermute(send, "core", SWAP)
     keep = dot(gram, keep, ((0,), (0,)))
     term = (keep + got.astype(jnp.float32)).astype(bf16)
-    term, narrow = lax.optimization_barrier((exchange(term.reshape(ny, 4 * n, h), "y"), narrow))
+    term = term.reshape(2 * nc, ny, n, h).transpose(1, 0, 2, 3).reshape(ny, 4 * n, h)
+    term, narrow = lax.optimization_barrier((exchange(term, "y"), narrow))
     first = total(term).astype(bf16)
-    firsts = lax.all_gather(first, "y", axis=0, tiled=True)
+    firsts = lax.all_gather(first.reshape(2 * nc, n, h), "y", axis=1).reshape(16 * n, h)
 
     term = dot(narrow, firsts, ((1,), (0,))).astype(bf16)
     second = total(exchange(term.reshape(nq, nc * n, h), "quarter"))
-    first = first.reshape(nc, 2, n, h)[:, 0].reshape(nc * n, h)
-    tile = lax.dynamic_index_in_dim(left.reshape(ny, nc, 2, n, w), lax.axis_index("y"), 0, False)
-    tile = tile[:, 0].reshape(nc * n, w)
+    first = first[: nc * n]
     tile = jnp.where(core == 0, tile[:, :h], tile[:, h:])
     mixed = A1 * tile.astype(jnp.float32) + A2 * first.astype(jnp.float32) + A3 * second
     mixed = math.sqrt(max(256 * m, k)) * mixed

time: 173 us -> 172 us (level)
  the two profiles are of different devices: /device:TPU:8 before, /device:TPU:384 now
where the time goes in v12:
time: 172 us; the launch traced here: 171 us
  blocking collectives  81.6 us (47%)
  starting transfers between devices  38.6 us (22%)
  waiting for transfers between devices  33.7 us (20%)
  other arithmetic  6.12 us (4%)
  local copies, waits for them, and re-layouts  5.73 us (3%)
  matrix products  5.09 us (3%)
    all_to_all x2, blocking collectives, exchange(): return lax.all_to_all(blocks, axis, 0, 0, tiled=True)  25.5 us
    all_to_all x3, waiting for transfers between devices, exchange(): return lax.all_to_all(blocks, axis, 0, 0, tiled=True)  21.2 us
    all_to_all x3, starting transfers between devices, exchange(): return lax.all_to_all(blocks, axis, 0, 0, tiled=True)  17.8 us
    all_gather x1, blocking collectives, shards(): lax.all_gather(first.reshape(2 * nc, n, h), 'y', axis=1).reshape(16 * n, h)  14.7 us
    all_gather x1, blocking collectives, shards(): gram = lax.all_gather(mine, 'x', axis=0, tiled=True)  14.6 us
    ppermute x1, starting transfers between devices, shards(): other = lax.ppermute(own, 'half', SWAP)  14.6 us
    all_gather x1, blocking collectives, shards(): early = lax.all_gather(own, 'y', axis=0)  13.8 us
    all_gather x1, blocking collectives, shards(): line = jnp.stack([early, lax.all_gather(other, 'y', axis=0)])  13.1 us
  transfers between devices with their start and end apart: 7, of which 4 were waited for; matrix products, arithmetic and copies ran while one was open for 4% of the time, Pallas kernels for 0%

profile of v12, /device:TPU:384, one launch (start us, length us, event | category | flops | bytes accessed | tf_op | source)
XLA Modules:
  0.0 171.0 jit_solution(3671014772995322595)
XLA Ops:
  0.9 10.1 %all_to_all.25 = bf16[4,14,1024]{2,1,0:T(8,128)(2,1)S(1)} all-to-all(bf16[4,14,1024]{2,1,0:T(8,128)(2,1)S(1)} %pad_maximum_fusion.4), channel_id=1, replica_groups=mesh['layer'=4,'quarter'=4,'y'=4,'half'=2,'x'=4,'core'=2] {'x'}, dimensions={0} | all-to-all | bytes 229376 | tf_op jit(solution)/shard_map/all_to_all | solution.py:22
  11.0 14.6 %collective-permute-start = (bf16[56,1024]{1,0:T(8,128)(2,1)S(1)}, bf16[56,1024]{1,0:T(8,128)(2,1)S(1)}, u32[]{:S(2)}, u32[]{:S(2)}) collective-permute-start(bf16[56,1024]{1,0:T(8,128)(2,1)S(1)} %reshape.54), channel_id=1, source_target_pairs={{0,8},{8,0},{1,9},{9,1},{2,10},{10,2},{3,11},{11,3},{4,12},{12,4},... | collective-permute-start | bytes 344072 | tf_op jit(solution)/shard_map/ppermute | solution.py:44
  25.6 13.8 %all_gather.15 = bf16[4,56,1024]{2,1,0:T(8,128)(2,1)S(1)} all-gather(bf16[1,56,1024]{2,1,0:T(8,128)(2,1)S(1)} %all_gather_reshape.6), channel_id=1, replica_groups=mesh['layer'=4,'quarter'=4,'y'=4,'half'=2,'x'=4,'core'=2] {'y'}, dimensions={0}, use_global_device_ids=true | all-gather | bytes 573440 | tf_op jit(solution)/shard_map/all_gather | solution.py:47
  39.3 9.9 %collective-permute-done = bf16[56,1024]{1,0:T(8,128)(2,1)S(1)} collective-permute-done((bf16[56,1024]{1,0:T(8,128)(2,1)S(1)}, bf16[56,1024]{1,0:T(8,128)(2,1)S(1)}, u32[]{:S(2)}, u32[]{:S(2)}) %collective-permute-start) | collective-permute-done | bytes 114720 | tf_op jit(solution)/shard_map/ppermute | solution.py:44
  50.3 8.9 %all-to-all-start.1 = ((bf16[4,112,1024]{2,1,0:T(8,128)(2,1)}), bf16[4,112,1024]{2,1,0:T(8,128)(2,1)}, u32[]{:S(2)}, u32[]{:S(2)}) async-start(bf16[4,112,1024]{2,1,0:T(8,128)(2,1)} %broadcast_in_dim.2), calls=%async_computation.1 | async-start | bytes 1835008 | tf_op jit(solution)/shard_map/all_to_all | solution.py:22
  59.2 13.1 %all-gather = bf16[224,1024]{1,0:T(8,128)(2,1)S(1)} all-gather(bf16[56,1024]{1,0:T(8,128)(2,1)S(1)} %collective-permute-done), channel_id=2, replica_groups=mesh['layer'=4,'quarter'=4,'y'=4,'half'=2,'x'=4,'core'=2] {'y'}, dimensions={0}, use_global_device_ids=true | all-gather | bytes 573440 | tf_op jit(solution)/shard_map/all_gather | solution.py:49
  72.4 1.9 %collective-permute-start.1 = (bf16[2,4,56,1024]{3,2,1,0:T(8,128)(2,1)S(1)}, bf16[2,4,56,1024]{3,2,1,0:T(8,128)(2,1)}, u32[]{:S(2)}, u32[]{:S(2)}) collective-permute-start(bf16[2,4,56,1024]{3,2,1,0:T(8,128)(2,1)S(1)} %pad_maximum_fusion.1), channel_id=1, source_target_pairs={{0,1},{1,0},{2,3},{3,2},{4,5},{5,4},{6,7},{7,6},{8,9},{9,8},{10,11... | collective-permute-start | bytes 2752520 | tf_op jit(solution)/shard_map/ppermute | solution.py:50
  74.4 2.6 %collective-permute-done.1 = bf16[2,4,56,1024]{3,2,1,0:T(8,128)(2,1)} collective-permute-done((bf16[2,4,56,1024]{3,2,1,0:T(8,128)(2,1)S(1)}, bf16[2,4,56,1024]{3,2,1,0:T(8,128)(2,1)}, u32[]{:S(2)}, u32[]{:S(2)}) %collective-permute-start.1) | collective-permute-done | bytes 917536 | tf_op jit(solution)/shard_map/ppermute | solution.py:50
  76.9 1.3 select_bitcast_fusion.1
  78.3 1.4 pad_maximum_fusion
  79.7 1.4 copy.12
  81.4 1.2 convolution_convert_fusion.1
  82.6 15.4 %all_to_all.26 = bf16[4,112,896]{2,1,0:T(8,128)(2,1)S(1)} all-to-all(bf16[4,112,896]{2,1,0:T(8,128)(2,1)S(1)} %bitcast.52), channel_id=1, replica_groups=mesh['layer'=4,'quarter'=4,'y'=4,'half'=2,'x'=4,'core'=2] {'x'}, dimensions={0} | all-to-all | bytes 1605632 | tf_op jit(solution)/shard_map/all_to_all | solution.py:22
  98.9 14.6 %all_gather.18 = bf16[448,896]{1,0:T(8,128)(2,1)S(1)} all-gather(bf16[112,896]{1,0:T(8,128)(2,1)} %reduce_sum.33), channel_id=1, replica_groups=mesh['layer'=4,'quarter'=4,'y'=4,'half'=2,'x'=4,'core'=2] {'x'}, dimensions={0}, use_global_device_ids=true | all-gather | bytes 1003520 | tf_op jit(solution)/shard_map/all_gather | solution.py:58
  114.1 1.9 %collective-permute-start.2 = (bf16[896,512]{1,0:T(8,128)(2,1)S(1)}, bf16[896,512]{1,0:T(8,128)(2,1)S(1)}, u32[]{:S(2)}, u32[]{:S(2)}) collective-permute-start(bf16[896,512]{1,0:T(8,128)(2,1)S(1)} %convolution_convert_fusion), channel_id=1, source_target_pairs={{0,1},{1,0},{2,3},{3,2},{4,5},{5,4},{6,7},{7,6},{8,9},{9,8},{10,11... | collective-permute-start | bytes 2752520 | tf_op jit(solution)/shard_map/ppermute | solution.py:65
  116.1 2.4 %collective-permute-start.3 = (bf16[4,56,896]{2,1,0:T(8,128)(2,1)S(1)}, bf16[4,56,896]{2,1,0:T(8,128)(2,1)}, u32[]{:S(2)}, u32[]{:S(2)}) collective-permute-start(bf16[4,56,896]{2,1,0:T(8,128)(2,1)S(1)} %bitcast.42), channel_id=1, source_target_pairs={{0,1},{1,0},{2,3},{3,2},{4,5},{5,4},{6,7},{7,6},{8,9},{9,8},{10,11... | collective-permute-start | bytes 1204232 | tf_op jit(solution)/shard_map/ppermute | solution.py:60
  119.2 1.0 copy.13
  120.2 3.8 %all-to-all-start.3 = ((bf16[4,224,512]{2,1,0:T(8,128)(2,1)}), bf16[4,224,512]{2,1,0:T(8,128)(2,1)S(1)}, u32[]{:S(2)}, u32[]{:S(2)}) async-start(bf16[4,224,512]{2,1,0:T(8,128)(2,1)} %bitcast.13), calls=%async_computation.3 | async-start | bytes 1835008 | tf_op jit(solution)/shard_map/all_to_all | solution.py:22
  124.0 1.1 select_bitcast_fusion.3
  126.1 11.9 %all-to-all-done.3 = bf16[4,224,512]{2,1,0:T(8,128)(2,1)S(1)} async-done(((bf16[4,224,512]{2,1,0:T(8,128)(2,1)}), bf16[4,224,512]{2,1,0:T(8,128)(2,1)S(1)}, u32[]{:S(2)}, u32[]{:S(2)}) %all-to-all-start.3) | async-done | bytes 917536 | tf_op jit(solution)/shard_map/all_to_all | solution.py:22
  138.2 14.7 %all_gather.19 = bf16[4,4,56,512]{3,2,1,0:T(8,128)(2,1)S(1)} all-gather(bf16[4,1,56,512]{3,2,1,0:T(8,128)(2,1)S(1)} %bitcast.44), channel_id=1, replica_groups=mesh['layer'=4,'quarter'=4,'y'=4,'half'=2,'x'=4,'core'=2] {'y'}, dimensions={1}, use_global_device_ids=true | all-gather | bytes 1146880 | tf_op jit(solution)/shard_map/all_gather | solution.py:71
  152.8 2.6 %convolution_convert_fusion.2 = bf16[448,512]{1,0:T(8,128)(2,1)} fusion(bf16[448,896]{1,0:T(8,128)(2,1)} %bitcast.51, bf16[896,512]{1,0:T(8,128)(2,1)S(1)} %bitcast.49), kind=kOutput, calls=%fused_computation.6 | convolution fusion | flops 411271168 | bytes 2179072 | tf_op jit(solution)/shard_map/dot_general | solution.py:14
  155.4 5.1 %all-to-all-start.4 = ((bf16[4,112,512]{2,1,0:T(8,128)(2,1)}), bf16[4,112,512]{2,1,0:T(8,128)(2,1)S(1)}, u32[]{:S(2)}, u32[]{:S(2)}) async-start(bf16[4,112,512]{2,1,0:T(8,128)(2,1)} %bitcast.21), calls=%async_computation.4 | async-start | bytes 917504 | tf_op jit(solution)/shard_map/all_to_all | solution.py:22
  160.7 9.3 %all-to-all-done.4 = bf16[4,112,512]{2,1,0:T(8,128)(2,1)S(1)} async-done(((bf16[4,112,512]{2,1,0:T(8,128)(2,1)}), bf16[4,112,512]{2,1,0:T(8,128)(2,1)S(1)}, u32[]{:S(2)}, u32[]{:S(2)}) %all-to-all-start.4) | async-done | bytes 458784 | tf_op jit(solution)/shard_map/all_to_all | solution.py:22
  (25 shorter events, 7.0 us)
Async XLA Ops:
  11.0 38.3 %collective-permute-start = (bf16[56,1024]{1,0:T(8,128)(2,1)S(1)}, bf16[56,1024]{1,0:T(8,128)(2,1)S(1)}, u32[]{:S(2)}, u32[]{:S(2)}) collective-permute-start(bf16[56,1024]{1,0:T(8,128)(2,1)S(1)} %reshape.54), channel_id=1, source_target_pairs={{0,8},{8,0},{1,9},{9,1},{2,10},{10,2},{3,11},{11,3},{4,12},{12,4},... | collective-permute-start | bytes 344072 | tf_op jit(solution)/shard_map/ppermute | solution.py:44
  50.3 29.4 %all-to-all-start.1 = ((bf16[4,112,1024]{2,1,0:T(8,128)(2,1)}), bf16[4,112,1024]{2,1,0:T(8,128)(2,1)}, u32[]{:S(2)}, u32[]{:S(2)}) async-start(bf16[4,112,1024]{2,1,0:T(8,128)(2,1)} %broadcast_in_dim.2), calls=%async_computation.1 | async-start | bytes 1835008 | tf_op jit(solution)/shard_map/all_to_all | solution.py:22
  72.4 4.5 %collective-permute-start.1 = (bf16[2,4,56,1024]{3,2,1,0:T(8,128)(2,1)S(1)}, bf16[2,4,56,1024]{3,2,1,0:T(8,128)(2,1)}, u32[]{:S(2)}, u32[]{:S(2)}) collective-permute-start(bf16[2,4,56,1024]{3,2,1,0:T(8,128)(2,1)S(1)} %pad_maximum_fusion.1), channel_id=1, source_target_pairs={{0,1},{1,0},{2,3},{3,2},{4,5},{5,4},{6,7},{7,6},{8,9},{9,8},{10,11... | collective-permute-start | bytes 2752520 | tf_op jit(solution)/shard_map/ppermute | solution.py:50
  79.7 1.8 %copy-start = (bf16[2,2,4,56,1024]{4,3,2,1,0:T(8,128)(2,1)S(1)}, bf16[2,2,4,56,1024]{4,3,2,1,0:T(8,128)(2,1)}, u32[]{:S(2)}) copy-start(bf16[2,2,4,56,1024]{4,3,2,1,0:T(8,128)(2,1)} %pad_maximum_fusion) | copy-start | bytes 5505028
  114.1 4.4 %collective-permute-start.2 = (bf16[896,512]{1,0:T(8,128)(2,1)S(1)}, bf16[896,512]{1,0:T(8,128)(2,1)S(1)}, u32[]{:S(2)}, u32[]{:S(2)}) collective-permute-start(bf16[896,512]{1,0:T(8,128)(2,1)S(1)} %convolution_convert_fusion), channel_id=1, source_target_pairs={{0,1},{1,0},{2,3},{3,2},{4,5},{5,4},{6,7},{7,6},{8,9},{9,8},{10,11... | collective-permute-start | bytes 2752520 | tf_op jit(solution)/shard_map/ppermute | solution.py:65
  116.1 7.9 %collective-permute-start.3 = (bf16[4,56,896]{2,1,0:T(8,128)(2,1)S(1)}, bf16[4,56,896]{2,1,0:T(8,128)(2,1)}, u32[]{:S(2)}, u32[]{:S(2)}) collective-permute-start(bf16[4,56,896]{2,1,0:T(8,128)(2,1)S(1)} %bitcast.42), channel_id=1, source_target_pairs={{0,1},{1,0},{2,3},{3,2},{4,5},{5,4},{6,7},{7,6},{8,9},{9,8},{10,11... | collective-permute-start | bytes 1204232 | tf_op jit(solution)/shard_map/ppermute | solution.py:60
  120.2 17.7 %all-to-all-start.3 = ((bf16[4,224,512]{2,1,0:T(8,128)(2,1)}), bf16[4,224,512]{2,1,0:T(8,128)(2,1)S(1)}, u32[]{:S(2)}, u32[]{:S(2)}) async-start(bf16[4,224,512]{2,1,0:T(8,128)(2,1)} %bitcast.13), calls=%async_computation.3 | async-start | bytes 1835008 | tf_op jit(solution)/shard_map/all_to_all | solution.py:22
  155.4 14.7 %all-to-all-start.4 = ((bf16[4,112,512]{2,1,0:T(8,128)(2,1)}), bf16[4,112,512]{2,1,0:T(8,128)(2,1)S(1)}, u32[]{:S(2)}, u32[]{:S(2)}) async-start(bf16[4,112,512]{2,1,0:T(8,128)(2,1)} %bitcast.21), calls=%async_computation.4 | async-start | bytes 917504 | tf_op jit(solution)/shard_map/all_to_all | solution.py:22

commit v13 on v9

--- a/solution.py
+++ b/solution.py
@@ -31,6 +31,10 @@
     return jnp.where(core == 0, mine, other), jnp.where(core == 0, other, mine)
 
 
+def half_pairs(layers):
+    return [(2 * i + g, 2 * i + 1 - g) for i in layers for g in range(2)]
+
+
 def shards(momentum):
     bf16 = jnp.bfloat16
     _, m, k = momentum.shape
@@ -40,8 +44,12 @@
     n = nx * m
     core = lax.axis_index("core")
     rows = jnp.stack([momentum[0, :, i * w : (i + 1) * w] for i in range(nx)])
+    layers = lax.axis_size("layer")
+    early = lax.ppermute(rows, ("layer", "half"), half_pairs(range(layers // 2)))
     own = exchange(rows, "x").reshape(n, w)
-    other = lax.ppermute(own, "half", SWAP)
+    late = lax.ppermute(own, ("layer", "half"), half_pairs(range(layers // 2, layers)))
+    early = exchange(early, "x").reshape(n, w)
+    other = jnp.where(lax.axis_index("layer") < layers // 2, early, late)
 
     both = jnp.stack([own, other])
     block = spread(both, "quarter")

time: 167 us -> 173 us (1.036)
  the two profiles are of different devices: /device:TPU:8 before, /device:TPU:256 now
where the time goes in v13:
time: 173 us; the launch traced here: 172 us
  blocking collectives  83 us (48%)
  starting transfers between devices  52.8 us (31%)
  waiting for transfers between devices  27.4 us (16%)
  matrix products  3.71 us (2%)
  local copies, waits for them, and re-layouts  2.86 us (2%)
  other arithmetic  2.08 us (1%)
    all_to_all x3, blocking collectives, exchange(): return lax.all_to_all(blocks, axis, 0, 0, tiled=True)  39.9 us
    all_to_all x3, starting transfers between devices, exchange(): return lax.all_to_all(blocks, axis, 0, 0, tiled=True)  25.9 us
    all_to_all x3, waiting for transfers between devices, exchange(): return lax.all_to_all(blocks, axis, 0, 0, tiled=True)  24.8 us
    ppermute x1, starting transfers between devices, shards(): lax.ppermute(own, ('layer', 'half'), half_pairs(range(layers // 2, layers)))  19.4 us
    all_gather x1, blocking collectives, shards(): firsts = lax.all_gather(first, 'y', axis=1).reshape(nc * ny * 2 * n, h)  14.4 us
    all_gather x1, blocking collectives, shards(): gram = lax.all_gather(mine, 'x', axis=0, tiled=True)  14.4 us
    all_gather x1, blocking collectives, shards(): left = lax.all_gather(both, 'y', axis=0).reshape(ny * 2 * n, w)  14.2 us
    dot_general x3, matrix products, dot(): lax.dot_general(lhs, rhs, (dims, ((), ())), preferred_element_type=jnp.fl...  3.71 us
  transfers between devices with their start and end apart: 8, of which 4 were waited for; matrix products, arithmetic and copies ran while one was open for 0% of the time, Pallas kernels for 0%

profile of v13, /device:TPU:256, one launch (start us, length us, event | category | flops | bytes accessed | tf_op | source)
XLA Modules:
  0.0 172.1 jit_solution(11434722361756862885)
XLA Ops:
  0.0 0.8 fusion.5
  0.9 1.3 collective-permute-start
  2.2 10.1 %all_to_all.30 = bf16[4,14,1024]{2,1,0:T(8,128)(2,1)S(1)} all-to-all(bf16[4,14,1024]{2,1,0:T(8,128)(2,1)S(1)} %pad_maximum_fusion.3), channel_id=1, replica_groups=mesh['layer'=4,'quarter'=4,'y'=4,'half'=2,'x'=4,'core'=2] {'x'}, dimensions={0} | all-to-all | bytes 229376 | tf_op jit(solution)/shard_map/all_to_all | solution.py:22
  12.3 19.4 %collective-permute-start.1 = (bf16[56,1024]{1,0:T(8,128)(2,1)S(1)}, bf16[56,1024]{1,0:T(8,128)(2,1)S(1)}, u32[]{:S(2)}, u32[]{:S(2)}) collective-permute-start(bf16[56,1024]{1,0:T(8,128)(2,1)S(1)} %reshape.54), channel_id=1, source_target_pairs={{512,520},{520,512},{768,776},{776,768},{513,521},{521,513},{769,7... | collective-permute-start | bytes 344072 | tf_op jit(solution)/shard_map/ppermute | solution.py:50
  31.6 3.3 %all-to-all-start.1 = ((bf16[4,14,1024]{2,1,0:T(8,128)(2,1)}), bf16[4,14,1024]{2,1,0:T(8,128)(2,1)S(1)}, u32[]{:S(2)}, u32[]{:S(2)}) async-start(bf16[4,14,1024]{2,1,0:T(8,128)(2,1)} %collective-permute-done), calls=%async_computation.1 | async-start | bytes 262144 | tf_op jit(solution)/shard_map/all_to_all | solution.py:22
  35.0 5.9 %all-to-all-done.1 = bf16[4,14,1024]{2,1,0:T(8,128)(2,1)S(1)} async-done(((bf16[4,14,1024]{2,1,0:T(8,128)(2,1)}), bf16[4,14,1024]{2,1,0:T(8,128)(2,1)S(1)}, u32[]{:S(2)}, u32[]{:S(2)}) %all-to-all-start.1) | async-done | bytes 114720 | tf_op jit(solution)/shard_map/all_to_all | solution.py:22
  41.0 1.0 broadcast_in_dim.4
  42.1 19.1 %all-to-all-start.2 = ((bf16[4,2,56,1024]{3,2,1,0:T(8,128)(2,1)}), bf16[4,2,56,1024]{3,2,1,0:T(8,128)(2,1)S(1)}, u32[]{:S(2)}, u32[]{:S(2)}) async-start(bf16[4,2,56,1024]{3,2,1,0:T(8,128)(2,1)} %broadcast_in_dim.4), calls=%async_computation.2 | async-start | bytes 1835008 | tf_op jit(solution)/shard_map/all_to_all | solution.py:22
  61.2 14.2 %all-gather = bf16[8,56,1024]{2,1,0:T(8,128)(2,1)S(1)} all-gather(bf16[2,56,1024]{2,1,0:T(8,128)(2,1)S(1)} %pad_maximum_fusion.1), channel_id=2, replica_groups=mesh['layer'=4,'quarter'=4,'y'=4,'half'=2,'x'=4,'core'=2] {'y'}, dimensions={0}, use_global_device_ids=true | all-gather | bytes 1146880 | tf_op jit(solution)/shard_map/all_gather | solution.py:56
  75.4 8.8 %all-to-all-done.2 = bf16[4,2,56,1024]{3,2,1,0:T(8,128)(2,1)S(1)} async-done(((bf16[4,2,56,1024]{3,2,1,0:T(8,128)(2,1)}), bf16[4,2,56,1024]{3,2,1,0:T(8,128)(2,1)S(1)}, u32[]{:S(2)}, u32[]{:S(2)}) %all-to-all-start.2) | async-done | bytes 917536 | tf_op jit(solution)/shard_map/all_to_all | solution.py:22
  84.3 1.9 %collective-permute-start.2 = (bf16[4,2,56,1024]{3,2,0,1:T(8,128)(2,1)S(1)}, bf16[4,2,56,1024]{3,2,0,1:T(8,128)(2,1)}, u32[]{:S(2)}, u32[]{:S(2)}) collective-permute-start(bf16[4,2,56,1024]{3,2,0,1:T(8,128)(2,1)S(1)} %copy.5), channel_id=1, source_target_pairs={{0,1},{1,0},{2,3},{3,2},{4,5},{5,4},{6,7},{7,6},{8,9},{9,8},{10,11... | collective-permute-start | bytes 2752520 | tf_op jit(solution)/shard_map/ppermute | solution.py:58
  86.2 2.6 %collective-permute-done.2 = bf16[4,2,56,1024]{3,2,0,1:T(8,128)(2,1)} collective-permute-done((bf16[4,2,56,1024]{3,2,0,1:T(8,128)(2,1)S(1)}, bf16[4,2,56,1024]{3,2,0,1:T(8,128)(2,1)}, u32[]{:S(2)}, u32[]{:S(2)}) %collective-permute-start.2) | collective-permute-done | bytes 917536 | tf_op jit(solution)/shard_map/ppermute | solution.py:58
  88.8 1.3 select_bitcast_fusion.1
  90.3 1.1 convolution_convert_fusion.1
  91.4 15.4 %all_to_all.31 = bf16[4,112,896]{2,1,0:T(8,128)(2,1)S(1)} all-to-all(bf16[4,112,896]{2,1,0:T(8,128)(2,1)S(1)} %bitcast.37), channel_id=1, replica_groups=mesh['layer'=4,'quarter'=4,'y'=4,'half'=2,'x'=4,'core'=2] {'x'}, dimensions={0} | all-to-all | bytes 1605632 | tf_op jit(solution)/shard_map/all_to_all | solution.py:22
  107.0 14.4 %all_gather.14 = bf16[448,896]{1,0:T(8,128)(2,1)S(1)} all-gather(bf16[112,896]{1,0:T(8,128)(2,1)S(1)} %reduce_sum.45), channel_id=1, replica_groups=mesh['layer'=4,'quarter'=4,'y'=4,'half'=2,'x'=4,'core'=2] {'x'}, dimensions={0}, use_global_device_ids=true | all-gather | bytes 1003520 | tf_op jit(solution)/shard_map/all_gather | solution.py:63
  121.3 1.1 convolution_convert_fusion
  122.5 14.5 %all_to_all.32 = bf16[4,112,1024]{2,1,0:T(8,128)(2,1)S(1)} all-to-all(bf16[4,112,1024]{2,1,0:T(8,128)(2,1)S(1)} %bitcast.34), channel_id=1, replica_groups=mesh['layer'=4,'quarter'=4,'y'=4,'half'=2,'x'=4,'core'=2] {'y'}, dimensions={0} | all-to-all | bytes 1835008 | tf_op jit(solution)/shard_map/all_to_all | solution.py:22
  137.1 1.9 %collective-permute-start.3 = (bf16[112,512]{1,0:T(8,128)(2,1)S(1)}, bf16[112,512]{1,0:T(8,128)(2,1)S(1)}, u32[]{:S(2)}, u32[]{:S(2)}) collective-permute-start(bf16[112,512]{1,0:T(8,128)(2,1)S(1)} %get-tuple-element.10), channel_id=1, source_target_pairs={{0,1},{1,0},{2,3},{3,2},{4,5},{5,4},{6,7},{7,6},{8,9},{9,8},{10,11... | collective-permute-start | bytes 344072 | tf_op jit(solution)/shard_map/ppermute | solution.py:70
  139.1 2.4 %collective-permute-start.4 = (bf16[448,448]{1,0:T(8,128)(2,1)S(1)}, bf16[448,448]{1,0:T(8,128)(2,1)S(1)}, u32[]{:S(2)}, u32[]{:S(2)}) collective-permute-start(bf16[448,448]{1,0:T(8,128)(2,1)S(1)} %slice.40), channel_id=1, source_target_pairs={{0,1},{1,0},{2,3},{3,2},{4,5},{5,4},{6,7},{7,6},{8,9},{9,8},{10,11... | collective-permute-start | bytes 1204232 | tf_op jit(solution)/shard_map/ppermute | solution.py:65
  141.5 14.4 %all-gather.1 = bf16[2,448,512]{2,1,0:T(8,128)(2,1)S(1)} all-gather(bf16[2,112,512]{2,1,0:T(8,128)(2,1)S(1)} %pad_maximum_fusion.2), channel_id=3, replica_groups=mesh['layer'=4,'quarter'=4,'y'=4,'half'=2,'x'=4,'core'=2] {'y'}, dimensions={1}, use_global_device_ids=true | all-gather | bytes 1146880 | tf_op jit(solution)/shard_map/all_gather | solution.py:72
  156.0 1.4 convolution_convert_fusion.2
  157.4 3.5 %all-to-all-start.5 = ((bf16[4,112,512]{2,1,0:T(8,128)(2,1)}), bf16[4,112,512]{2,1,0:T(8,128)(2,1)S(1)}, u32[]{:S(2)}, u32[]{:S(2)}) async-start(bf16[4,112,512]{2,1,0:T(8,128)(2,1)} %bitcast.15), calls=%async_computation.5 | async-start | bytes 917504 | tf_op jit(solution)/shard_map/all_to_all | solution.py:22
  161.1 10.2 %all-to-all-done.5 = bf16[4,112,512]{2,1,0:T(8,128)(2,1)S(1)} async-done(((bf16[4,112,512]{2,1,0:T(8,128)(2,1)}), bf16[4,112,512]{2,1,0:T(8,128)(2,1)S(1)}, u32[]{:S(2)}, u32[]{:S(2)}) %all-to-all-start.5) | async-done | bytes 458784 | tf_op jit(solution)/shard_map/all_to_all | solution.py:22
  (27 shorter events, 1.8 us)
Async XLA Ops:
  0.9 30.8 %collective-permute-start = (bf16[4,14,1024]{2,1,0:T(8,128)(2,1)S(1)}, bf16[4,14,1024]{2,1,0:T(8,128)(2,1)}, u32[]{:S(2)}, u32[]{:S(2)}) collective-permute-start(bf16[4,14,1024]{2,1,0:T(8,128)(2,1)S(1)} %pad_maximum_fusion.3), channel_id=1, source_target_pairs={{0,8},{8,0},{256,264},{264,256},{1,9},{9,1},{257,265},{265,257},{2... | collective-permute-start | bytes 344072 | tf_op jit(solution)/shard_map/ppermute | solution.py:48
  12.3 28.7 %collective-permute-start.1 = (bf16[56,1024]{1,0:T(8,128)(2,1)S(1)}, bf16[56,1024]{1,0:T(8,128)(2,1)S(1)}, u32[]{:S(2)}, u32[]{:S(2)}) collective-permute-start(bf16[56,1024]{1,0:T(8,128)(2,1)S(1)} %reshape.54), channel_id=1, source_target_pairs={{512,520},{520,512},{768,776},{776,768},{513,521},{521,513},{769,7... | collective-permute-start | bytes 344072 | tf_op jit(solution)/shard_map/ppermute | solution.py:50
  31.6 9.3 %all-to-all-start.1 = ((bf16[4,14,1024]{2,1,0:T(8,128)(2,1)}), bf16[4,14,1024]{2,1,0:T(8,128)(2,1)S(1)}, u32[]{:S(2)}, u32[]{:S(2)}) async-start(bf16[4,14,1024]{2,1,0:T(8,128)(2,1)} %collective-permute-done), calls=%async_computation.1 | async-start | bytes 262144 | tf_op jit(solution)/shard_map/all_to_all | solution.py:22
  42.1 42.1 %all-to-all-start.2 = ((bf16[4,2,56,1024]{3,2,1,0:T(8,128)(2,1)}), bf16[4,2,56,1024]{3,2,1,0:T(8,128)(2,1)S(1)}, u32[]{:S(2)}, u32[]{:S(2)}) async-start(bf16[4,2,56,1024]{3,2,1,0:T(8,128)(2,1)} %broadcast_in_dim.4), calls=%async_computation.2 | async-start | bytes 1835008 | tf_op jit(solution)/shard_map/all_to_all | solution.py:22
  84.3 4.5 %collective-permute-start.2 = (bf16[4,2,56,1024]{3,2,0,1:T(8,128)(2,1)S(1)}, bf16[4,2,56,1024]{3,2,0,1:T(8,128)(2,1)}, u32[]{:S(2)}, u32[]{:S(2)}) collective-permute-start(bf16[4,2,56,1024]{3,2,0,1:T(8,128)(2,1)S(1)} %copy.5), channel_id=1, source_target_pairs={{0,1},{1,0},{2,3},{3,2},{4,5},{5,4},{6,7},{7,6},{8,9},{9,8},{10,11... | collective-permute-start | bytes 2752520 | tf_op jit(solution)/shard_map/ppermute | solution.py:58
  137.1 4.4 %collective-permute-start.3 = (bf16[112,512]{1,0:T(8,128)(2,1)S(1)}, bf16[112,512]{1,0:T(8,128)(2,1)S(1)}, u32[]{:S(2)}, u32[]{:S(2)}) collective-permute-start(bf16[112,512]{1,0:T(8,128)(2,1)S(1)} %get-tuple-element.10), channel_id=1, source_target_pairs={{0,1},{1,0},{2,3},{3,2},{4,5},{5,4},{6,7},{7,6},{8,9},{9,8},{10,11... | collective-permute-start | bytes 344072 | tf_op jit(solution)/shard_map/ppermute | solution.py:70
  139.1 16.9 %collective-permute-start.4 = (bf16[448,448]{1,0:T(8,128)(2,1)S(1)}, bf16[448,448]{1,0:T(8,128)(2,1)S(1)}, u32[]{:S(2)}, u32[]{:S(2)}) collective-permute-start(bf16[448,448]{1,0:T(8,128)(2,1)S(1)} %slice.40), channel_id=1, source_target_pairs={{0,1},{1,0},{2,3},{3,2},{4,5},{5,4},{6,7},{7,6},{8,9},{9,8},{10,11... | collective-permute-start | bytes 1204232 | tf_op jit(solution)/shard_map/ppermute | solution.py:65
  157.4 13.8 %all-to-all-start.5 = ((bf16[4,112,512]{2,1,0:T(8,128)(2,1)}), bf16[4,112,512]{2,1,0:T(8,128)(2,1)S(1)}, u32[]{:S(2)}, u32[]{:S(2)}) async-start(bf16[4,112,512]{2,1,0:T(8,128)(2,1)} %bitcast.15), calls=%async_computation.5 | async-start | bytes 917504 | tf_op jit(solution)/shard_map/all_to_all | solution.py:22

commit v14 on v13

--- a/solution.py
+++ b/solution.py
@@ -45,11 +45,11 @@
     core = lax.axis_index("core")
     rows = jnp.stack([momentum[0, :, i * w : (i + 1) * w] for i in range(nx)])
     layers = lax.axis_size("layer")
-    early = lax.ppermute(rows, ("layer", "half"), half_pairs(range(layers // 2)))
+    early = lax.ppermute(rows, ("layer", "half"), half_pairs(range(layers // 4)))
     own = exchange(rows, "x").reshape(n, w)
-    late = lax.ppermute(own, ("layer", "half"), half_pairs(range(layers // 2, layers)))
+    late = lax.ppermute(own, ("layer", "half"), half_pairs(range(layers // 4, layers)))
     early = exchange(early, "x").reshape(n, w)
-    other = jnp.where(lax.axis_index("layer") < layers // 2, early, late)
+    other = jnp.where(lax.axis_index("layer") < layers // 4, early, late)
 
     both = jnp.stack([own, other])
     block = spread(both, "quarter")

time: 173 us -> 171 us (0.988)
  starting transfers between devices: 52.8 us -> 49.9 us
    all_to_all x3, starting transfers between devices: 25.9 us -> 23 us  [exchange(): return lax.all_to_all(blocks, axis, 0, 0, tiled=True)]
  transfers between devices with their start and end apart: 8 -> 8, of which waited for: 4 -> 5; matrix products, arithmetic and copies ran while one was open for 0% -> 0% of each run, Pallas kernels for 0% -> 0%
where the time goes in v14:
time: 171 us; the launch traced here: 170 us
  blocking collectives  83 us (49%)
  starting transfers between devices  49.9 us (29%)
  waiting for transfers between devices  28.5 us (17%)
  matrix products  3.72 us (2%)
  local copies, waits for them, and re-layouts  2.86 us (2%)
  other arithmetic  2.08 us (1%)
    all_to_all x3, blocking collectives, exchange(): return lax.all_to_all(blocks, axis, 0, 0, tiled=True)  39.9 us
    all_to_all x3, waiting for transfers between devices, exchange(): return lax.all_to_all(blocks, axis, 0, 0, tiled=True)  24.9 us
    all_to_all x3, starting transfers between devices, exchange(): return lax.all_to_all(blocks, axis, 0, 0, tiled=True)  23 us
    ppermute x1, starting transfers between devices, shards(): lax.ppermute(own, ('layer', 'half'), half_pairs(range(layers // 4, layers)))  19.4 us
    all_gather x1, blocking collectives, shards(): firsts = lax.all_gather(first, 'y', axis=1).reshape(nc * ny * 2 * n, h)  14.4 us
    all_gather x1, blocking collectives, shards(): gram = lax.all_gather(mine, 'x', axis=0, tiled=True)  14.4 us
    all_gather x1, blocking collectives, shards(): left = lax.all_gather(both, 'y', axis=0).reshape(ny * 2 * n, w)  14.2 us
    dot_general x3, matrix products, dot(): lax.dot_general(lhs, rhs, (dims, ((), ())), preferred_element_type=jnp.fl...  3.72 us
  transfers between devices with their start and end apart: 8, of which 5 were waited for; matrix products, arithmetic and copies ran while one was open for 0% of the time, Pallas kernels for 0%

profile of v14, /device:TPU:256, one launch (start us, length us, event | category | flops | bytes accessed | tf_op | source)
XLA Modules:
  0.0 170.3 jit_solution(5580431106862729433)
XLA Ops:
  0.9 1.3 collective-permute-start
  2.2 10.1 %all_to_all.30 = bf16[4,14,1024]{2,1,0:T(8,128)(2,1)S(1)} all-to-all(bf16[4,14,1024]{2,1,0:T(8,128)(2,1)S(1)} %pad_maximum_fusion.3), channel_id=1, replica_groups=mesh['layer'=4,'quarter'=4,'y'=4,'half'=2,'x'=4,'core'=2] {'x'}, dimensions={0} | all-to-all | bytes 229376 | tf_op jit(solution)/shard_map/all_to_all | solution.py:22
  12.3 19.4 %collective-permute-start.1 = (bf16[56,1024]{1,0:T(8,128)(2,1)S(1)}, bf16[56,1024]{1,0:T(8,128)(2,1)S(1)}, u32[]{:S(2)}, u32[]{:S(2)}) collective-permute-start(bf16[56,1024]{1,0:T(8,128)(2,1)S(1)} %reshape.54), channel_id=1, source_target_pairs={{256,264},{264,256},{512,520},{520,512},{768,776},{776,768},{257,2... | collective-permute-start | bytes 344072 | tf_op jit(solution)/shard_map/ppermute | solution.py:50
  31.6 3.3 %all-to-all-start.1 = ((bf16[4,14,1024]{2,1,0:T(8,128)(2,1)}), bf16[4,14,1024]{2,1,0:T(8,128)(2,1)S(1)}, u32[]{:S(2)}, u32[]{:S(2)}) async-start(bf16[4,14,1024]{2,1,0:T(8,128)(2,1)} %collective-permute-done), calls=%async_computation.1 | async-start | bytes 262144 | tf_op jit(solution)/shard_map/all_to_all | solution.py:22
  35.0 5.9 %all-to-all-done.1 = bf16[4,14,1024]{2,1,0:T(8,128)(2,1)S(1)} async-done(((bf16[4,14,1024]{2,1,0:T(8,128)(2,1)}), bf16[4,14,1024]{2,1,0:T(8,128)(2,1)S(1)}, u32[]{:S(2)}, u32[]{:S(2)}) %all-to-all-start.1) | async-done | bytes 114720 | tf_op jit(solution)/shard_map/all_to_all | solution.py:22
  41.0 1.1 collective-permute-done.1
  42.1 1.0 broadcast_in_dim.4
  43.1 16.2 %all-to-all-start.2 = ((bf16[4,2,56,1024]{3,2,1,0:T(8,128)(2,1)}), bf16[4,2,56,1024]{3,2,1,0:T(8,128)(2,1)S(1)}, u32[]{:S(2)}, u32[]{:S(2)}) async-start(bf16[4,2,56,1024]{3,2,1,0:T(8,128)(2,1)} %broadcast_in_dim.4), calls=%async_computation.2 | async-start | bytes 1835008 | tf_op jit(solution)/shard_map/all_to_all | solution.py:22
  59.3 14.2 %all-gather = bf16[8,56,1024]{2,1,0:T(8,128)(2,1)S(1)} all-gather(bf16[2,56,1024]{2,1,0:T(8,128)(2,1)S(1)} %pad_maximum_fusion.1), channel_id=2, replica_groups=mesh['layer'=4,'quarter'=4,'y'=4,'half'=2,'x'=4,'core'=2] {'y'}, dimensions={0}, use_global_device_ids=true | all-gather | bytes 1146880 | tf_op jit(solution)/shard_map/all_gather | solution.py:56
  73.5 8.8 %all-to-all-done.2 = bf16[4,2,56,1024]{3,2,1,0:T(8,128)(2,1)S(1)} async-done(((bf16[4,2,56,1024]{3,2,1,0:T(8,128)(2,1)}), bf16[4,2,56,1024]{3,2,1,0:T(8,128)(2,1)S(1)}, u32[]{:S(2)}, u32[]{:S(2)}) %all-to-all-start.2) | async-done | bytes 917536 | tf_op jit(solution)/shard_map/all_to_all | solution.py:22
  82.4 1.9 %collective-permute-start.2 = (bf16[4,2,56,1024]{3,2,0,1:T(8,128)(2,1)S(1)}, bf16[4,2,56,1024]{3,2,0,1:T(8,128)(2,1)}, u32[]{:S(2)}, u32[]{:S(2)}) collective-permute-start(bf16[4,2,56,1024]{3,2,0,1:T(8,128)(2,1)S(1)} %copy.5), channel_id=1, source_target_pairs={{0,1},{1,0},{2,3},{3,2},{4,5},{5,4},{6,7},{7,6},{8,9},{9,8},{10,11... | collective-permute-start | bytes 2752520 | tf_op jit(solution)/shard_map/ppermute | solution.py:58
  84.4 2.6 %collective-permute-done.2 = bf16[4,2,56,1024]{3,2,0,1:T(8,128)(2,1)} collective-permute-done((bf16[4,2,56,1024]{3,2,0,1:T(8,128)(2,1)S(1)}, bf16[4,2,56,1024]{3,2,0,1:T(8,128)(2,1)}, u32[]{:S(2)}, u32[]{:S(2)}) %collective-permute-start.2) | collective-permute-done | bytes 917536 | tf_op jit(solution)/shard_map/ppermute | solution.py:58
  86.9 1.3 select_bitcast_fusion.1
  88.4 1.2 convolution_convert_fusion.1
  89.6 15.4 %all_to_all.31 = bf16[4,112,896]{2,1,0:T(8,128)(2,1)S(1)} all-to-all(bf16[4,112,896]{2,1,0:T(8,128)(2,1)S(1)} %bitcast.37), channel_id=1, replica_groups=mesh['layer'=4,'quarter'=4,'y'=4,'half'=2,'x'=4,'core'=2] {'x'}, dimensions={0} | all-to-all | bytes 1605632 | tf_op jit(solution)/shard_map/all_to_all | solution.py:22
  105.1 14.4 %all_gather.14 = bf16[448,896]{1,0:T(8,128)(2,1)S(1)} all-gather(bf16[112,896]{1,0:T(8,128)(2,1)S(1)} %reduce_sum.45), channel_id=1, replica_groups=mesh['layer'=4,'quarter'=4,'y'=4,'half'=2,'x'=4,'core'=2] {'x'}, dimensions={0}, use_global_device_ids=true | all-gather | bytes 1003520 | tf_op jit(solution)/shard_map/all_gather | solution.py:63
  119.5 1.1 convolution_convert_fusion
  120.6 14.5 %all_to_all.32 = bf16[4,112,1024]{2,1,0:T(8,128)(2,1)S(1)} all-to-all(bf16[4,112,1024]{2,1,0:T(8,128)(2,1)S(1)} %bitcast.34), channel_id=1, replica_groups=mesh['layer'=4,'quarter'=4,'y'=4,'half'=2,'x'=4,'core'=2] {'y'}, dimensions={0} | all-to-all | bytes 1835008 | tf_op jit(solution)/shard_map/all_to_all | solution.py:22
  135.3 1.9 %collective-permute-start.3 = (bf16[112,512]{1,0:T(8,128)(2,1)S(1)}, bf16[112,512]{1,0:T(8,128)(2,1)S(1)}, u32[]{:S(2)}, u32[]{:S(2)}) collective-permute-start(bf16[112,512]{1,0:T(8,128)(2,1)S(1)} %get-tuple-element.10), channel_id=1, source_target_pairs={{0,1},{1,0},{2,3},{3,2},{4,5},{5,4},{6,7},{7,6},{8,9},{9,8},{10,11... | collective-permute-start | bytes 344072 | tf_op jit(solution)/shard_map/ppermute | solution.py:70
  137.2 2.4 %collective-permute-start.4 = (bf16[448,448]{1,0:T(8,128)(2,1)S(1)}, bf16[448,448]{1,0:T(8,128)(2,1)S(1)}, u32[]{:S(2)}, u32[]{:S(2)}) collective-permute-start(bf16[448,448]{1,0:T(8,128)(2,1)S(1)} %slice.40), channel_id=1, source_target_pairs={{0,1},{1,0},{2,3},{3,2},{4,5},{5,4},{6,7},{7,6},{8,9},{9,8},{10,11... | collective-permute-start | bytes 1204232 | tf_op jit(solution)/shard_map/ppermute | solution.py:65
  139.7 14.4 %all-gather.1 = bf16[2,448,512]{2,1,0:T(8,128)(2,1)S(1)} all-gather(bf16[2,112,512]{2,1,0:T(8,128)(2,1)S(1)} %pad_maximum_fusion.2), channel_id=3, replica_groups=mesh['layer'=4,'quarter'=4,'y'=4,'half'=2,'x'=4,'core'=2] {'y'}, dimensions={1}, use_global_device_ids=true | all-gather | bytes 1146880 | tf_op jit(solution)/shard_map/all_gather | solution.py:72
  154.1 1.4 convolution_convert_fusion.2
  155.6 3.5 %all-to-all-start.5 = ((bf16[4,112,512]{2,1,0:T(8,128)(2,1)}), bf16[4,112,512]{2,1,0:T(8,128)(2,1)S(1)}, u32[]{:S(2)}, u32[]{:S(2)}) async-start(bf16[4,112,512]{2,1,0:T(8,128)(2,1)} %bitcast.15), calls=%async_computation.5 | async-start | bytes 917504 | tf_op jit(solution)/shard_map/all_to_all | solution.py:22
  159.2 10.1 %all-to-all-done.5 = bf16[4,112,512]{2,1,0:T(8,128)(2,1)S(1)} async-done(((bf16[4,112,512]{2,1,0:T(8,128)(2,1)}), bf16[4,112,512]{2,1,0:T(8,128)(2,1)S(1)}, u32[]{:S(2)}, u32[]{:S(2)}) %all-to-all-start.5) | async-done | bytes 458784 | tf_op jit(solution)/shard_map/all_to_all | solution.py:22
  (27 shorter events, 2.6 us)
Async XLA Ops:
  0.9 30.8 %collective-permute-start = (bf16[4,14,1024]{2,1,0:T(8,128)(2,1)S(1)}, bf16[4,14,1024]{2,1,0:T(8,128)(2,1)}, u32[]{:S(2)}, u32[]{:S(2)}) collective-permute-start(bf16[4,14,1024]{2,1,0:T(8,128)(2,1)S(1)} %pad_maximum_fusion.3), channel_id=1, source_target_pairs={{0,8},{8,0},{1,9},{9,1},{2,10},{10,2},{3,11},{11,3},{4,12},{12,4},... | collective-permute-start | bytes 344072 | tf_op jit(solution)/shard_map/ppermute | solution.py:48
  12.3 29.8 %collective-permute-start.1 = (bf16[56,1024]{1,0:T(8,128)(2,1)S(1)}, bf16[56,1024]{1,0:T(8,128)(2,1)S(1)}, u32[]{:S(2)}, u32[]{:S(2)}) collective-permute-start(bf16[56,1024]{1,0:T(8,128)(2,1)S(1)} %reshape.54), channel_id=1, source_target_pairs={{256,264},{264,256},{512,520},{520,512},{768,776},{776,768},{257,2... | collective-permute-start | bytes 344072 | tf_op jit(solution)/shard_map/ppermute | solution.py:50
  31.6 9.3 %all-to-all-start.1 = ((bf16[4,14,1024]{2,1,0:T(8,128)(2,1)}), bf16[4,14,1024]{2,1,0:T(8,128)(2,1)S(1)}, u32[]{:S(2)}, u32[]{:S(2)}) async-start(bf16[4,14,1024]{2,1,0:T(8,128)(2,1)} %collective-permute-done), calls=%async_computation.1 | async-start | bytes 262144 | tf_op jit(solution)/shard_map/all_to_all | solution.py:22
  43.1 39.2 %all-to-all-start.2 = ((bf16[4,2,56,1024]{3,2,1,0:T(8,128)(2,1)}), bf16[4,2,56,1024]{3,2,1,0:T(8,128)(2,1)S(1)}, u32[]{:S(2)}, u32[]{:S(2)}) async-start(bf16[4,2,56,1024]{3,2,1,0:T(8,128)(2,1)} %broadcast_in_dim.4), calls=%async_computation.2 | async-start | bytes 1835008 | tf_op jit(solution)/shard_map/all_to_all | solution.py:22
  82.4 4.5 %collective-permute-start.2 = (bf16[4,2,56,1024]{3,2,0,1:T(8,128)(2,1)S(1)}, bf16[4,2,56,1024]{3,2,0,1:T(8,128)(2,1)}, u32[]{:S(2)}, u32[]{:S(2)}) collective-permute-start(bf16[4,2,56,1024]{3,2,0,1:T(8,128)(2,1)S(1)} %copy.5), channel_id=1, source_target_pairs={{0,1},{1,0},{2,3},{3,2},{4,5},{5,4},{6,7},{7,6},{8,9},{9,8},{10,11... | collective-permute-start | bytes 2752520 | tf_op jit(solution)/shard_map/ppermute | solution.py:58
  135.3 4.4 %collective-permute-start.3 = (bf16[112,512]{1,0:T(8,128)(2,1)S(1)}, bf16[112,512]{1,0:T(8,128)(2,1)S(1)}, u32[]{:S(2)}, u32[]{:S(2)}) collective-permute-start(bf16[112,512]{1,0:T(8,128)(2,1)S(1)} %get-tuple-element.10), channel_id=1, source_target_pairs={{0,1},{1,0},{2,3},{3,2},{4,5},{5,4},{6,7},{7,6},{8,9},{9,8},{10,11... | collective-permute-start | bytes 344072 | tf_op jit(solution)/shard_map/ppermute | solution.py:70
  137.2 16.9 %collective-permute-start.4 = (bf16[448,448]{1,0:T(8,128)(2,1)S(1)}, bf16[448,448]{1,0:T(8,128)(2,1)S(1)}, u32[]{:S(2)}, u32[]{:S(2)}) collective-permute-start(bf16[448,448]{1,0:T(8,128)(2,1)S(1)} %slice.40), channel_id=1, source_target_pairs={{0,1},{1,0},{2,3},{3,2},{4,5},{5,4},{6,7},{7,6},{8,9},{9,8},{10,11... | collective-permute-start | bytes 1204232 | tf_op jit(solution)/shard_map/ppermute | solution.py:65
  155.6 13.8 %all-to-all-start.5 = ((bf16[4,112,512]{2,1,0:T(8,128)(2,1)}), bf16[4,112,512]{2,1,0:T(8,128)(2,1)S(1)}, u32[]{:S(2)}, u32[]{:S(2)}) async-start(bf16[4,112,512]{2,1,0:T(8,128)(2,1)} %bitcast.15), calls=%async_computation.5 | async-start | bytes 917504 | tf_op jit(solution)/shard_map/all_to_all | solution.py:22

commit v15 on v9

--- a/solution.py
+++ b/solution.py
@@ -41,7 +41,8 @@
     core = lax.axis_index("core")
     rows = jnp.stack([momentum[0, :, i * w : (i + 1) * w] for i in range(nx)])
     own = exchange(rows, "x").reshape(n, w)
-    other = lax.ppermute(own, "half", SWAP)
+    crossed = [(2 * q + g, 2 * (q ^ 1) + 1 - g) for q in range(nq) for g in range(2)]
+    other = lax.ppermute(own, ("quarter", "half"), crossed)
 
     both = jnp.stack([own, other])
     block = spread(both, "quarter")

time: 167 us -> 168 us (level)
  waiting for transfers between devices: 23.9 us -> 36.1 us
  starting transfers between devices: 53.2 us -> 41.8 us
    ppermute x1, waiting for transfers between devices: 3.41 us -> 14.7 us  [shards(): other = lax.ppermute(own, ('quarter', 'half'), crossed)]
    all_to_all x2, starting transfers between devices: 18 us -> 6.97 us  [exchange(): return lax.all_to_all(blocks, axis, 0, 0, tiled=True)]
where the time goes in v15:
time: 168 us
  blocking collectives  80.8 us (48%)
  starting transfers between devices  41.8 us (25%)
  waiting for transfers between devices  36.1 us (21%)
  matrix products  3.71 us (2%)
  local copies, waits for them, and re-layouts  2.82 us (2%)
  other arithmetic  2.07 us (1%)
    all_to_all x3, blocking collectives, exchange(): return lax.all_to_all(blocks, axis, 0, 0, tiled=True)  38.9 us
    ppermute x1, starting transfers between devices, shards(): other = lax.ppermute(own, ('quarter', 'half'), crossed)  28.5 us
    all_to_all x2, waiting for transfers between devices, exchange(): return lax.all_to_all(blocks, axis, 0, 0, tiled=True)  18.9 us
    ppermute x1, waiting for transfers between devices, shards(): other = lax.ppermute(own, ('quarter', 'half'), crossed)  14.7 us
    all_gather x1, blocking collectives, shards(): gram = lax.all_gather(mine, 'x', axis=0, tiled=True)  14.4 us
    all_gather x1, blocking collectives, shards(): left = lax.all_gather(both, 'y', axis=0).reshape(ny * 2 * n, w)  13.9 us
    all_gather x1, blocking collectives, shards(): firsts = lax.all_gather(first, 'y', axis=1).reshape(nc * ny * 2 * n, h)  13.6 us
    all_to_all x2, starting transfers between devices, exchange(): return lax.all_to_all(blocks, axis, 0, 0, tiled=True)  6.97 us
  transfers between devices with their start and end apart: 6, of which 4 were waited for; matrix products, arithmetic and copies ran while one was open for 0% of the time, Pallas kernels for 0%

profile of v15, /device:TPU:8, one launch (start us, length us, event | category | flops | bytes accessed | tf_op | source)
XLA Modules:
  0.0 167.5 jit_solution(16586994378179875226)
XLA Ops:
  0.0 0.8 fusion.5
  0.9 10.1 %all_to_all.25 = bf16[4,14,1024]{2,1,0:T(8,128)(2,1)S(1)} all-to-all(bf16[4,14,1024]{2,1,0:T(8,128)(2,1)S(1)} %pad_maximum_fusion.3), channel_id=1, replica_groups=mesh['layer'=4,'quarter'=4,'y'=4,'half'=2,'x'=4,'core'=2] {'x'}, dimensions={0} | all-to-all | bytes 229376 | tf_op jit(solution)/shard_map/all_to_all | solution.py:22
  11.0 28.5 %collective-permute-start = (bf16[56,1024]{1,0:T(8,128)(2,1)S(1)}, bf16[56,1024]{1,0:T(8,128)(2,1)S(1)}, u32[]{:S(2)}, u32[]{:S(2)}) collective-permute-start(bf16[56,1024]{1,0:T(8,128)(2,1)S(1)} %reshape.50), channel_id=1, source_target_pairs={{0,72},{8,64},{64,8},{72,0},{128,200},{136,192},{192,136},{200,128... | collective-permute-start | bytes 344072 | tf_op jit(solution)/shard_map/ppermute | solution.py:45
  39.6 14.7 %collective-permute-done = bf16[56,1024]{1,0:T(8,128)(2,1)S(1)} collective-permute-done((bf16[56,1024]{1,0:T(8,128)(2,1)S(1)}, bf16[56,1024]{1,0:T(8,128)(2,1)S(1)}, u32[]{:S(2)}, u32[]{:S(2)}) %collective-permute-start) | collective-permute-done | bytes 114720 | tf_op jit(solution)/shard_map/ppermute | solution.py:45
  54.2 1.0 broadcast_in_dim.4
  55.3 3.5 %all-to-all-start.1 = ((bf16[4,2,56,1024]{3,2,1,0:T(8,128)(2,1)}), bf16[4,2,56,1024]{3,2,1,0:T(8,128)(2,1)S(1)}, u32[]{:S(2)}, u32[]{:S(2)}) async-start(bf16[4,2,56,1024]{3,2,1,0:T(8,128)(2,1)} %broadcast_in_dim.4), calls=%async_computation.1 | async-start | bytes 1835008 | tf_op jit(solution)/shard_map/all_to_all | solution.py:22
  58.8 13.9 %all-gather = bf16[8,56,1024]{2,1,0:T(8,128)(2,1)S(1)} all-gather(bf16[2,56,1024]{2,1,0:T(8,128)(2,1)S(1)} %pad_maximum_fusion.1), channel_id=2, replica_groups=mesh['layer'=4,'quarter'=4,'y'=4,'half'=2,'x'=4,'core'=2] {'y'}, dimensions={0}, use_global_device_ids=true | all-gather | bytes 1146880 | tf_op jit(solution)/shard_map/all_gather | solution.py:49
  72.7 7.6 %all-to-all-done.1 = bf16[4,2,56,1024]{3,2,1,0:T(8,128)(2,1)S(1)} async-done(((bf16[4,2,56,1024]{3,2,1,0:T(8,128)(2,1)}), bf16[4,2,56,1024]{3,2,1,0:T(8,128)(2,1)S(1)}, u32[]{:S(2)}, u32[]{:S(2)}) %all-to-all-start.1) | async-done | bytes 917536 | tf_op jit(solution)/shard_map/all_to_all | solution.py:22
  80.4 1.9 %collective-permute-start.1 = (bf16[4,2,56,1024]{3,2,0,1:T(8,128)(2,1)S(1)}, bf16[4,2,56,1024]{3,2,0,1:T(8,128)(2,1)}, u32[]{:S(2)}, u32[]{:S(2)}) collective-permute-start(bf16[4,2,56,1024]{3,2,0,1:T(8,128)(2,1)S(1)} %copy.5), channel_id=1, source_target_pairs={{0,1},{1,0},{2,3},{3,2},{4,5},{5,4},{6,7},{7,6},{8,9},{9,8},{10,11... | collective-permute-start | bytes 2752520 | tf_op jit(solution)/shard_map/ppermute | solution.py:51
  82.3 2.6 %collective-permute-done.1 = bf16[4,2,56,1024]{3,2,0,1:T(8,128)(2,1)} collective-permute-done((bf16[4,2,56,1024]{3,2,0,1:T(8,128)(2,1)S(1)}, bf16[4,2,56,1024]{3,2,0,1:T(8,128)(2,1)}, u32[]{:S(2)}, u32[]{:S(2)}) %collective-permute-start.1) | collective-permute-done | bytes 917536 | tf_op jit(solution)/shard_map/ppermute | solution.py:51
  84.9 1.3 select_bitcast_fusion.1
  86.4 1.2 convolution_convert_fusion.1
  87.5 15.4 %all_to_all.26 = bf16[4,112,896]{2,1,0:T(8,128)(2,1)S(1)} all-to-all(bf16[4,112,896]{2,1,0:T(8,128)(2,1)S(1)} %bitcast.36), channel_id=1, replica_groups=mesh['layer'=4,'quarter'=4,'y'=4,'half'=2,'x'=4,'core'=2] {'x'}, dimensions={0} | all-to-all | bytes 1605632 | tf_op jit(solution)/shard_map/all_to_all | solution.py:22
  103.1 14.4 %all_gather.14 = bf16[448,896]{1,0:T(8,128)(2,1)S(1)} all-gather(bf16[112,896]{1,0:T(8,128)(2,1)S(1)} %reduce_sum.45), channel_id=1, replica_groups=mesh['layer'=4,'quarter'=4,'y'=4,'half'=2,'x'=4,'core'=2] {'x'}, dimensions={0}, use_global_device_ids=true | all-gather | bytes 1003520 | tf_op jit(solution)/shard_map/all_gather | solution.py:56
  117.4 1.1 convolution_convert_fusion
  118.6 13.4 %all_to_all.27 = bf16[4,112,1024]{2,1,0:T(8,128)(2,1)S(1)} all-to-all(bf16[4,112,1024]{2,1,0:T(8,128)(2,1)S(1)} %bitcast.33), channel_id=1, replica_groups=mesh['layer'=4,'quarter'=4,'y'=4,'half'=2,'x'=4,'core'=2] {'y'}, dimensions={0} | all-to-all | bytes 1835008 | tf_op jit(solution)/shard_map/all_to_all | solution.py:22
  132.0 0.2 select_reduce_fusion.1
  132.2 1.9 %collective-permute-start.2 = (bf16[112,512]{1,0:T(8,128)(2,1)S(1)}, bf16[112,512]{1,0:T(8,128)(2,1)S(1)}, u32[]{:S(2)}, u32[]{:S(2)}) collective-permute-start(bf16[112,512]{1,0:T(8,128)(2,1)S(1)} %get-tuple-element.10), channel_id=1, source_target_pairs={{0,1},{1,0},{2,3},{3,2},{4,5},{5,4},{6,7},{7,6},{8,9},{9,8},{10,11... | collective-permute-start | bytes 344072 | tf_op jit(solution)/shard_map/ppermute | solution.py:63
  134.2 2.4 %collective-permute-start.3 = (bf16[448,448]{1,0:T(8,128)(2,1)S(1)}, bf16[448,448]{1,0:T(8,128)(2,1)S(1)}, u32[]{:S(2)}, u32[]{:S(2)}) collective-permute-start(bf16[448,448]{1,0:T(8,128)(2,1)S(1)} %slice.40), channel_id=1, source_target_pairs={{0,1},{1,0},{2,3},{3,2},{4,5},{5,4},{6,7},{7,6},{8,9},{9,8},{10,11... | collective-permute-start | bytes 1204232 | tf_op jit(solution)/shard_map/ppermute | solution.py:58
  136.6 13.6 %all-gather.1 = bf16[2,448,512]{2,1,0:T(8,128)(2,1)S(1)} all-gather(bf16[2,112,512]{2,1,0:T(8,128)(2,1)S(1)} %pad_maximum_fusion.2), channel_id=3, replica_groups=mesh['layer'=4,'quarter'=4,'y'=4,'half'=2,'x'=4,'core'=2] {'y'}, dimensions={1}, use_global_device_ids=true | all-gather | bytes 1146880 | tf_op jit(solution)/shard_map/all_gather | solution.py:65
  150.2 1.4 convolution_convert_fusion.2
  151.6 3.5 %all-to-all-start.4 = ((bf16[4,112,512]{2,1,0:T(8,128)(2,1)}), bf16[4,112,512]{2,1,0:T(8,128)(2,1)S(1)}, u32[]{:S(2)}, u32[]{:S(2)}) async-start(bf16[4,112,512]{2,1,0:T(8,128)(2,1)} %bitcast.15), calls=%async_computation.4 | async-start | bytes 917504 | tf_op jit(solution)/shard_map/all_to_all | solution.py:22
  155.3 11.3 %all-to-all-done.4 = bf16[4,112,512]{2,1,0:T(8,128)(2,1)S(1)} async-done(((bf16[4,112,512]{2,1,0:T(8,128)(2,1)}), bf16[4,112,512]{2,1,0:T(8,128)(2,1)S(1)}, u32[]{:S(2)}, u32[]{:S(2)}) %all-to-all-start.4) | async-done | bytes 458784 | tf_op jit(solution)/shard_map/all_to_all | solution.py:22
  166.8 0.7 convert_element_type.52
  (21 shorter events, 0.9 us)
Async XLA Ops:
  11.0 43.2 %collective-permute-start = (bf16[56,1024]{1,0:T(8,128)(2,1)S(1)}, bf16[56,1024]{1,0:T(8,128)(2,1)S(1)}, u32[]{:S(2)}, u32[]{:S(2)}) collective-permute-start(bf16[56,1024]{1,0:T(8,128)(2,1)S(1)} %reshape.50), channel_id=1, source_target_pairs={{0,72},{8,64},{64,8},{72,0},{128,200},{136,192},{192,136},{200,128... | collective-permute-start | bytes 344072 | tf_op jit(solution)/shard_map/ppermute | solution.py:45
  55.3 25.0 %all-to-all-start.1 = ((bf16[4,2,56,1024]{3,2,1,0:T(8,128)(2,1)}), bf16[4,2,56,1024]{3,2,1,0:T(8,128)(2,1)S(1)}, u32[]{:S(2)}, u32[]{:S(2)}) async-start(bf16[4,2,56,1024]{3,2,1,0:T(8,128)(2,1)} %broadcast_in_dim.4), calls=%async_computation.1 | async-start | bytes 1835008 | tf_op jit(solution)/shard_map/all_to_all | solution.py:22
  80.4 4.5 %collective-permute-start.1 = (bf16[4,2,56,1024]{3,2,0,1:T(8,128)(2,1)S(1)}, bf16[4,2,56,1024]{3,2,0,1:T(8,128)(2,1)}, u32[]{:S(2)}, u32[]{:S(2)}) collective-permute-start(bf16[4,2,56,1024]{3,2,0,1:T(8,128)(2,1)S(1)} %copy.5), channel_id=1, source_target_pairs={{0,1},{1,0},{2,3},{3,2},{4,5},{5,4},{6,7},{7,6},{8,9},{9,8},{10,11... | collective-permute-start | bytes 2752520 | tf_op jit(solution)/shard_map/ppermute | solution.py:51
  132.2 4.4 %collective-permute-start.2 = (bf16[112,512]{1,0:T(8,128)(2,1)S(1)}, bf16[112,512]{1,0:T(8,128)(2,1)S(1)}, u32[]{:S(2)}, u32[]{:S(2)}) collective-permute-start(bf16[112,512]{1,0:T(8,128)(2,1)S(1)} %get-tuple-element.10), channel_id=1, source_target_pairs={{0,1},{1,0},{2,3},{3,2},{4,5},{5,4},{6,7},{7,6},{8,9},{9,8},{10,11... | collective-permute-start | bytes 344072 | tf_op jit(solution)/shard_map/ppermute | solution.py:63
  134.2 16.0 %collective-permute-start.3 = (bf16[448,448]{1,0:T(8,128)(2,1)S(1)}, bf16[448,448]{1,0:T(8,128)(2,1)S(1)}, u32[]{:S(2)}, u32[]{:S(2)}) collective-permute-start(bf16[448,448]{1,0:T(8,128)(2,1)S(1)} %slice.40), channel_id=1, source_target_pairs={{0,1},{1,0},{2,3},{3,2},{4,5},{5,4},{6,7},{7,6},{8,9},{9,8},{10,11... | collective-permute-start | bytes 1204232 | tf_op jit(solution)/shard_map/ppermute | solution.py:58
  151.6 15.0 %all-to-all-start.4 = ((bf16[4,112,512]{2,1,0:T(8,128)(2,1)}), bf16[4,112,512]{2,1,0:T(8,128)(2,1)S(1)}, u32[]{:S(2)}, u32[]{:S(2)}) async-start(bf16[4,112,512]{2,1,0:T(8,128)(2,1)} %bitcast.15), calls=%async_computation.4 | async-start | bytes 917504 | tf_op jit(solution)/shard_map/all_to_all | solution.py:22

commit v16 on v9

--- a/solution.py
+++ b/solution.py
@@ -42,13 +42,14 @@
     rows = jnp.stack([momentum[0, :, i * w : (i + 1) * w] for i in range(nx)])
     own = exchange(rows, "x").reshape(n, w)
     other = lax.ppermute(own, "half", SWAP)
-
-    both = jnp.stack([own, other])
-    block = spread(both, "quarter")
-    left = lax.all_gather(both, "y", axis=0).reshape(ny * 2 * n, w)
-    block, left = lax.optimization_barrier((block, left))
-    block = jnp.stack(ordered(core, block, lax.ppermute(block, "core", SWAP)), 2)
-    right = block.transpose(1, 0, 2, 3, 4).reshape(2 * nq * nc * n, w)
+    own_block = spread(own, "quarter")
+    other_block = spread(other, "quarter")
+    left = lax.all_gather(jnp.stack([own, other]), "y", axis=0).reshape(ny * 2 * n, w)
+    other_block, left = lax.optimization_barrier((other_block, left))
+    right = []
+    for block in (own_block, other_block):
+        right.append(jnp.stack(ordered(core, block, lax.ppermute(block, "core", SWAP)), 1))
+    right = jnp.stack(right).reshape(2 * nq * nc * n, w)
 
     term = dot(left, right, ((1,), (1,))).astype(bf16)
     mine = total(exchange(term.reshape(nx, 2 * n, 16 * n), "x")).astype(bf16)

time: 167 us -> 178 us (1.066)
  starting transfers between devices: 53.2 us -> 66.5 us
  waiting for transfers between devices: 23.9 us -> 20.6 us
    all_to_all x2 -> x3, starting transfers between devices: 18 us -> 31.8 us  [exchange(): return lax.all_to_all(blocks, axis, 0, 0, tiled=True)]
    all_to_all x2 -> x3, waiting for transfers between devices: 18 us -> 11.1 us  [exchange(): return lax.all_to_all(blocks, axis, 0, 0, tiled=True)]
    ppermute x1, waiting for transfers between devices: 3.41 us -> 7.76 us  [shards(): other = lax.ppermute(own, 'half', SWAP)]
    ppermute x1, starting transfers between devices: 29 us -> 26.6 us  [shards(): other = lax.ppermute(own, 'half', SWAP)]
    ppermute x1 -> x2, starting transfers between devices: 1.92 us -> 3.83 us  [shards(): lax.ppermute(block, 'core', SWAP)]
  transfers between devices with their start and end apart: 6 -> 8, of which waited for: 4 -> 3; matrix products, arithmetic and copies ran while one was open for 0% -> 0% of each run, Pallas kernels for 0% -> 0%
where the time goes in v16:
time: 178 us; the launch traced here: 177 us
  blocking collectives  81.7 us (46%)
  starting transfers between devices  66.5 us (37%)
  waiting for transfers between devices  20.6 us (12%)
  matrix products  3.7 us (2%)
  local copies, waits for them, and re-layouts  3.34 us (2%)
    all_to_all x3, blocking collectives, exchange(): return lax.all_to_all(blocks, axis, 0, 0, tiled=True)  38.5 us
    all_to_all x3, starting transfers between devices, exchange(): return lax.all_to_all(blocks, axis, 0, 0, tiled=True)  31.8 us
    ppermute x1, starting transfers between devices, shards(): other = lax.ppermute(own, 'half', SWAP)  26.6 us
    all_gather x1, blocking collectives, shards(): lax.all_gather(jnp.stack([own, other]), 'y', axis=0).reshape(ny * 2 * n, w)  15.2 us
    all_gather x1, blocking collectives, shards(): gram = lax.all_gather(mine, 'x', axis=0, tiled=True)  14.4 us
    all_gather x1, blocking collectives, shards(): firsts = lax.all_gather(first, 'y', axis=1).reshape(nc * ny * 2 * n, h)  13.6 us
    all_to_all x3, waiting for transfers between devices, exchange(): return lax.all_to_all(blocks, axis, 0, 0, tiled=True)  11.1 us
    ppermute x1, waiting for transfers between devices, shards(): other = lax.ppermute(own, 'half', SWAP)  7.76 us
  transfers between devices with their start and end apart: 8, of which 3 were waited for; matrix products, arithmetic and copies ran while one was open for 0% of the time, Pallas kernels for 0%

profile of v16, /device:TPU:8, one launch (start us, length us, event | category | flops | bytes accessed | tf_op | source)
XLA Modules:
  0.0 177.0 jit_solution(17527590735830348843)
XLA Ops:
  0.0 0.8 fusion.5
  0.9 10.1 %all_to_all.30 = bf16[4,14,1024]{2,1,0:T(8,128)(2,1)S(1)} all-to-all(bf16[4,14,1024]{2,1,0:T(8,128)(2,1)S(1)} %pad_maximum_fusion.3), channel_id=1, replica_groups=mesh['layer'=4,'quarter'=4,'y'=4,'half'=2,'x'=4,'core'=2] {'x'}, dimensions={0} | all-to-all | bytes 229376 | tf_op jit(solution)/shard_map/all_to_all | solution.py:22
  11.0 0.8 broadcast_in_dim.17
  11.8 5.9 %all-to-all-start.1 = ((bf16[4,56,1024]{2,1,0:T(8,128)(2,1)}), bf16[4,56,1024]{2,1,0:T(8,128)(2,1)S(1)}, u32[]{:S(2)}, u32[]{:S(2)}) async-start(bf16[4,56,1024]{2,1,0:T(8,128)(2,1)} %broadcast_in_dim.17), calls=%async_computation.1 | async-start | bytes 917504 | tf_op jit(solution)/shard_map/all_to_all | solution.py:22
  17.7 26.6 %collective-permute-start.1 = (bf16[56,1024]{1,0:T(8,128)(2,1)S(1)}, bf16[56,1024]{1,0:T(8,128)(2,1)S(1)}, u32[]{:S(2)}, u32[]{:S(2)}) collective-permute-start(bf16[56,1024]{1,0:T(8,128)(2,1)S(1)} %broadcast_in_dim.16), channel_id=1, source_target_pairs={{0,8},{8,0},{1,9},{9,1},{2,10},{10,2},{3,11},{11,3},{4,12},{12,4},... | collective-permute-start | bytes 344072 | tf_op jit(solution)/shard_map/ppermute | solution.py:44
  44.2 7.8 %collective-permute-done.1 = bf16[56,1024]{1,0:T(8,128)(2,1)S(1)} collective-permute-done((bf16[56,1024]{1,0:T(8,128)(2,1)S(1)}, bf16[56,1024]{1,0:T(8,128)(2,1)S(1)}, u32[]{:S(2)}, u32[]{:S(2)}) %collective-permute-start.1) | collective-permute-done | bytes 114720 | tf_op jit(solution)/shard_map/ppermute | solution.py:44
  52.0 0.8 broadcast_in_dim.18
  52.8 20.8 %all-to-all-start.2 = ((bf16[4,56,1024]{2,1,0:T(8,128)(2,1)}), bf16[4,56,1024]{2,1,0:T(8,128)(2,1)S(1)}, u32[]{:S(2)}, u32[]{:S(2)}) async-start(bf16[4,56,1024]{2,1,0:T(8,128)(2,1)} %broadcast_in_dim.18), calls=%async_computation.2 | async-start | bytes 917504 | tf_op jit(solution)/shard_map/all_to_all | solution.py:22
  73.7 1.9 %collective-permute-start = (bf16[4,56,1024]{2,1,0:T(8,128)(2,1)S(1)}, bf16[4,56,1024]{2,1,0:T(8,128)(2,1)S(1)}, u32[]{:S(2)}, u32[]{:S(2)}) collective-permute-start(bf16[4,56,1024]{2,1,0:T(8,128)(2,1)S(1)} %all-to-all-done.1), channel_id=1, source_target_pairs={{0,1},{1,0},{2,3},{3,2},{4,5},{5,4},{6,7},{7,6},{8,9},{9,8},{10,11... | collective-permute-start | bytes 1376264 | tf_op jit(solution)/shard_map/ppermute | solution.py:51
  75.6 15.2 %all-gather = bf16[8,56,1024]{2,1,0:T(8,128)(2,1)S(1)} all-gather(bf16[2,56,1024]{2,1,0:T(8,128)(2,1)S(1)} %pad_maximum_fusion.1), channel_id=2, replica_groups=mesh['layer'=4,'quarter'=4,'y'=4,'half'=2,'x'=4,'core'=2] {'y'}, dimensions={0}, use_global_device_ids=true | all-gather | bytes 1146880 | tf_op jit(solution)/shard_map/all_gather | solution.py:47
  90.8 1.9 %collective-permute-start.2 = (bf16[4,56,1024]{2,1,0:T(8,128)(2,1)S(1)}, bf16[4,56,1024]{2,1,0:T(8,128)(2,1)S(1)}, u32[]{:S(2)}, u32[]{:S(2)}) collective-permute-start(bf16[4,56,1024]{2,1,0:T(8,128)(2,1)S(1)} %all-to-all-done.2), channel_id=1, source_target_pairs={{0,1},{1,0},{2,3},{3,2},{4,5},{5,4},{6,7},{7,6},{8,9},{9,8},{10,11... | collective-permute-start | bytes 1376264 | tf_op jit(solution)/shard_map/ppermute | solution.py:51
  92.8 1.7 collective-permute-done.2
  94.8 1.1 convolution_convert_fusion.1
  96.0 15.4 %all_to_all.31 = bf16[4,112,896]{2,1,0:T(8,128)(2,1)S(1)} all-to-all(bf16[4,112,896]{2,1,0:T(8,128)(2,1)S(1)} %bitcast.43), channel_id=1, replica_groups=mesh['layer'=4,'quarter'=4,'y'=4,'half'=2,'x'=4,'core'=2] {'x'}, dimensions={0} | all-to-all | bytes 1605632 | tf_op jit(solution)/shard_map/all_to_all | solution.py:22
  111.5 14.4 %all_gather.17 = bf16[448,896]{1,0:T(8,128)(2,1)S(1)} all-gather(bf16[112,896]{1,0:T(8,128)(2,1)S(1)} %reduce_sum.45), channel_id=1, replica_groups=mesh['layer'=4,'quarter'=4,'y'=4,'half'=2,'x'=4,'core'=2] {'x'}, dimensions={0}, use_global_device_ids=true | all-gather | bytes 1003520 | tf_op jit(solution)/shard_map/all_gather | solution.py:56
  125.9 1.1 convolution_convert_fusion
  127.0 13.0 %all_to_all.32 = bf16[4,112,1024]{2,1,0:T(8,128)(2,1)S(1)} all-to-all(bf16[4,112,1024]{2,1,0:T(8,128)(2,1)S(1)} %bitcast.40), channel_id=1, replica_groups=mesh['layer'=4,'quarter'=4,'y'=4,'half'=2,'x'=4,'core'=2] {'y'}, dimensions={0} | all-to-all | bytes 1835008 | tf_op jit(solution)/shard_map/all_to_all | solution.py:22
  140.3 1.9 %collective-permute-start.3 = (bf16[112,512]{1,0:T(8,128)(2,1)S(1)}, bf16[112,512]{1,0:T(8,128)(2,1)S(1)}, u32[]{:S(2)}, u32[]{:S(2)}) collective-permute-start(bf16[112,512]{1,0:T(8,128)(2,1)S(1)} %get-tuple-element.10), channel_id=1, source_target_pairs={{0,1},{1,0},{2,3},{3,2},{4,5},{5,4},{6,7},{7,6},{8,9},{9,8},{10,11... | collective-permute-start | bytes 344072 | tf_op jit(solution)/shard_map/ppermute | solution.py:63
  142.2 2.4 %collective-permute-start.4 = (bf16[448,448]{1,0:T(8,128)(2,1)S(1)}, bf16[448,448]{1,0:T(8,128)(2,1)S(1)}, u32[]{:S(2)}, u32[]{:S(2)}) collective-permute-start(bf16[448,448]{1,0:T(8,128)(2,1)S(1)} %slice.40), channel_id=1, source_target_pairs={{0,1},{1,0},{2,3},{3,2},{4,5},{5,4},{6,7},{7,6},{8,9},{9,8},{10,11... | collective-permute-start | bytes 1204232 | tf_op jit(solution)/shard_map/ppermute | solution.py:58
  144.7 13.6 %all-gather.1 = bf16[2,448,512]{2,1,0:T(8,128)(2,1)S(1)} all-gather(bf16[2,112,512]{2,1,0:T(8,128)(2,1)S(1)} %pad_maximum_fusion.2), channel_id=3, replica_groups=mesh['layer'=4,'quarter'=4,'y'=4,'half'=2,'x'=4,'core'=2] {'y'}, dimensions={1}, use_global_device_ids=true | all-gather | bytes 1146880 | tf_op jit(solution)/shard_map/all_gather | solution.py:65
  158.3 1.4 convolution_convert_fusion.2
  159.7 5.1 %all-to-all-start.5 = ((bf16[4,112,512]{2,1,0:T(8,128)(2,1)}), bf16[4,112,512]{2,1,0:T(8,128)(2,1)S(1)}, u32[]{:S(2)}, u32[]{:S(2)}) async-start(bf16[4,112,512]{2,1,0:T(8,128)(2,1)} %bitcast.18), calls=%async_computation.5 | async-start | bytes 917504 | tf_op jit(solution)/shard_map/all_to_all | solution.py:22
  164.9 11.1 %all-to-all-done.5 = bf16[4,112,512]{2,1,0:T(8,128)(2,1)S(1)} async-done(((bf16[4,112,512]{2,1,0:T(8,128)(2,1)}), bf16[4,112,512]{2,1,0:T(8,128)(2,1)S(1)}, u32[]{:S(2)}, u32[]{:S(2)}) %all-to-all-start.5) | async-done | bytes 458784 | tf_op jit(solution)/shard_map/all_to_all | solution.py:22
  176.3 0.7 convert_element_type.52
  (27 shorter events, 1.2 us)
Async XLA Ops:
  11.8 40.2 %all-to-all-start.1 = ((bf16[4,56,1024]{2,1,0:T(8,128)(2,1)}), bf16[4,56,1024]{2,1,0:T(8,128)(2,1)S(1)}, u32[]{:S(2)}, u32[]{:S(2)}) async-start(bf16[4,56,1024]{2,1,0:T(8,128)(2,1)} %broadcast_in_dim.17), calls=%async_computation.1 | async-start | bytes 917504 | tf_op jit(solution)/shard_map/all_to_all | solution.py:22
  17.7 34.3 %collective-permute-start.1 = (bf16[56,1024]{1,0:T(8,128)(2,1)S(1)}, bf16[56,1024]{1,0:T(8,128)(2,1)S(1)}, u32[]{:S(2)}, u32[]{:S(2)}) collective-permute-start(bf16[56,1024]{1,0:T(8,128)(2,1)S(1)} %broadcast_in_dim.16), channel_id=1, source_target_pairs={{0,8},{8,0},{1,9},{9,1},{2,10},{10,2},{3,11},{11,3},{4,12},{12,4},... | collective-permute-start | bytes 344072 | tf_op jit(solution)/shard_map/ppermute | solution.py:44
  52.8 38.0 %all-to-all-start.2 = ((bf16[4,56,1024]{2,1,0:T(8,128)(2,1)}), bf16[4,56,1024]{2,1,0:T(8,128)(2,1)S(1)}, u32[]{:S(2)}, u32[]{:S(2)}) async-start(bf16[4,56,1024]{2,1,0:T(8,128)(2,1)} %broadcast_in_dim.18), calls=%async_computation.2 | async-start | bytes 917504 | tf_op jit(solution)/shard_map/all_to_all | solution.py:22
  73.7 19.1 %collective-permute-start = (bf16[4,56,1024]{2,1,0:T(8,128)(2,1)S(1)}, bf16[4,56,1024]{2,1,0:T(8,128)(2,1)S(1)}, u32[]{:S(2)}, u32[]{:S(2)}) collective-permute-start(bf16[4,56,1024]{2,1,0:T(8,128)(2,1)S(1)} %all-to-all-done.1), channel_id=1, source_target_pairs={{0,1},{1,0},{2,3},{3,2},{4,5},{5,4},{6,7},{7,6},{8,9},{9,8},{10,11... | collective-permute-start | bytes 1376264 | tf_op jit(solution)/shard_map/ppermute | solution.py:51
  90.8 3.7 %collective-permute-start.2 = (bf16[4,56,1024]{2,1,0:T(8,128)(2,1)S(1)}, bf16[4,56,1024]{2,1,0:T(8,128)(2,1)S(1)}, u32[]{:S(2)}, u32[]{:S(2)}) collective-permute-start(bf16[4,56,1024]{2,1,0:T(8,128)(2,1)S(1)} %all-to-all-done.2), channel_id=1, source_target_pairs={{0,1},{1,0},{2,3},{3,2},{4,5},{5,4},{6,7},{7,6},{8,9},{9,8},{10,11... | collective-permute-start | bytes 1376264 | tf_op jit(solution)/shard_map/ppermute | solution.py:51
  140.3 4.4 %collective-permute-start.3 = (bf16[112,512]{1,0:T(8,128)(2,1)S(1)}, bf16[112,512]{1,0:T(8,128)(2,1)S(1)}, u32[]{:S(2)}, u32[]{:S(2)}) collective-permute-start(bf16[112,512]{1,0:T(8,128)(2,1)S(1)} %get-tuple-element.10), channel_id=1, source_target_pairs={{0,1},{1,0},{2,3},{3,2},{4,5},{5,4},{6,7},{7,6},{8,9},{9,8},{10,11... | collective-permute-start | bytes 344072 | tf_op jit(solution)/shard_map/ppermute | solution.py:63
  142.2 16.0 %collective-permute-start.4 = (bf16[448,448]{1,0:T(8,128)(2,1)S(1)}, bf16[448,448]{1,0:T(8,128)(2,1)S(1)}, u32[]{:S(2)}, u32[]{:S(2)}) collective-permute-start(bf16[448,448]{1,0:T(8,128)(2,1)S(1)} %slice.40), channel_id=1, source_target_pairs={{0,1},{1,0},{2,3},{3,2},{4,5},{5,4},{6,7},{7,6},{8,9},{9,8},{10,11... | collective-permute-start | bytes 1204232 | tf_op jit(solution)/shard_map/ppermute | solution.py:58
  159.7 16.3 %all-to-all-start.5 = ((bf16[4,112,512]{2,1,0:T(8,128)(2,1)}), bf16[4,112,512]{2,1,0:T(8,128)(2,1)S(1)}, u32[]{:S(2)}, u32[]{:S(2)}) async-start(bf16[4,112,512]{2,1,0:T(8,128)(2,1)} %bitcast.18), calls=%async_computation.5 | async-start | bytes 917504 | tf_op jit(solution)/shard_map/all_to_all | solution.py:22

commit v17 on v9

--- a/solution.py
+++ b/solution.py
@@ -47,8 +47,9 @@
     block = spread(both, "quarter")
     left = lax.all_gather(both, "y", axis=0).reshape(ny * 2 * n, w)
     block, left = lax.optimization_barrier((block, left))
-    block = jnp.stack(ordered(core, block, lax.ppermute(block, "core", SWAP)), 2)
-    right = block.transpose(1, 0, 2, 3, 4).reshape(2 * nq * nc * n, w)
+    across = lax.ppermute(block, "core", SWAP)
+    right = jnp.stack([jnp.stack(ordered(core, block[:, g], across[:, g]), 1) for g in range(2)])
+    right = right.reshape(2 * nq * nc * n, w)
 
     term = dot(left, right, ((1,), (1,))).astype(bf16)
     mine = total(exchange(term.reshape(nx, 2 * n, 16 * n), "x")).astype(bf16)

time: 167 us -> 166 us (level)
  no operation moved by 1% of the time
where the time goes in v17:
time: 166 us; the launch traced here: 165 us
  blocking collectives  80.7 us (49%)
  starting transfers between devices  53.2 us (32%)
  waiting for transfers between devices  23.8 us (14%)
  matrix products  3.7 us (2%)
  local copies, waits for them, and re-layouts  2.75 us (2%)
    all_to_all x3, blocking collectives, exchange(): return lax.all_to_all(blocks, axis, 0, 0, tiled=True)  38.9 us
    ppermute x1, starting transfers between devices, shards(): other = lax.ppermute(own, 'half', SWAP)  29 us
    all_to_all x2, starting transfers between devices, exchange(): return lax.all_to_all(blocks, axis, 0, 0, tiled=True)  18 us
    all_to_all x2, waiting for transfers between devices, exchange(): return lax.all_to_all(blocks, axis, 0, 0, tiled=True)  18 us
    all_gather x1, blocking collectives, shards(): gram = lax.all_gather(mine, 'x', axis=0, tiled=True)  14.4 us
    all_gather x1, blocking collectives, shards(): left = lax.all_gather(both, 'y', axis=0).reshape(ny * 2 * n, w)  13.8 us
    all_gather x1, blocking collectives, shards(): firsts = lax.all_gather(first, 'y', axis=1).reshape(nc * ny * 2 * n, h)  13.6 us
    dot_general x3, matrix products, dot(): lax.dot_general(lhs, rhs, (dims, ((), ())), preferred_element_type=jnp.fl...  3.7 us
  transfers between devices with their start and end apart: 6, of which 4 were waited for; matrix products, arithmetic and copies ran while one was open for 0% of the time, Pallas kernels for 0%

profile of v17, /device:TPU:8, one launch (start us, length us, event | category | flops | bytes accessed | tf_op | source)
XLA Modules:
  0.0 165.4 jit_solution(10176615859772362461)
XLA Ops:
  0.0 0.8 fusion.5
  0.9 10.1 %all_to_all.25 = bf16[4,14,1024]{2,1,0:T(8,128)(2,1)S(1)} all-to-all(bf16[4,14,1024]{2,1,0:T(8,128)(2,1)S(1)} %pad_maximum_fusion.3), channel_id=1, replica_groups=mesh['layer'=4,'quarter'=4,'y'=4,'half'=2,'x'=4,'core'=2] {'x'}, dimensions={0} | all-to-all | bytes 229376 | tf_op jit(solution)/shard_map/all_to_all | solution.py:22
  11.0 29.0 %collective-permute-start = (bf16[56,1024]{1,0:T(8,128)(2,1)S(1)}, bf16[56,1024]{1,0:T(8,128)(2,1)S(1)}, u32[]{:S(2)}, u32[]{:S(2)}) collective-permute-start(bf16[56,1024]{1,0:T(8,128)(2,1)S(1)} %reshape.50), channel_id=1, source_target_pairs={{0,8},{8,0},{1,9},{9,1},{2,10},{10,2},{3,11},{11,3},{4,12},{12,4},... | collective-permute-start | bytes 344072 | tf_op jit(solution)/shard_map/ppermute | solution.py:44
  40.0 3.4 %collective-permute-done = bf16[56,1024]{1,0:T(8,128)(2,1)S(1)} collective-permute-done((bf16[56,1024]{1,0:T(8,128)(2,1)S(1)}, bf16[56,1024]{1,0:T(8,128)(2,1)S(1)}, u32[]{:S(2)}, u32[]{:S(2)}) %collective-permute-start) | collective-permute-done | bytes 114720 | tf_op jit(solution)/shard_map/ppermute | solution.py:44
  43.4 1.0 broadcast_in_dim.4
  44.5 14.5 %all-to-all-start.1 = ((bf16[4,2,56,1024]{3,2,1,0:T(8,128)(2,1)}), bf16[4,2,56,1024]{3,2,1,0:T(8,128)(2,1)S(1)}, u32[]{:S(2)}, u32[]{:S(2)}) async-start(bf16[4,2,56,1024]{3,2,1,0:T(8,128)(2,1)} %broadcast_in_dim.4), calls=%async_computation.1 | async-start | bytes 1835008 | tf_op jit(solution)/shard_map/all_to_all | solution.py:22
  59.0 13.8 %all-gather = bf16[8,56,1024]{2,1,0:T(8,128)(2,1)S(1)} all-gather(bf16[2,56,1024]{2,1,0:T(8,128)(2,1)S(1)} %pad_maximum_fusion.1), channel_id=2, replica_groups=mesh['layer'=4,'quarter'=4,'y'=4,'half'=2,'x'=4,'core'=2] {'y'}, dimensions={0}, use_global_device_ids=true | all-gather | bytes 1146880 | tf_op jit(solution)/shard_map/all_gather | solution.py:48
  72.8 6.6 %all-to-all-done.1 = bf16[4,2,56,1024]{3,2,1,0:T(8,128)(2,1)S(1)} async-done(((bf16[4,2,56,1024]{3,2,1,0:T(8,128)(2,1)}), bf16[4,2,56,1024]{3,2,1,0:T(8,128)(2,1)S(1)}, u32[]{:S(2)}, u32[]{:S(2)}) %all-to-all-start.1) | async-done | bytes 917536 | tf_op jit(solution)/shard_map/all_to_all | solution.py:22
  79.4 1.9 %collective-permute-start.1 = (bf16[4,2,56,1024]{3,2,1,0:T(8,128)(2,1)S(1)}, bf16[4,2,56,1024]{3,2,1,0:T(8,128)(2,1)S(1)}, u32[]{:S(2)}, u32[]{:S(2)}) collective-permute-start(bf16[4,2,56,1024]{3,2,1,0:T(8,128)(2,1)S(1)} %all-to-all-done.1), channel_id=1, source_target_pairs={{0,1},{1,0},{2,3},{3,2},{4,5},{5,4},{6,7},{7,6},{8,9},{9,8},{10,11... | collective-permute-start | bytes 2752520 | tf_op jit(solution)/shard_map/ppermute | solution.py:50
  81.3 2.4 %collective-permute-done.1 = bf16[4,2,56,1024]{3,2,1,0:T(8,128)(2,1)S(1)} collective-permute-done((bf16[4,2,56,1024]{3,2,1,0:T(8,128)(2,1)S(1)}, bf16[4,2,56,1024]{3,2,1,0:T(8,128)(2,1)S(1)}, u32[]{:S(2)}, u32[]{:S(2)}) %collective-permute-start.1) | collective-permute-done | bytes 917536 | tf_op jit(solution)/shard_map/ppermute | solution.py:50
  84.1 0.2 pad_maximum_fusion
  84.2 1.1 convolution_convert_fusion.1
  85.4 15.4 %all_to_all.26 = bf16[4,112,896]{2,1,0:T(8,128)(2,1)S(1)} all-to-all(bf16[4,112,896]{2,1,0:T(8,128)(2,1)S(1)} %bitcast.31), channel_id=1, replica_groups=mesh['layer'=4,'quarter'=4,'y'=4,'half'=2,'x'=4,'core'=2] {'x'}, dimensions={0} | all-to-all | bytes 1605632 | tf_op jit(solution)/shard_map/all_to_all | solution.py:22
  100.9 14.4 %all_gather.14 = bf16[448,896]{1,0:T(8,128)(2,1)S(1)} all-gather(bf16[112,896]{1,0:T(8,128)(2,1)S(1)} %reduce_sum.45), channel_id=1, replica_groups=mesh['layer'=4,'quarter'=4,'y'=4,'half'=2,'x'=4,'core'=2] {'x'}, dimensions={0}, use_global_device_ids=true | all-gather | bytes 1003520 | tf_op jit(solution)/shard_map/all_gather | solution.py:56
  115.3 1.1 convolution_convert_fusion
  116.4 13.4 %all_to_all.27 = bf16[4,112,1024]{2,1,0:T(8,128)(2,1)S(1)} all-to-all(bf16[4,112,1024]{2,1,0:T(8,128)(2,1)S(1)} %bitcast.28), channel_id=1, replica_groups=mesh['layer'=4,'quarter'=4,'y'=4,'half'=2,'x'=4,'core'=2] {'y'}, dimensions={0} | all-to-all | bytes 1835008 | tf_op jit(solution)/shard_map/all_to_all | solution.py:22
  129.9 0.2 select_reduce_fusion.1
  130.1 1.9 %collective-permute-start.2 = (bf16[112,512]{1,0:T(8,128)(2,1)S(1)}, bf16[112,512]{1,0:T(8,128)(2,1)S(1)}, u32[]{:S(2)}, u32[]{:S(2)}) collective-permute-start(bf16[112,512]{1,0:T(8,128)(2,1)S(1)} %get-tuple-element.10), channel_id=1, source_target_pairs={{0,1},{1,0},{2,3},{3,2},{4,5},{5,4},{6,7},{7,6},{8,9},{9,8},{10,11... | collective-permute-start | bytes 344072 | tf_op jit(solution)/shard_map/ppermute | solution.py:63
  132.0 2.4 %collective-permute-start.3 = (bf16[448,448]{1,0:T(8,128)(2,1)S(1)}, bf16[448,448]{1,0:T(8,128)(2,1)S(1)}, u32[]{:S(2)}, u32[]{:S(2)}) collective-permute-start(bf16[448,448]{1,0:T(8,128)(2,1)S(1)} %slice.58), channel_id=1, source_target_pairs={{0,1},{1,0},{2,3},{3,2},{4,5},{5,4},{6,7},{7,6},{8,9},{9,8},{10,11... | collective-permute-start | bytes 1204232 | tf_op jit(solution)/shard_map/ppermute | solution.py:58
  134.5 13.6 %all-gather.1 = bf16[2,448,512]{2,1,0:T(8,128)(2,1)S(1)} all-gather(bf16[2,112,512]{2,1,0:T(8,128)(2,1)S(1)} %pad_maximum_fusion.2), channel_id=3, replica_groups=mesh['layer'=4,'quarter'=4,'y'=4,'half'=2,'x'=4,'core'=2] {'y'}, dimensions={1}, use_global_device_ids=true | all-gather | bytes 1146880 | tf_op jit(solution)/shard_map/all_gather | solution.py:65
  148.1 1.4 convolution_convert_fusion.2
  149.5 3.5 %all-to-all-start.4 = ((bf16[4,112,512]{2,1,0:T(8,128)(2,1)}), bf16[4,112,512]{2,1,0:T(8,128)(2,1)S(1)}, u32[]{:S(2)}, u32[]{:S(2)}) async-start(bf16[4,112,512]{2,1,0:T(8,128)(2,1)} %bitcast.13), calls=%async_computation.4 | async-start | bytes 917504 | tf_op jit(solution)/shard_map/all_to_all | solution.py:22
  153.1 11.3 %all-to-all-done.4 = bf16[4,112,512]{2,1,0:T(8,128)(2,1)S(1)} async-done(((bf16[4,112,512]{2,1,0:T(8,128)(2,1)}), bf16[4,112,512]{2,1,0:T(8,128)(2,1)S(1)}, u32[]{:S(2)}, u32[]{:S(2)}) %all-to-all-start.4) | async-done | bytes 458784 | tf_op jit(solution)/shard_map/all_to_all | solution.py:22
  164.7 0.7 convert_element_type.52
  (21 shorter events, 0.9 us)
Async XLA Ops:
  11.0 32.4 %collective-permute-start = (bf16[56,1024]{1,0:T(8,128)(2,1)S(1)}, bf16[56,1024]{1,0:T(8,128)(2,1)S(1)}, u32[]{:S(2)}, u32[]{:S(2)}) collective-permute-start(bf16[56,1024]{1,0:T(8,128)(2,1)S(1)} %reshape.50), channel_id=1, source_target_pairs={{0,8},{8,0},{1,9},{9,1},{2,10},{10,2},{3,11},{11,3},{4,12},{12,4},... | collective-permute-start | bytes 344072 | tf_op jit(solution)/shard_map/ppermute | solution.py:44
  44.5 34.9 %all-to-all-start.1 = ((bf16[4,2,56,1024]{3,2,1,0:T(8,128)(2,1)}), bf16[4,2,56,1024]{3,2,1,0:T(8,128)(2,1)S(1)}, u32[]{:S(2)}, u32[]{:S(2)}) async-start(bf16[4,2,56,1024]{3,2,1,0:T(8,128)(2,1)} %broadcast_in_dim.4), calls=%async_computation.1 | async-start | bytes 1835008 | tf_op jit(solution)/shard_map/all_to_all | solution.py:22
  79.4 4.4 %collective-permute-start.1 = (bf16[4,2,56,1024]{3,2,1,0:T(8,128)(2,1)S(1)}, bf16[4,2,56,1024]{3,2,1,0:T(8,128)(2,1)S(1)}, u32[]{:S(2)}, u32[]{:S(2)}) collective-permute-start(bf16[4,2,56,1024]{3,2,1,0:T(8,128)(2,1)S(1)} %all-to-all-done.1), channel_id=1, source_target_pairs={{0,1},{1,0},{2,3},{3,2},{4,5},{5,4},{6,7},{7,6},{8,9},{9,8},{10,11... | collective-permute-start | bytes 2752520 | tf_op jit(solution)/shard_map/ppermute | solution.py:50
  130.1 4.4 %collective-permute-start.2 = (bf16[112,512]{1,0:T(8,128)(2,1)S(1)}, bf16[112,512]{1,0:T(8,128)(2,1)S(1)}, u32[]{:S(2)}, u32[]{:S(2)}) collective-permute-start(bf16[112,512]{1,0:T(8,128)(2,1)S(1)} %get-tuple-element.10), channel_id=1, source_target_pairs={{0,1},{1,0},{2,3},{3,2},{4,5},{5,4},{6,7},{7,6},{8,9},{9,8},{10,11... | collective-permute-start | bytes 344072 | tf_op jit(solution)/shard_map/ppermute | solution.py:63
  132.0 16.0 %collective-permute-start.3 = (bf16[448,448]{1,0:T(8,128)(2,1)S(1)}, bf16[448,448]{1,0:T(8,128)(2,1)S(1)}, u32[]{:S(2)}, u32[]{:S(2)}) collective-permute-start(bf16[448,448]{1,0:T(8,128)(2,1)S(1)} %slice.58), channel_id=1, source_target_pairs={{0,1},{1,0},{2,3},{3,2},{4,5},{5,4},{6,7},{7,6},{8,9},{9,8},{10,11... | collective-permute-start | bytes 1204232 | tf_op jit(solution)/shard_map/ppermute | solution.py:58
  149.5 15.0 %all-to-all-start.4 = ((bf16[4,112,512]{2,1,0:T(8,128)(2,1)}), bf16[4,112,512]{2,1,0:T(8,128)(2,1)S(1)}, u32[]{:S(2)}, u32[]{:S(2)}) async-start(bf16[4,112,512]{2,1,0:T(8,128)(2,1)} %bitcast.13), calls=%async_computation.4 | async-start | bytes 917504 | tf_op jit(solution)/shard_map/all_to_all | solution.py:22

commit v18 on v17

--- a/solution.py
+++ b/solution.py
@@ -54,14 +54,15 @@
     term = dot(left, right, ((1,), (1,))).astype(bf16)
     mine = total(exchange(term.reshape(nx, 2 * n, 16 * n), "x")).astype(bf16)
     gram = lax.all_gather(mine, "x", axis=0, tiled=True)
+    term = dot(gram, right, ((1,), (0,))).astype(bf16)
     narrow = gram[:, : 8 * n]
-    narrow = jnp.concatenate([narrow, lax.ppermute(narrow, "core", SWAP)], 0)
-
-    term = dot(gram, right, ((1,), (0,))).astype(bf16)
+    wide = jnp.pad(narrow, ((0, 0), (0, h - 8 * n)))
+    term, wide = lax.optimization_barrier((term, wide))
     terms = exchange(term.reshape(ny, 2 * n, w), "y")
     keep, send = ordered(core, terms[..., :h], terms[..., h:])
-    send = lax.ppermute(total(send).astype(bf16), "core", SWAP)
-    first = jnp.stack([total(keep).astype(bf16), send])
+    got = lax.ppermute(jnp.concatenate([total(send).astype(bf16), wide], 0), "core", SWAP)
+    first = jnp.stack([total(keep).astype(bf16), got[: 2 * n]])
+    narrow = jnp.concatenate([narrow, got[2 * n :, : 8 * n]], 0)
     firsts = lax.all_gather(first, "y", axis=1).reshape(nc * ny * 2 * n, h)
 
     term = dot(narrow, firsts, ((0,), (0,))).astype(bf16)

time: 166 us -> 166 us (level)
  starting transfers between devices: 53.2 us -> 50.8 us
  waiting for transfers between devices: 23.8 us -> 25.7 us
    ppermute x2 -> x1, starting transfers between devices: 4.33 us -> 1.92 us  [shards(): lax.ppermute(jnp.concatenate([total(send).astype(bf16), wide], 0), 'core'...]
    ppermute x2 -> x1, waiting for transfers between devices: 0.01 us -> 1.93 us  [shards(): lax.ppermute(jnp.concatenate([total(send).astype(bf16), wide], 0), 'core'...]
  transfers between devices with their start and end apart: 6 -> 5, of which waited for: 4 -> 5; matrix products, arithmetic and copies ran while one was open for 0% -> 0% of each run, Pallas kernels for 0% -> 0%
where the time goes in v18:
time: 166 us; the launch traced here: 165 us
  blocking collectives  80.8 us (49%)
  starting transfers between devices  50.8 us (31%)
  waiting for transfers between devices  25.7 us (15%)
  matrix products  3.71 us (2%)
  local copies, waits for them, and re-layouts  2.77 us (2%)
    all_to_all x3, blocking collectives, exchange(): return lax.all_to_all(blocks, axis, 0, 0, tiled=True)  38.9 us
    ppermute x1, starting transfers between devices, shards(): other = lax.ppermute(own, 'half', SWAP)  29 us
    all_to_all x2, starting transfers between devices, exchange(): return lax.all_to_all(blocks, axis, 0, 0, tiled=True)  18 us
    all_to_all x2, waiting for transfers between devices, exchange(): return lax.all_to_all(blocks, axis, 0, 0, tiled=True)  18 us
    all_gather x1, blocking collectives, shards(): gram = lax.all_gather(mine, 'x', axis=0, tiled=True)  14.4 us
    all_gather x1, blocking collectives, shards(): left = lax.all_gather(both, 'y', axis=0).reshape(ny * 2 * n, w)  13.8 us
    all_gather x1, blocking collectives, shards(): firsts = lax.all_gather(first, 'y', axis=1).reshape(nc * ny * 2 * n, h)  13.7 us
    dot_general x3, matrix products, dot(): lax.dot_general(lhs, rhs, (dims, ((), ())), preferred_element_type=jnp.fl...  3.71 us
  transfers between devices with their start and end apart: 5, of which 5 were waited for; matrix products, arithmetic and copies ran while one was open for 0% of the time, Pallas kernels for 0%

profile of v18, /device:TPU:8, one launch (start us, length us, event | category | flops | bytes accessed | tf_op | source)
XLA Modules:
  0.0 165.2 jit_solution(10469201061286310182)
XLA Ops:
  0.0 0.8 fusion.5
  0.9 10.1 %all_to_all.25 = bf16[4,14,1024]{2,1,0:T(8,128)(2,1)S(1)} all-to-all(bf16[4,14,1024]{2,1,0:T(8,128)(2,1)S(1)} %pad_maximum_fusion.4), channel_id=1, replica_groups=mesh['layer'=4,'quarter'=4,'y'=4,'half'=2,'x'=4,'core'=2] {'x'}, dimensions={0} | all-to-all | bytes 229376 | tf_op jit(solution)/shard_map/all_to_all | solution.py:22
  11.0 29.0 %collective-permute-start = (bf16[56,1024]{1,0:T(8,128)(2,1)S(1)}, bf16[56,1024]{1,0:T(8,128)(2,1)S(1)}, u32[]{:S(2)}, u32[]{:S(2)}) collective-permute-start(bf16[56,1024]{1,0:T(8,128)(2,1)S(1)} %reshape.50), channel_id=1, source_target_pairs={{0,8},{8,0},{1,9},{9,1},{2,10},{10,2},{3,11},{11,3},{4,12},{12,4},... | collective-permute-start | bytes 344072 | tf_op jit(solution)/shard_map/ppermute | solution.py:44
  40.0 3.4 %collective-permute-done = bf16[56,1024]{1,0:T(8,128)(2,1)S(1)} collective-permute-done((bf16[56,1024]{1,0:T(8,128)(2,1)S(1)}, bf16[56,1024]{1,0:T(8,128)(2,1)S(1)}, u32[]{:S(2)}, u32[]{:S(2)}) %collective-permute-start) | collective-permute-done | bytes 114720 | tf_op jit(solution)/shard_map/ppermute | solution.py:44
  43.4 1.0 broadcast_in_dim.4
  44.5 14.5 %all-to-all-start.1 = ((bf16[4,2,56,1024]{3,2,1,0:T(8,128)(2,1)}), bf16[4,2,56,1024]{3,2,1,0:T(8,128)(2,1)S(1)}, u32[]{:S(2)}, u32[]{:S(2)}) async-start(bf16[4,2,56,1024]{3,2,1,0:T(8,128)(2,1)} %broadcast_in_dim.4), calls=%async_computation.1 | async-start | bytes 1835008 | tf_op jit(solution)/shard_map/all_to_all | solution.py:22
  59.0 13.8 %all-gather = bf16[8,56,1024]{2,1,0:T(8,128)(2,1)S(1)} all-gather(bf16[2,56,1024]{2,1,0:T(8,128)(2,1)S(1)} %pad_maximum_fusion.2), channel_id=2, replica_groups=mesh['layer'=4,'quarter'=4,'y'=4,'half'=2,'x'=4,'core'=2] {'y'}, dimensions={0}, use_global_device_ids=true | all-gather | bytes 1146880 | tf_op jit(solution)/shard_map/all_gather | solution.py:48
  72.8 6.6 %all-to-all-done.1 = bf16[4,2,56,1024]{3,2,1,0:T(8,128)(2,1)S(1)} async-done(((bf16[4,2,56,1024]{3,2,1,0:T(8,128)(2,1)}), bf16[4,2,56,1024]{3,2,1,0:T(8,128)(2,1)S(1)}, u32[]{:S(2)}, u32[]{:S(2)}) %all-to-all-start.1) | async-done | bytes 917536 | tf_op jit(solution)/shard_map/all_to_all | solution.py:22
  79.4 1.9 %collective-permute-start.1 = (bf16[4,2,56,1024]{3,2,1,0:T(8,128)(2,1)S(1)}, bf16[4,2,56,1024]{3,2,1,0:T(8,128)(2,1)S(1)}, u32[]{:S(2)}, u32[]{:S(2)}) collective-permute-start(bf16[4,2,56,1024]{3,2,1,0:T(8,128)(2,1)S(1)} %all-to-all-done.1), channel_id=1, source_target_pairs={{0,1},{1,0},{2,3},{3,2},{4,5},{5,4},{6,7},{7,6},{8,9},{9,8},{10,11... | collective-permute-start | bytes 2752520 | tf_op jit(solution)/shard_map/ppermute | solution.py:50
  81.3 2.4 %collective-permute-done.1 = bf16[4,2,56,1024]{3,2,1,0:T(8,128)(2,1)S(1)} collective-permute-done((bf16[4,2,56,1024]{3,2,1,0:T(8,128)(2,1)S(1)}, bf16[4,2,56,1024]{3,2,1,0:T(8,128)(2,1)S(1)}, u32[]{:S(2)}, u32[]{:S(2)}) %collective-permute-start.1) | collective-permute-done | bytes 917536 | tf_op jit(solution)/shard_map/ppermute | solution.py:50
  84.1 0.2 pad_maximum_fusion
  84.2 1.1 convolution_convert_fusion.1
  85.4 15.4 %all_to_all.26 = bf16[4,112,896]{2,1,0:T(8,128)(2,1)S(1)} all-to-all(bf16[4,112,896]{2,1,0:T(8,128)(2,1)S(1)} %bitcast.32), channel_id=1, replica_groups=mesh['layer'=4,'quarter'=4,'y'=4,'half'=2,'x'=4,'core'=2] {'x'}, dimensions={0} | all-to-all | bytes 1605632 | tf_op jit(solution)/shard_map/all_to_all | solution.py:22
  100.9 14.4 %all_gather.14 = bf16[448,896]{1,0:T(8,128)(2,1)S(1)} all-gather(bf16[112,896]{1,0:T(8,128)(2,1)S(1)} %reduce_sum.45), channel_id=1, replica_groups=mesh['layer'=4,'quarter'=4,'y'=4,'half'=2,'x'=4,'core'=2] {'x'}, dimensions={0}, use_global_device_ids=true | all-gather | bytes 1003520 | tf_op jit(solution)/shard_map/all_gather | solution.py:56
  115.3 1.1 convolution_convert_fusion
  116.5 13.4 %all_to_all.27 = bf16[4,112,1024]{2,1,0:T(8,128)(2,1)S(1)} all-to-all(bf16[4,112,1024]{2,1,0:T(8,128)(2,1)S(1)} %bitcast.29), channel_id=1, replica_groups=mesh['layer'=4,'quarter'=4,'y'=4,'half'=2,'x'=4,'core'=2] {'y'}, dimensions={0} | all-to-all | bytes 1835008 | tf_op jit(solution)/shard_map/all_to_all | solution.py:22
  129.9 0.2 select_reduce_fusion.1
  130.2 1.9 %collective-permute-start.2 = (bf16[560,512]{1,0:T(8,128)(2,1)S(1)}, bf16[560,512]{1,0:T(8,128)(2,1)S(1)}, u32[]{:S(2)}, u32[]{:S(2)}) collective-permute-start(bf16[560,512]{1,0:T(8,128)(2,1)S(1)} %pad_maximum_fusion.1), channel_id=1, source_target_pairs={{0,1},{1,0},{2,3},{3,2},{4,5},{5,4},{6,7},{7,6},{8,9},{9,8},{10,11... | collective-permute-start | bytes 1720328 | tf_op jit(solution)/shard_map/ppermute | solution.py:63
  132.1 1.9 %collective-permute-done.2 = bf16[560,512]{1,0:T(8,128)(2,1)S(1)} collective-permute-done((bf16[560,512]{1,0:T(8,128)(2,1)S(1)}, bf16[560,512]{1,0:T(8,128)(2,1)S(1)}, u32[]{:S(2)}, u32[]{:S(2)}) %collective-permute-start.2) | collective-permute-done | bytes 573472 | tf_op jit(solution)/shard_map/ppermute | solution.py:63
  134.1 13.7 %all-gather.1 = bf16[2,448,512]{2,1,0:T(8,128)(2,1)S(1)} all-gather(bf16[2,112,512]{2,1,0:T(8,128)(2,1)S(1)} %pad_maximum_fusion.3), channel_id=3, replica_groups=mesh['layer'=4,'quarter'=4,'y'=4,'half'=2,'x'=4,'core'=2] {'y'}, dimensions={1}, use_global_device_ids=true | all-gather | bytes 1146880 | tf_op jit(solution)/shard_map/all_gather | solution.py:66
  147.8 1.4 convolution_convert_fusion.2
  149.3 3.5 %all-to-all-start.4 = ((bf16[4,112,512]{2,1,0:T(8,128)(2,1)}), bf16[4,112,512]{2,1,0:T(8,128)(2,1)S(1)}, u32[]{:S(2)}, u32[]{:S(2)}) async-start(bf16[4,112,512]{2,1,0:T(8,128)(2,1)} %bitcast.13), calls=%async_computation.4 | async-start | bytes 917504 | tf_op jit(solution)/shard_map/all_to_all | solution.py:22
  152.9 11.3 %all-to-all-done.4 = bf16[4,112,512]{2,1,0:T(8,128)(2,1)S(1)} async-done(((bf16[4,112,512]{2,1,0:T(8,128)(2,1)}), bf16[4,112,512]{2,1,0:T(8,128)(2,1)S(1)}, u32[]{:S(2)}, u32[]{:S(2)}) %all-to-all-start.4) | async-done | bytes 458784 | tf_op jit(solution)/shard_map/all_to_all | solution.py:22
  164.5 0.7 convert_element_type.54
  (28 shorter events, 1.0 us)
Async XLA Ops:
  11.0 32.4 %collective-permute-start = (bf16[56,1024]{1,0:T(8,128)(2,1)S(1)}, bf16[56,1024]{1,0:T(8,128)(2,1)S(1)}, u32[]{:S(2)}, u32[]{:S(2)}) collective-permute-start(bf16[56,1024]{1,0:T(8,128)(2,1)S(1)} %reshape.50), channel_id=1, source_target_pairs={{0,8},{8,0},{1,9},{9,1},{2,10},{10,2},{3,11},{11,3},{4,12},{12,4},... | collective-permute-start | bytes 344072 | tf_op jit(solution)/shard_map/ppermute | solution.py:44
  44.5 34.9 %all-to-all-start.1 = ((bf16[4,2,56,1024]{3,2,1,0:T(8,128)(2,1)}), bf16[4,2,56,1024]{3,2,1,0:T(8,128)(2,1)S(1)}, u32[]{:S(2)}, u32[]{:S(2)}) async-start(bf16[4,2,56,1024]{3,2,1,0:T(8,128)(2,1)} %broadcast_in_dim.4), calls=%async_computation.1 | async-start | bytes 1835008 | tf_op jit(solution)/shard_map/all_to_all | solution.py:22
  79.4 4.4 %collective-permute-start.1 = (bf16[4,2,56,1024]{3,2,1,0:T(8,128)(2,1)S(1)}, bf16[4,2,56,1024]{3,2,1,0:T(8,128)(2,1)S(1)}, u32[]{:S(2)}, u32[]{:S(2)}) collective-permute-start(bf16[4,2,56,1024]{3,2,1,0:T(8,128)(2,1)S(1)} %all-to-all-done.1), channel_id=1, source_target_pairs={{0,1},{1,0},{2,3},{3,2},{4,5},{5,4},{6,7},{7,6},{8,9},{9,8},{10,11... | collective-permute-start | bytes 2752520 | tf_op jit(solution)/shard_map/ppermute | solution.py:50
  115.3 16.8 %copy-start = (bf16[448,896]{1,0:T(8,128)(2,1)}, bf16[448,896]{1,0:T(8,128)(2,1)S(1)}, u32[]{:S(2)}) copy-start(bf16[448,896]{1,0:T(8,128)(2,1)S(1)} %all_gather.14) | copy-start | bytes 2408452
  115.3 1.1 copy-start.1
  130.2 3.9 %collective-permute-start.2 = (bf16[560,512]{1,0:T(8,128)(2,1)S(1)}, bf16[560,512]{1,0:T(8,128)(2,1)S(1)}, u32[]{:S(2)}, u32[]{:S(2)}) collective-permute-start(bf16[560,512]{1,0:T(8,128)(2,1)S(1)} %pad_maximum_fusion.1), channel_id=1, source_target_pairs={{0,1},{1,0},{2,3},{3,2},{4,5},{5,4},{6,7},{7,6},{8,9},{9,8},{10,11... | collective-permute-start | bytes 1720328 | tf_op jit(solution)/shard_map/ppermute | solution.py:63
  132.1 15.7 %slice-start = ((bf16[448,896]{1,0:T(8,128)(2,1)}), bf16[448,448]{1,0:T(8,128)(2,1)S(1)}, s32[]{:S(2)}) async-start(bf16[448,896]{1,0:T(8,128)(2,1)} %copy-done), calls=%async_computation.5 | async-start | bytes 917504 | tf_op jit(solution)/shard_map/slice | solution.py:58
  149.3 15.0 %all-to-all-start.4 = ((bf16[4,112,512]{2,1,0:T(8,128)(2,1)}), bf16[4,112,512]{2,1,0:T(8,128)(2,1)S(1)}, u32[]{:S(2)}, u32[]{:S(2)}) async-start(bf16[4,112,512]{2,1,0:T(8,128)(2,1)} %bitcast.13), calls=%async_computation.4 | async-start | bytes 917504 | tf_op jit(solution)/shard_map/all_to_all | solution.py:22

commit v19 on v18

--- a/solution.py
+++ b/solution.py
@@ -61,20 +61,23 @@
     terms = exchange(term.reshape(ny, 2 * n, w), "y")
     keep, send = ordered(core, terms[..., :h], terms[..., h:])
     got = lax.ppermute(jnp.concatenate([total(send).astype(bf16), wide], 0), "core", SWAP)
+    tile = lax.dynamic_slice(
+        right.reshape(2 * nq, nc * n, w), (lax.axis_index("quarter"), 0, core * h), (1, nc * n, h)
+    )[0]
+    tile, got = lax.optimization_barrier((A1 * tile.astype(jnp.float32), got))
     first = jnp.stack([total(keep).astype(bf16), got[: 2 * n]])
     narrow = jnp.concatenate([narrow, got[2 * n :, : 8 * n]], 0)
     firsts = lax.all_gather(first, "y", axis=1).reshape(nc * ny * 2 * n, h)
+    first = jnp.concatenate(ordered(core, first[0, :n], first[1, :n]), 0)
+    part = tile + A2 * first.astype(jnp.float32)
 
     term = dot(narrow, firsts, ((0,), (0,))).astype(bf16)
+    term, part = lax.optimization_barrier((term, part))
     second = total(exchange(term.reshape(nq, nc * n, h), "quarter"))
-    first = jnp.concatenate(ordered(core, first[0, :n], first[1, :n]), 0)
-    tile = lax.dynamic_slice(
-        right.reshape(2 * nq, nc * n, w), (lax.axis_index("quarter"), 0, core * h), (1, nc * n, h)
-    )[0]
-    mixed = A1 * tile.astype(jnp.float32) + A2 * first.astype(jnp.float32) + A3 * second
-    mixed = math.sqrt(max(256 * m, k)) * mixed
-    mixed = mixed.reshape(nc, nx, m, h).transpose(1, 0, 2, 3).reshape(nc * n, h)
-    return mixed.astype(bf16)[None]
+    mixed = math.sqrt(max(256 * m, k)) * (part + A3 * second)
+    mixed = mixed.astype(bf16)
+    pieces = [mixed[(c * nx + i) * m : (c * nx + i + 1) * m] for i in range(nx) for c in range(nc)]
+    return jnp.concatenate(pieces, 0)[None]
 
 
 def solution(mesh):

time: 166 us -> 175 us (1.054)
  the two profiles are of different devices: /device:TPU:8 before, /device:TPU:2 now
where the time goes in v19:
time: 175 us; the launch traced here: 174 us
  blocking collectives  108 us (62%)
  starting transfers between devices  32.4 us (19%)
  waiting for transfers between devices  17 us (10%)
  local copies, waits for them, and re-layouts  11.6 us (7%)
  matrix products  2.94 us (2%)
  other arithmetic  1.9 us (1%)
    all_to_all x4, blocking collectives, exchange(): return lax.all_to_all(blocks, axis, 0, 0, tiled=True)  64.7 us
    ppermute x1, starting transfers between devices, shards(): other = lax.ppermute(own, 'half', SWAP)  18 us
    all_gather x1, blocking collectives, shards(): left = lax.all_gather(both, 'y', axis=0).reshape(ny * 2 * n, w)  15.3 us
    all_gather x1, blocking collectives, shards(): firsts = lax.all_gather(first, 'y', axis=1).reshape(nc * ny * 2 * n, h)  14.6 us
    all_gather x1, blocking collectives, shards(): gram = lax.all_gather(mine, 'x', axis=0, tiled=True)  13.3 us
    all_to_all x1, starting transfers between devices, exchange(): return lax.all_to_all(blocks, axis, 0, 0, tiled=True)  10.6 us
    concatenate x1, local copies, waits for them, and re-layouts, shards(): return jnp.concatenate(pieces, 0)[None]  9.53 us
    ppermute x1, waiting for transfers between devices, shards(): other = lax.ppermute(own, 'half', SWAP)  7.36 us
  transfers between devices with their start and end apart: 4, of which 4 were waited for; matrix products, arithmetic and copies ran while one was open for 0% of the time, Pallas kernels for 0%

profile of v19, /device:TPU:2, one launch (start us, length us, event | category | flops | bytes accessed | tf_op | source)
XLA Modules:
  0.0 173.9 jit_solution(968699762080601228)
XLA Ops:
  0.0 0.8 fusion.4
  0.9 20.1 %all_to_all.25 = bf16[4,14,1024]{2,1,0:T(8,128)(2,1)S(1)} all-to-all(bf16[4,14,1024]{2,1,0:T(8,128)(2,1)S(1)} %pad_maximum_fusion.4), channel_id=1, replica_groups=mesh['layer'=4,'quarter'=4,'y'=4,'half'=2,'x'=4,'core'=2] {'x'}, dimensions={0} | all-to-all | bytes 229376 | tf_op jit(solution)/shard_map/all_to_all | solution.py:22
  21.0 18.0 %collective-permute-start = (bf16[56,1024]{1,0:T(8,128)(2,1)S(1)}, bf16[56,1024]{1,0:T(8,128)(2,1)S(1)}, u32[]{:S(2)}, u32[]{:S(2)}) collective-permute-start(bf16[56,1024]{1,0:T(8,128)(2,1)S(1)} %reshape.29), channel_id=1, source_target_pairs={{0,8},{8,0},{1,9},{9,1},{2,10},{10,2},{3,11},{11,3},{4,12},{12,4},... | collective-permute-start | bytes 344072 | tf_op jit(solution)/shard_map/ppermute | solution.py:44
  39.1 7.4 %collective-permute-done = bf16[56,1024]{1,0:T(8,128)(2,1)S(1)} collective-permute-done((bf16[56,1024]{1,0:T(8,128)(2,1)S(1)}, bf16[56,1024]{1,0:T(8,128)(2,1)S(1)}, u32[]{:S(2)}, u32[]{:S(2)}) %collective-permute-start) | collective-permute-done | bytes 114720 | tf_op jit(solution)/shard_map/ppermute | solution.py:44
  46.5 1.0 broadcast_in_dim.11
  47.5 10.6 %all-to-all-start.1 = ((bf16[4,2,56,1024]{3,2,1,0:T(8,128)(2,1)}), bf16[4,2,56,1024]{3,2,1,0:T(8,128)(2,1)S(1)}, u32[]{:S(2)}, u32[]{:S(2)}) async-start(bf16[4,2,56,1024]{3,2,1,0:T(8,128)(2,1)} %broadcast_in_dim.11), calls=%async_computation.1 | async-start | bytes 1835008 | tf_op jit(solution)/shard_map/all_to_all | solution.py:22
  58.1 15.3 %all-gather = bf16[8,56,1024]{2,1,0:T(8,128)(2,1)S(1)} all-gather(bf16[2,56,1024]{2,1,0:T(8,128)(2,1)S(1)} %pad_maximum_fusion.2), channel_id=2, replica_groups=mesh['layer'=4,'quarter'=4,'y'=4,'half'=2,'x'=4,'core'=2] {'y'}, dimensions={0}, use_global_device_ids=true | all-gather | bytes 1146880 | tf_op jit(solution)/shard_map/all_gather | solution.py:48
  73.4 5.1 %all-to-all-done.1 = bf16[4,2,56,1024]{3,2,1,0:T(8,128)(2,1)S(1)} async-done(((bf16[4,2,56,1024]{3,2,1,0:T(8,128)(2,1)}), bf16[4,2,56,1024]{3,2,1,0:T(8,128)(2,1)S(1)}, u32[]{:S(2)}, u32[]{:S(2)}) %all-to-all-start.1) | async-done | bytes 917536 | tf_op jit(solution)/shard_map/all_to_all | solution.py:22
  78.5 1.9 %collective-permute-start.1 = (bf16[4,2,56,1024]{3,2,1,0:T(8,128)(2,1)S(1)}, bf16[4,2,56,1024]{3,2,1,0:T(8,128)(2,1)S(1)}, u32[]{:S(2)}, u32[]{:S(2)}) collective-permute-start(bf16[4,2,56,1024]{3,2,1,0:T(8,128)(2,1)S(1)} %all-to-all-done.1), channel_id=1, source_target_pairs={{0,1},{1,0},{2,3},{3,2},{4,5},{5,4},{6,7},{7,6},{8,9},{9,8},{10,11... | collective-permute-start | bytes 2752520 | tf_op jit(solution)/shard_map/ppermute | solution.py:50
  80.4 2.4 %collective-permute-done.1 = bf16[4,2,56,1024]{3,2,1,0:T(8,128)(2,1)S(1)} collective-permute-done((bf16[4,2,56,1024]{3,2,1,0:T(8,128)(2,1)S(1)}, bf16[4,2,56,1024]{3,2,1,0:T(8,128)(2,1)S(1)}, u32[]{:S(2)}, u32[]{:S(2)}) %collective-permute-start.1) | collective-permute-done | bytes 917536 | tf_op jit(solution)/shard_map/ppermute | solution.py:50
  83.1 0.2 pad_maximum_fusion
  83.3 1.1 convolution_convert_fusion.1
  84.5 15.4 %all_to_all.26 = bf16[4,112,896]{2,1,0:T(8,128)(2,1)S(1)} all-to-all(bf16[4,112,896]{2,1,0:T(8,128)(2,1)S(1)} %bitcast.33), channel_id=1, replica_groups=mesh['layer'=4,'quarter'=4,'y'=4,'half'=2,'x'=4,'core'=2] {'x'}, dimensions={0} | all-to-all | bytes 1605632 | tf_op jit(solution)/shard_map/all_to_all | solution.py:22
  100.0 13.3 %all_gather.14 = bf16[448,896]{1,0:T(8,128)(2,1)S(1)} all-gather(bf16[112,896]{1,0:T(8,128)(2,1)S(1)} %reduce_sum.45), channel_id=1, replica_groups=mesh['layer'=4,'quarter'=4,'y'=4,'half'=2,'x'=4,'core'=2] {'x'}, dimensions={0}, use_global_device_ids=true | all-gather | bytes 1003520 | tf_op jit(solution)/shard_map/all_gather | solution.py:56
  113.4 1.1 convolution_convert_fusion
  114.5 15.7 %all_to_all.27 = bf16[4,112,1024]{2,1,0:T(8,128)(2,1)S(1)} all-to-all(bf16[4,112,1024]{2,1,0:T(8,128)(2,1)S(1)} %bitcast.30), channel_id=1, replica_groups=mesh['layer'=4,'quarter'=4,'y'=4,'half'=2,'x'=4,'core'=2] {'y'}, dimensions={0} | all-to-all | bytes 1835008 | tf_op jit(solution)/shard_map/all_to_all | solution.py:22
  130.2 0.2 select_reduce_fusion
  130.4 0.8 pad_maximum_fusion.1
  131.3 1.9 %collective-permute-start.2 = (bf16[560,512]{1,0:T(8,128)(2,1)}, bf16[560,512]{1,0:T(8,128)(2,1)S(1)}, u32[]{:S(2)}, u32[]{:S(2)}) collective-permute-start(bf16[560,512]{1,0:T(8,128)(2,1)} %pad_maximum_fusion.1), channel_id=1, source_target_pairs={{0,1},{1,0},{2,3},{3,2},{4,5},{5,4},{6,7},{7,6},{8,9},{9,8},{10,11... | collective-permute-start | bytes 1720328 | tf_op jit(solution)/shard_map/ppermute | solution.py:63
  133.2 2.1 %collective-permute-done.2 = bf16[560,512]{1,0:T(8,128)(2,1)S(1)} collective-permute-done((bf16[560,512]{1,0:T(8,128)(2,1)}, bf16[560,512]{1,0:T(8,128)(2,1)S(1)}, u32[]{:S(2)}, u32[]{:S(2)}) %collective-permute-start.2) | collective-permute-done | bytes 573472 | tf_op jit(solution)/shard_map/ppermute | solution.py:63
  135.4 14.6 %all-gather.1 = bf16[2,448,512]{2,1,0:T(8,128)(2,1)S(1)} all-gather(bf16[2,112,512]{2,1,0:T(8,128)(2,1)S(1)} %pad_maximum_fusion.3), channel_id=3, replica_groups=mesh['layer'=4,'quarter'=4,'y'=4,'half'=2,'x'=4,'core'=2] {'y'}, dimensions={1}, use_global_device_ids=true | all-gather | bytes 1146880 | tf_op jit(solution)/shard_map/all_gather | solution.py:70
  150.1 0.7 convolution_convert_fusion.2
  150.7 13.5 %all_to_all.28 = bf16[4,112,512]{2,1,0:T(8,128)(2,1)S(1)} all-to-all(bf16[4,112,512]{2,1,0:T(8,128)(2,1)S(1)} %bitcast.36), channel_id=1, replica_groups=mesh['layer'=4,'quarter'=4,'y'=4,'half'=2,'x'=4,'core'=2] {'quarter'}, dimensions={0} | all-to-all | bytes 917504 | tf_op jit(solution)/shard_map/all_to_all | solution.py:22
  164.4 9.5 %concatenate.15 = bf16[112,512]{1,0:T(8,128)(2,1)} concatenate(bf16[14,512]{1,0:T(8,128)(2,1)S(1)} %get-tuple-element.40, bf16[14,512]{1,0:T(8,128)(2,1)S(1)} %get-tuple-element.39, bf16[14,512]{1,0:T(8,128)(2,1)S(1)} %get-tuple-element.38, bf16[14,512]{1,0:T(8,128)(2,1)S(1)} %get-tuple-element.37, bf16[14,512]{1,0:T(8,128)(2,1)S(1)} %get-tuple-element.36, ...), dimensions={0} | concatenate | bytes 229376 | tf_op jit(solution)/shard_map/concatenate | solution.py:80
  (23 shorter events, 0.9 us)
Async XLA Ops:
  21.0 25.4 %collective-permute-start = (bf16[56,1024]{1,0:T(8,128)(2,1)S(1)}, bf16[56,1024]{1,0:T(8,128)(2,1)S(1)}, u32[]{:S(2)}, u32[]{:S(2)}) collective-permute-start(bf16[56,1024]{1,0:T(8,128)(2,1)S(1)} %reshape.29), channel_id=1, source_target_pairs={{0,8},{8,0},{1,9},{9,1},{2,10},{10,2},{3,11},{11,3},{4,12},{12,4},... | collective-permute-start | bytes 344072 | tf_op jit(solution)/shard_map/ppermute | solution.py:44
  47.5 31.0 %all-to-all-start.1 = ((bf16[4,2,56,1024]{3,2,1,0:T(8,128)(2,1)}), bf16[4,2,56,1024]{3,2,1,0:T(8,128)(2,1)S(1)}, u32[]{:S(2)}, u32[]{:S(2)}) async-start(bf16[4,2,56,1024]{3,2,1,0:T(8,128)(2,1)} %broadcast_in_dim.11), calls=%async_computation.1 | async-start | bytes 1835008 | tf_op jit(solution)/shard_map/all_to_all | solution.py:22
  78.5 4.4 %collective-permute-start.1 = (bf16[4,2,56,1024]{3,2,1,0:T(8,128)(2,1)S(1)}, bf16[4,2,56,1024]{3,2,1,0:T(8,128)(2,1)S(1)}, u32[]{:S(2)}, u32[]{:S(2)}) collective-permute-start(bf16[4,2,56,1024]{3,2,1,0:T(8,128)(2,1)S(1)} %all-to-all-done.1), channel_id=1, source_target_pairs={{0,1},{1,0},{2,3},{3,2},{4,5},{5,4},{6,7},{7,6},{8,9},{9,8},{10,11... | collective-permute-start | bytes 2752520 | tf_op jit(solution)/shard_map/ppermute | solution.py:50
  113.4 19.9 %copy-start = (bf16[448,896]{1,0:T(8,128)(2,1)}, bf16[448,896]{1,0:T(8,128)(2,1)S(1)}, u32[]{:S(2)}) copy-start(bf16[448,896]{1,0:T(8,128)(2,1)S(1)} %all_gather.14) | copy-start | bytes 2408452
  113.4 1.1 copy-start.1
  131.3 4.1 %collective-permute-start.2 = (bf16[560,512]{1,0:T(8,128)(2,1)}, bf16[560,512]{1,0:T(8,128)(2,1)S(1)}, u32[]{:S(2)}, u32[]{:S(2)}) collective-permute-start(bf16[560,512]{1,0:T(8,128)(2,1)} %pad_maximum_fusion.1), channel_id=1, source_target_pairs={{0,1},{1,0},{2,3},{3,2},{4,5},{5,4},{6,7},{7,6},{8,9},{9,8},{10,11... | collective-permute-start | bytes 1720328 | tf_op jit(solution)/shard_map/ppermute | solution.py:63
  133.2 16.8 %slice-start = ((bf16[448,896]{1,0:T(8,128)(2,1)}), bf16[448,448]{1,0:T(8,128)(2,1)S(1)}, s32[]{:S(2)}) async-start(bf16[448,896]{1,0:T(8,128)(2,1)} %copy-done), calls=%async_computation.5 | async-start | bytes 917504 | tf_op jit(solution)/shard_map/slice | solution.py:58

commit v20 on v17

--- a/solution.py
+++ b/solution.py
@@ -64,14 +64,16 @@
     first = jnp.stack([total(keep).astype(bf16), send])
     firsts = lax.all_gather(first, "y", axis=1).reshape(nc * ny * 2 * n, h)
 
-    term = dot(narrow, firsts, ((0,), (0,))).astype(bf16)
-    second = total(exchange(term.reshape(nq, nc * n, h), "quarter"))
     first = jnp.concatenate(ordered(core, first[0, :n], first[1, :n]), 0)
     tile = lax.dynamic_slice(
         right.reshape(2 * nq, nc * n, w), (lax.axis_index("quarter"), 0, core * h), (1, nc * n, h)
     )[0]
-    mixed = A1 * tile.astype(jnp.float32) + A2 * first.astype(jnp.float32) + A3 * second
-    mixed = math.sqrt(max(256 * m, k)) * mixed
+    part = A1 * tile.astype(jnp.float32) + A2 * first.astype(jnp.float32)
+
+    term = dot(narrow, firsts, ((0,), (0,))).astype(bf16)
+    term, part = lax.optimization_barrier((term, part))
+    second = total(exchange(term.reshape(nq, nc * n, h), "quarter"))
+    mixed = math.sqrt(max(256 * m, k)) * (part + A3 * second)
     mixed = mixed.reshape(nc, nx, m, h).transpose(1, 0, 2, 3).reshape(nc * n, h)
     return mixed.astype(bf16)[None]
 

time: 166 us -> 165 us (level)
  blocking collectives: 80.7 us -> 95.2 us
  waiting for transfers between devices: 23.8 us -> 12.5 us
  starting transfers between devices: 53.2 us -> 49.7 us
    all_to_all x3 -> x4, blocking collectives: 38.9 us -> 53.5 us  [exchange(): return lax.all_to_all(blocks, axis, 0, 0, tiled=True)]
    all_to_all x2 -> x1, waiting for transfers between devices: 18 us -> 6.65 us  [exchange(): return lax.all_to_all(blocks, axis, 0, 0, tiled=True)]
    all_to_all x2 -> x1, starting transfers between devices: 18 us -> 14.5 us  [exchange(): return lax.all_to_all(blocks, axis, 0, 0, tiled=True)]
  transfers between devices with their start and end apart: 6 -> 5, of which waited for: 4 -> 3; matrix products, arithmetic and copies ran while one was open for 0% -> 0% of each run, Pallas kernels for 0% -> 0%
where the time goes in v20:
time: 165 us; the launch traced here: 164 us
  blocking collectives  95.2 us (58%)
  starting transfers between devices  49.7 us (30%)
  waiting for transfers between devices  12.5 us (8%)
  matrix products  2.94 us (2%)
  local copies, waits for them, and re-layouts  2.7 us (2%)
    all_to_all x4, blocking collectives, exchange(): return lax.all_to_all(blocks, axis, 0, 0, tiled=True)  53.5 us
    ppermute x1, starting transfers between devices, shards(): other = lax.ppermute(own, 'half', SWAP)  29 us
    all_to_all x1, starting transfers between devices, exchange(): return lax.all_to_all(blocks, axis, 0, 0, tiled=True)  14.5 us
    all_gather x1, blocking collectives, shards(): gram = lax.all_gather(mine, 'x', axis=0, tiled=True)  14.4 us
    all_gather x1, blocking collectives, shards(): left = lax.all_gather(both, 'y', axis=0).reshape(ny * 2 * n, w)  13.8 us
    all_gather x1, blocking collectives, shards(): firsts = lax.all_gather(first, 'y', axis=1).reshape(nc * ny * 2 * n, h)  13.6 us
    all_to_all x1, waiting for transfers between devices, exchange(): return lax.all_to_all(blocks, axis, 0, 0, tiled=True)  6.65 us
    ppermute x1, waiting for transfers between devices, shards(): other = lax.ppermute(own, 'half', SWAP)  3.41 us
  transfers between devices with their start and end apart: 5, of which 3 were waited for; matrix products, arithmetic and copies ran while one was open for 0% of the time, Pallas kernels for 0%

profile of v20, /device:TPU:8, one launch (start us, length us, event | category | flops | bytes accessed | tf_op | source)
XLA Modules:
  0.0 164.2 jit_solution(2730487524544383031)
XLA Ops:
  0.0 0.8 fusion.4
  0.9 10.1 %all_to_all.25 = bf16[4,14,1024]{2,1,0:T(8,128)(2,1)S(1)} all-to-all(bf16[4,14,1024]{2,1,0:T(8,128)(2,1)S(1)} %pad_maximum_fusion.3), channel_id=1, replica_groups=mesh['layer'=4,'quarter'=4,'y'=4,'half'=2,'x'=4,'core'=2] {'x'}, dimensions={0} | all-to-all | bytes 229376 | tf_op jit(solution)/shard_map/all_to_all | solution.py:22
  11.0 29.0 %collective-permute-start = (bf16[56,1024]{1,0:T(8,128)(2,1)S(1)}, bf16[56,1024]{1,0:T(8,128)(2,1)S(1)}, u32[]{:S(2)}, u32[]{:S(2)}) collective-permute-start(bf16[56,1024]{1,0:T(8,128)(2,1)S(1)} %reshape.43), channel_id=1, source_target_pairs={{0,8},{8,0},{1,9},{9,1},{2,10},{10,2},{3,11},{11,3},{4,12},{12,4},... | collective-permute-start | bytes 344072 | tf_op jit(solution)/shard_map/ppermute | solution.py:44
  40.0 3.4 %collective-permute-done = bf16[56,1024]{1,0:T(8,128)(2,1)S(1)} collective-permute-done((bf16[56,1024]{1,0:T(8,128)(2,1)S(1)}, bf16[56,1024]{1,0:T(8,128)(2,1)S(1)}, u32[]{:S(2)}, u32[]{:S(2)}) %collective-permute-start) | collective-permute-done | bytes 114720 | tf_op jit(solution)/shard_map/ppermute | solution.py:44
  43.4 1.0 broadcast_in_dim.4
  44.5 14.5 %all-to-all-start.1 = ((bf16[4,2,56,1024]{3,2,1,0:T(8,128)(2,1)}), bf16[4,2,56,1024]{3,2,1,0:T(8,128)(2,1)S(1)}, u32[]{:S(2)}, u32[]{:S(2)}) async-start(bf16[4,2,56,1024]{3,2,1,0:T(8,128)(2,1)} %broadcast_in_dim.4), calls=%async_computation.1 | async-start | bytes 1835008 | tf_op jit(solution)/shard_map/all_to_all | solution.py:22
  59.0 13.8 %all-gather = bf16[8,56,1024]{2,1,0:T(8,128)(2,1)S(1)} all-gather(bf16[2,56,1024]{2,1,0:T(8,128)(2,1)S(1)} %pad_maximum_fusion.1), channel_id=2, replica_groups=mesh['layer'=4,'quarter'=4,'y'=4,'half'=2,'x'=4,'core'=2] {'y'}, dimensions={0}, use_global_device_ids=true | all-gather | bytes 1146880 | tf_op jit(solution)/shard_map/all_gather | solution.py:48
  72.8 6.6 %all-to-all-done.1 = bf16[4,2,56,1024]{3,2,1,0:T(8,128)(2,1)S(1)} async-done(((bf16[4,2,56,1024]{3,2,1,0:T(8,128)(2,1)}), bf16[4,2,56,1024]{3,2,1,0:T(8,128)(2,1)S(1)}, u32[]{:S(2)}, u32[]{:S(2)}) %all-to-all-start.1) | async-done | bytes 917536 | tf_op jit(solution)/shard_map/all_to_all | solution.py:22
  79.4 1.9 %collective-permute-start.1 = (bf16[4,2,56,1024]{3,2,1,0:T(8,128)(2,1)S(1)}, bf16[4,2,56,1024]{3,2,1,0:T(8,128)(2,1)S(1)}, u32[]{:S(2)}, u32[]{:S(2)}) collective-permute-start(bf16[4,2,56,1024]{3,2,1,0:T(8,128)(2,1)S(1)} %all-to-all-done.1), channel_id=1, source_target_pairs={{0,1},{1,0},{2,3},{3,2},{4,5},{5,4},{6,7},{7,6},{8,9},{9,8},{10,11... | collective-permute-start | bytes 2752520 | tf_op jit(solution)/shard_map/ppermute | solution.py:50
  81.3 2.4 %collective-permute-done.1 = bf16[4,2,56,1024]{3,2,1,0:T(8,128)(2,1)S(1)} collective-permute-done((bf16[4,2,56,1024]{3,2,1,0:T(8,128)(2,1)S(1)}, bf16[4,2,56,1024]{3,2,1,0:T(8,128)(2,1)S(1)}, u32[]{:S(2)}, u32[]{:S(2)}) %collective-permute-start.1) | collective-permute-done | bytes 917536 | tf_op jit(solution)/shard_map/ppermute | solution.py:50
  83.9 0.2 maximum_bitcast_fusion
  84.1 0.2 pad_maximum_fusion
  84.2 1.1 convolution_convert_fusion.1
  85.4 15.4 %all_to_all.26 = bf16[4,112,896]{2,1,0:T(8,128)(2,1)S(1)} all-to-all(bf16[4,112,896]{2,1,0:T(8,128)(2,1)S(1)} %bitcast.32), channel_id=1, replica_groups=mesh['layer'=4,'quarter'=4,'y'=4,'half'=2,'x'=4,'core'=2] {'x'}, dimensions={0} | all-to-all | bytes 1605632 | tf_op jit(solution)/shard_map/all_to_all | solution.py:22
  101.0 14.4 %all_gather.14 = bf16[448,896]{1,0:T(8,128)(2,1)S(1)} all-gather(bf16[112,896]{1,0:T(8,128)(2,1)S(1)} %reduce_sum.45), channel_id=1, replica_groups=mesh['layer'=4,'quarter'=4,'y'=4,'half'=2,'x'=4,'core'=2] {'x'}, dimensions={0}, use_global_device_ids=true | all-gather | bytes 1003520 | tf_op jit(solution)/shard_map/all_gather | solution.py:56
  115.3 1.1 convolution_convert_fusion
  116.4 13.4 %all_to_all.27 = bf16[4,112,1024]{2,1,0:T(8,128)(2,1)S(1)} all-to-all(bf16[4,112,1024]{2,1,0:T(8,128)(2,1)S(1)} %bitcast.29), channel_id=1, replica_groups=mesh['layer'=4,'quarter'=4,'y'=4,'half'=2,'x'=4,'core'=2] {'y'}, dimensions={0} | all-to-all | bytes 1835008 | tf_op jit(solution)/shard_map/all_to_all | solution.py:22
  129.9 0.2 select_reduce_fusion.1
  130.1 1.9 %collective-permute-start.3 = (bf16[112,512]{1,0:T(8,128)(2,1)S(1)}, bf16[112,512]{1,0:T(8,128)(2,1)S(1)}, u32[]{:S(2)}, u32[]{:S(2)}) collective-permute-start(bf16[112,512]{1,0:T(8,128)(2,1)S(1)} %get-tuple-element.14), channel_id=1, source_target_pairs={{0,1},{1,0},{2,3},{3,2},{4,5},{5,4},{6,7},{7,6},{8,9},{9,8},{10,11... | collective-permute-start | bytes 344072 | tf_op jit(solution)/shard_map/ppermute | solution.py:63
  132.0 2.4 %collective-permute-start.2 = (bf16[448,448]{1,0:T(8,128)(2,1)S(1)}, bf16[448,448]{1,0:T(8,128)(2,1)S(1)}, u32[]{:S(2)}, u32[]{:S(2)}) collective-permute-start(bf16[448,448]{1,0:T(8,128)(2,1)S(1)} %slice.54), channel_id=1, source_target_pairs={{0,1},{1,0},{2,3},{3,2},{4,5},{5,4},{6,7},{7,6},{8,9},{9,8},{10,11... | collective-permute-start | bytes 1204232 | tf_op jit(solution)/shard_map/ppermute | solution.py:58
  134.6 13.6 %all-gather.1 = bf16[2,448,512]{2,1,0:T(8,128)(2,1)S(1)} all-gather(bf16[2,112,512]{2,1,0:T(8,128)(2,1)S(1)} %pad_maximum_fusion.2), channel_id=3, replica_groups=mesh['layer'=4,'quarter'=4,'y'=4,'half'=2,'x'=4,'core'=2] {'y'}, dimensions={1}, use_global_device_ids=true | all-gather | bytes 1146880 | tf_op jit(solution)/shard_map/all_gather | solution.py:65
  148.2 0.7 convolution_convert_fusion.2
  148.8 14.5 %all_to_all.28 = bf16[4,112,512]{2,1,0:T(8,128)(2,1)S(1)} all-to-all(bf16[4,112,512]{2,1,0:T(8,128)(2,1)S(1)} %bitcast.36), channel_id=1, replica_groups=mesh['layer'=4,'quarter'=4,'y'=4,'half'=2,'x'=4,'core'=2] {'quarter'}, dimensions={0} | all-to-all | bytes 917504 | tf_op jit(solution)/shard_map/all_to_all | solution.py:22
  163.5 0.7 convert_element_type.53
  (16 shorter events, 0.6 us)
Async XLA Ops:
  11.0 32.4 %collective-permute-start = (bf16[56,1024]{1,0:T(8,128)(2,1)S(1)}, bf16[56,1024]{1,0:T(8,128)(2,1)S(1)}, u32[]{:S(2)}, u32[]{:S(2)}) collective-permute-start(bf16[56,1024]{1,0:T(8,128)(2,1)S(1)} %reshape.43), channel_id=1, source_target_pairs={{0,8},{8,0},{1,9},{9,1},{2,10},{10,2},{3,11},{11,3},{4,12},{12,4},... | collective-permute-start | bytes 344072 | tf_op jit(solution)/shard_map/ppermute | solution.py:44
  44.5 34.9 %all-to-all-start.1 = ((bf16[4,2,56,1024]{3,2,1,0:T(8,128)(2,1)}), bf16[4,2,56,1024]{3,2,1,0:T(8,128)(2,1)S(1)}, u32[]{:S(2)}, u32[]{:S(2)}) async-start(bf16[4,2,56,1024]{3,2,1,0:T(8,128)(2,1)} %broadcast_in_dim.4), calls=%async_computation.1 | async-start | bytes 1835008 | tf_op jit(solution)/shard_map/all_to_all | solution.py:22
  79.4 4.4 %collective-permute-start.1 = (bf16[4,2,56,1024]{3,2,1,0:T(8,128)(2,1)S(1)}, bf16[4,2,56,1024]{3,2,1,0:T(8,128)(2,1)S(1)}, u32[]{:S(2)}, u32[]{:S(2)}) collective-permute-start(bf16[4,2,56,1024]{3,2,1,0:T(8,128)(2,1)S(1)} %all-to-all-done.1), channel_id=1, source_target_pairs={{0,1},{1,0},{2,3},{3,2},{4,5},{5,4},{6,7},{7,6},{8,9},{9,8},{10,11... | collective-permute-start | bytes 2752520 | tf_op jit(solution)/shard_map/ppermute | solution.py:50
  130.1 4.4 %collective-permute-start.3 = (bf16[112,512]{1,0:T(8,128)(2,1)S(1)}, bf16[112,512]{1,0:T(8,128)(2,1)S(1)}, u32[]{:S(2)}, u32[]{:S(2)}) collective-permute-start(bf16[112,512]{1,0:T(8,128)(2,1)S(1)} %get-tuple-element.14), channel_id=1, source_target_pairs={{0,1},{1,0},{2,3},{3,2},{4,5},{5,4},{6,7},{7,6},{8,9},{9,8},{10,11... | collective-permute-start | bytes 344072 | tf_op jit(solution)/shard_map/ppermute | solution.py:63
  132.0 16.1 %collective-permute-start.2 = (bf16[448,448]{1,0:T(8,128)(2,1)S(1)}, bf16[448,448]{1,0:T(8,128)(2,1)S(1)}, u32[]{:S(2)}, u32[]{:S(2)}) collective-permute-start(bf16[448,448]{1,0:T(8,128)(2,1)S(1)} %slice.54), channel_id=1, source_target_pairs={{0,1},{1,0},{2,3},{3,2},{4,5},{5,4},{6,7},{7,6},{8,9},{9,8},{10,11... | collective-permute-start | bytes 1204232 | tf_op jit(solution)/shard_map/ppermute | solution.py:58

commit v21 on v20

--- a/solution.py
+++ b/solution.py
@@ -41,7 +41,8 @@
     core = lax.axis_index("core")
     rows = jnp.stack([momentum[0, :, i * w : (i + 1) * w] for i in range(nx)])
     own = exchange(rows, "x").reshape(n, w)
-    other = lax.ppermute(own, "half", SWAP)
+    crossed = [(2 * q + g, 2 * (q ^ 1) + 1 - g) for q in range(nq) for g in range(2)]
+    other = lax.ppermute(own, ("quarter", "half"), crossed)
 
     both = jnp.stack([own, other])
     block = spread(both, "quarter")

time: 165 us -> 166 us (level)
  waiting for transfers between devices: 12.5 us -> 24.7 us
  starting transfers between devices: 49.7 us -> 38.3 us
    ppermute x1, waiting for transfers between devices: 3.41 us -> 14.7 us  [shards(): other = lax.ppermute(own, ('quarter', 'half'), crossed)]
    all_to_all x1, starting transfers between devices: 14.5 us -> 3.5 us  [exchange(): return lax.all_to_all(blocks, axis, 0, 0, tiled=True)]
where the time goes in v21:
time: 166 us; the launch traced here: 165 us
  blocking collectives  95.3 us (57%)
  starting transfers between devices  38.3 us (23%)
  waiting for transfers between devices  24.7 us (15%)
  matrix products  2.93 us (2%)
  local copies, waits for them, and re-layouts  2.7 us (2%)
    all_to_all x4, blocking collectives, exchange(): return lax.all_to_all(blocks, axis, 0, 0, tiled=True)  53.5 us
    ppermute x1, starting transfers between devices, shards(): other = lax.ppermute(own, ('quarter', 'half'), crossed)  28.5 us
    ppermute x1, waiting for transfers between devices, shards(): other = lax.ppermute(own, ('quarter', 'half'), crossed)  14.7 us
    all_gather x1, blocking collectives, shards(): gram = lax.all_gather(mine, 'x', axis=0, tiled=True)  14.4 us
    all_gather x1, blocking collectives, shards(): left = lax.all_gather(both, 'y', axis=0).reshape(ny * 2 * n, w)  13.9 us
    all_gather x1, blocking collectives, shards(): firsts = lax.all_gather(first, 'y', axis=1).reshape(nc * ny * 2 * n, h)  13.6 us
    all_to_all x1, waiting for transfers between devices, exchange(): return lax.all_to_all(blocks, axis, 0, 0, tiled=True)  7.59 us
    all_to_all x1, starting transfers between devices, exchange(): return lax.all_to_all(blocks, axis, 0, 0, tiled=True)  3.5 us
  transfers between devices with their start and end apart: 5, of which 3 were waited for; matrix products, arithmetic and copies ran while one was open for 0% of the time, Pallas kernels for 0%

profile of v21, /device:TPU:8, one launch (start us, length us, event | category | flops | bytes accessed | tf_op | source)
XLA Modules:
  0.0 165.1 jit_solution(12572598299814410986)
XLA Ops:
  0.0 0.8 fusion.4
  0.9 10.1 %all_to_all.25 = bf16[4,14,1024]{2,1,0:T(8,128)(2,1)S(1)} all-to-all(bf16[4,14,1024]{2,1,0:T(8,128)(2,1)S(1)} %pad_maximum_fusion.3), channel_id=1, replica_groups=mesh['layer'=4,'quarter'=4,'y'=4,'half'=2,'x'=4,'core'=2] {'x'}, dimensions={0} | all-to-all | bytes 229376 | tf_op jit(solution)/shard_map/all_to_all | solution.py:22
  11.0 28.5 %collective-permute-start = (bf16[56,1024]{1,0:T(8,128)(2,1)S(1)}, bf16[56,1024]{1,0:T(8,128)(2,1)S(1)}, u32[]{:S(2)}, u32[]{:S(2)}) collective-permute-start(bf16[56,1024]{1,0:T(8,128)(2,1)S(1)} %reshape.43), channel_id=1, source_target_pairs={{0,72},{8,64},{64,8},{72,0},{128,200},{136,192},{192,136},{200,128... | collective-permute-start | bytes 344072 | tf_op jit(solution)/shard_map/ppermute | solution.py:45
  39.6 14.7 %collective-permute-done = bf16[56,1024]{1,0:T(8,128)(2,1)S(1)} collective-permute-done((bf16[56,1024]{1,0:T(8,128)(2,1)S(1)}, bf16[56,1024]{1,0:T(8,128)(2,1)S(1)}, u32[]{:S(2)}, u32[]{:S(2)}) %collective-permute-start) | collective-permute-done | bytes 114720 | tf_op jit(solution)/shard_map/ppermute | solution.py:45
  54.2 1.0 broadcast_in_dim.4
  55.3 3.5 %all-to-all-start.1 = ((bf16[4,2,56,1024]{3,2,1,0:T(8,128)(2,1)}), bf16[4,2,56,1024]{3,2,1,0:T(8,128)(2,1)S(1)}, u32[]{:S(2)}, u32[]{:S(2)}) async-start(bf16[4,2,56,1024]{3,2,1,0:T(8,128)(2,1)} %broadcast_in_dim.4), calls=%async_computation.1 | async-start | bytes 1835008 | tf_op jit(solution)/shard_map/all_to_all | solution.py:22
  58.8 13.9 %all-gather = bf16[8,56,1024]{2,1,0:T(8,128)(2,1)S(1)} all-gather(bf16[2,56,1024]{2,1,0:T(8,128)(2,1)S(1)} %pad_maximum_fusion.1), channel_id=2, replica_groups=mesh['layer'=4,'quarter'=4,'y'=4,'half'=2,'x'=4,'core'=2] {'y'}, dimensions={0}, use_global_device_ids=true | all-gather | bytes 1146880 | tf_op jit(solution)/shard_map/all_gather | solution.py:49
  72.7 7.6 %all-to-all-done.1 = bf16[4,2,56,1024]{3,2,1,0:T(8,128)(2,1)S(1)} async-done(((bf16[4,2,56,1024]{3,2,1,0:T(8,128)(2,1)}), bf16[4,2,56,1024]{3,2,1,0:T(8,128)(2,1)S(1)}, u32[]{:S(2)}, u32[]{:S(2)}) %all-to-all-start.1) | async-done | bytes 917536 | tf_op jit(solution)/shard_map/all_to_all | solution.py:22
  80.3 1.9 %collective-permute-start.1 = (bf16[4,2,56,1024]{3,2,1,0:T(8,128)(2,1)S(1)}, bf16[4,2,56,1024]{3,2,1,0:T(8,128)(2,1)S(1)}, u32[]{:S(2)}, u32[]{:S(2)}) collective-permute-start(bf16[4,2,56,1024]{3,2,1,0:T(8,128)(2,1)S(1)} %all-to-all-done.1), channel_id=1, source_target_pairs={{0,1},{1,0},{2,3},{3,2},{4,5},{5,4},{6,7},{7,6},{8,9},{9,8},{10,11... | collective-permute-start | bytes 2752520 | tf_op jit(solution)/shard_map/ppermute | solution.py:51
  82.2 2.4 %collective-permute-done.1 = bf16[4,2,56,1024]{3,2,1,0:T(8,128)(2,1)S(1)} collective-permute-done((bf16[4,2,56,1024]{3,2,1,0:T(8,128)(2,1)S(1)}, bf16[4,2,56,1024]{3,2,1,0:T(8,128)(2,1)S(1)}, u32[]{:S(2)}, u32[]{:S(2)}) %collective-permute-start.1) | collective-permute-done | bytes 917536 | tf_op jit(solution)/shard_map/ppermute | solution.py:51
  84.8 0.2 maximum_bitcast_fusion
  85.0 0.2 pad_maximum_fusion
  85.1 1.1 convolution_convert_fusion.1
  86.3 15.4 %all_to_all.26 = bf16[4,112,896]{2,1,0:T(8,128)(2,1)S(1)} all-to-all(bf16[4,112,896]{2,1,0:T(8,128)(2,1)S(1)} %bitcast.32), channel_id=1, replica_groups=mesh['layer'=4,'quarter'=4,'y'=4,'half'=2,'x'=4,'core'=2] {'x'}, dimensions={0} | all-to-all | bytes 1605632 | tf_op jit(solution)/shard_map/all_to_all | solution.py:22
  101.8 14.4 %all_gather.14 = bf16[448,896]{1,0:T(8,128)(2,1)S(1)} all-gather(bf16[112,896]{1,0:T(8,128)(2,1)S(1)} %reduce_sum.45), channel_id=1, replica_groups=mesh['layer'=4,'quarter'=4,'y'=4,'half'=2,'x'=4,'core'=2] {'x'}, dimensions={0}, use_global_device_ids=true | all-gather | bytes 1003520 | tf_op jit(solution)/shard_map/all_gather | solution.py:57
  116.2 1.1 convolution_convert_fusion
  117.3 13.4 %all_to_all.27 = bf16[4,112,1024]{2,1,0:T(8,128)(2,1)S(1)} all-to-all(bf16[4,112,1024]{2,1,0:T(8,128)(2,1)S(1)} %bitcast.29), channel_id=1, replica_groups=mesh['layer'=4,'quarter'=4,'y'=4,'half'=2,'x'=4,'core'=2] {'y'}, dimensions={0} | all-to-all | bytes 1835008 | tf_op jit(solution)/shard_map/all_to_all | solution.py:22
  130.8 0.2 select_reduce_fusion.1
  131.0 1.9 %collective-permute-start.3 = (bf16[112,512]{1,0:T(8,128)(2,1)S(1)}, bf16[112,512]{1,0:T(8,128)(2,1)S(1)}, u32[]{:S(2)}, u32[]{:S(2)}) collective-permute-start(bf16[112,512]{1,0:T(8,128)(2,1)S(1)} %get-tuple-element.14), channel_id=1, source_target_pairs={{0,1},{1,0},{2,3},{3,2},{4,5},{5,4},{6,7},{7,6},{8,9},{9,8},{10,11... | collective-permute-start | bytes 344072 | tf_op jit(solution)/shard_map/ppermute | solution.py:64
  132.9 2.4 %collective-permute-start.2 = (bf16[448,448]{1,0:T(8,128)(2,1)S(1)}, bf16[448,448]{1,0:T(8,128)(2,1)S(1)}, u32[]{:S(2)}, u32[]{:S(2)}) collective-permute-start(bf16[448,448]{1,0:T(8,128)(2,1)S(1)} %slice.54), channel_id=1, source_target_pairs={{0,1},{1,0},{2,3},{3,2},{4,5},{5,4},{6,7},{7,6},{8,9},{9,8},{10,11... | collective-permute-start | bytes 1204232 | tf_op jit(solution)/shard_map/ppermute | solution.py:59
  135.5 13.6 %all-gather.1 = bf16[2,448,512]{2,1,0:T(8,128)(2,1)S(1)} all-gather(bf16[2,112,512]{2,1,0:T(8,128)(2,1)S(1)} %pad_maximum_fusion.2), channel_id=3, replica_groups=mesh['layer'=4,'quarter'=4,'y'=4,'half'=2,'x'=4,'core'=2] {'y'}, dimensions={1}, use_global_device_ids=true | all-gather | bytes 1146880 | tf_op jit(solution)/shard_map/all_gather | solution.py:66
  149.0 0.7 convolution_convert_fusion.2
  149.7 14.5 %all_to_all.28 = bf16[4,112,512]{2,1,0:T(8,128)(2,1)S(1)} all-to-all(bf16[4,112,512]{2,1,0:T(8,128)(2,1)S(1)} %bitcast.36), channel_id=1, replica_groups=mesh['layer'=4,'quarter'=4,'y'=4,'half'=2,'x'=4,'core'=2] {'quarter'}, dimensions={0} | all-to-all | bytes 917504 | tf_op jit(solution)/shard_map/all_to_all | solution.py:22
  164.4 0.7 convert_element_type.53
  (16 shorter events, 0.6 us)
Async XLA Ops:
  11.0 43.2 %collective-permute-start = (bf16[56,1024]{1,0:T(8,128)(2,1)S(1)}, bf16[56,1024]{1,0:T(8,128)(2,1)S(1)}, u32[]{:S(2)}, u32[]{:S(2)}) collective-permute-start(bf16[56,1024]{1,0:T(8,128)(2,1)S(1)} %reshape.43), channel_id=1, source_target_pairs={{0,72},{8,64},{64,8},{72,0},{128,200},{136,192},{192,136},{200,128... | collective-permute-start | bytes 344072 | tf_op jit(solution)/shard_map/ppermute | solution.py:45
  55.3 25.0 %all-to-all-start.1 = ((bf16[4,2,56,1024]{3,2,1,0:T(8,128)(2,1)}), bf16[4,2,56,1024]{3,2,1,0:T(8,128)(2,1)S(1)}, u32[]{:S(2)}, u32[]{:S(2)}) async-start(bf16[4,2,56,1024]{3,2,1,0:T(8,128)(2,1)} %broadcast_in_dim.4), calls=%async_computation.1 | async-start | bytes 1835008 | tf_op jit(solution)/shard_map/all_to_all | solution.py:22
  80.3 4.4 %collective-permute-start.1 = (bf16[4,2,56,1024]{3,2,1,0:T(8,128)(2,1)S(1)}, bf16[4,2,56,1024]{3,2,1,0:T(8,128)(2,1)S(1)}, u32[]{:S(2)}, u32[]{:S(2)}) collective-permute-start(bf16[4,2,56,1024]{3,2,1,0:T(8,128)(2,1)S(1)} %all-to-all-done.1), channel_id=1, source_target_pairs={{0,1},{1,0},{2,3},{3,2},{4,5},{5,4},{6,7},{7,6},{8,9},{9,8},{10,11... | collective-permute-start | bytes 2752520 | tf_op jit(solution)/shard_map/ppermute | solution.py:51
  131.0 4.4 %collective-permute-start.3 = (bf16[112,512]{1,0:T(8,128)(2,1)S(1)}, bf16[112,512]{1,0:T(8,128)(2,1)S(1)}, u32[]{:S(2)}, u32[]{:S(2)}) collective-permute-start(bf16[112,512]{1,0:T(8,128)(2,1)S(1)} %get-tuple-element.14), channel_id=1, source_target_pairs={{0,1},{1,0},{2,3},{3,2},{4,5},{5,4},{6,7},{7,6},{8,9},{9,8},{10,11... | collective-permute-start | bytes 344072 | tf_op jit(solution)/shard_map/ppermute | solution.py:64
  132.9 16.1 %collective-permute-start.2 = (bf16[448,448]{1,0:T(8,128)(2,1)S(1)}, bf16[448,448]{1,0:T(8,128)(2,1)S(1)}, u32[]{:S(2)}, u32[]{:S(2)}) collective-permute-start(bf16[448,448]{1,0:T(8,128)(2,1)S(1)} %slice.54), channel_id=1, source_target_pairs={{0,1},{1,0},{2,3},{3,2},{4,5},{5,4},{6,7},{7,6},{8,9},{9,8},{10,11... | collective-permute-start | bytes 1204232 | tf_op jit(solution)/shard_map/ppermute | solution.py:59

commit v22 on v20

--- a/solution.py
+++ b/solution.py
@@ -44,7 +44,7 @@
     other = lax.ppermute(own, "half", SWAP)
 
     both = jnp.stack([own, other])
-    block = spread(both, "quarter")
+    block = spread(both.reshape(2 * n, w), "quarter").reshape(nq, 2, n, w)
     left = lax.all_gather(both, "y", axis=0).reshape(ny * 2 * n, w)
     block, left = lax.optimization_barrier((block, left))
     across = lax.ppermute(block, "core", SWAP)

time: 165 us -> 165 us (level)
  no operation moved by 1% of the time
where the time goes in v22:
time: 165 us; the launch traced here: 164 us
  blocking collectives  95.2 us (58%)
  starting transfers between devices  49.7 us (30%)
  waiting for transfers between devices  12.5 us (8%)
  matrix products  2.94 us (2%)
  local copies, waits for them, and re-layouts  2.7 us (2%)
    all_to_all x4, blocking collectives, exchange(): return lax.all_to_all(blocks, axis, 0, 0, tiled=True)  53.5 us
    ppermute x1, starting transfers between devices, shards(): other = lax.ppermute(own, 'half', SWAP)  29 us
    all_to_all x1, starting transfers between devices, exchange(): return lax.all_to_all(blocks, axis, 0, 0, tiled=True)  14.5 us
    all_gather x1, blocking collectives, shards(): gram = lax.all_gather(mine, 'x', axis=0, tiled=True)  14.4 us
    all_gather x1, blocking collectives, shards(): left = lax.all_gather(both, 'y', axis=0).reshape(ny * 2 * n, w)  13.8 us
    all_gather x1, blocking collectives, shards(): firsts = lax.all_gather(first, 'y', axis=1).reshape(nc * ny * 2 * n, h)  13.6 us
    all_to_all x1, waiting for transfers between devices, exchange(): return lax.all_to_all(blocks, axis, 0, 0, tiled=True)  6.65 us
    ppermute x1, waiting for transfers between devices, shards(): other = lax.ppermute(own, 'half', SWAP)  3.41 us
  transfers between devices with their start and end apart: 5, of which 3 were waited for; matrix products, arithmetic and copies ran while one was open for 0% of the time, Pallas kernels for 0%

profile of v22, /device:TPU:8, one launch (start us, length us, event | category | flops | bytes accessed | tf_op | source)
XLA Modules:
  0.0 164.2 jit_solution(10265237464986158394)
XLA Ops:
  0.0 0.8 fusion.4
  0.9 10.1 %all_to_all.25 = bf16[4,14,1024]{2,1,0:T(8,128)(2,1)S(1)} all-to-all(bf16[4,14,1024]{2,1,0:T(8,128)(2,1)S(1)} %pad_maximum_fusion.3), channel_id=1, replica_groups=mesh['layer'=4,'quarter'=4,'y'=4,'half'=2,'x'=4,'core'=2] {'x'}, dimensions={0} | all-to-all | bytes 229376 | tf_op jit(solution)/shard_map/all_to_all | solution.py:22
  11.0 29.0 %collective-permute-start = (bf16[56,1024]{1,0:T(8,128)(2,1)S(1)}, bf16[56,1024]{1,0:T(8,128)(2,1)S(1)}, u32[]{:S(2)}, u32[]{:S(2)}) collective-permute-start(bf16[56,1024]{1,0:T(8,128)(2,1)S(1)} %reshape.46), channel_id=1, source_target_pairs={{0,8},{8,0},{1,9},{9,1},{2,10},{10,2},{3,11},{11,3},{4,12},{12,4},... | collective-permute-start | bytes 344072 | tf_op jit(solution)/shard_map/ppermute | solution.py:44
  40.0 3.4 %collective-permute-done = bf16[56,1024]{1,0:T(8,128)(2,1)S(1)} collective-permute-done((bf16[56,1024]{1,0:T(8,128)(2,1)S(1)}, bf16[56,1024]{1,0:T(8,128)(2,1)S(1)}, u32[]{:S(2)}, u32[]{:S(2)}) %collective-permute-start) | collective-permute-done | bytes 114720 | tf_op jit(solution)/shard_map/ppermute | solution.py:44
  43.4 1.0 broadcast_in_dim.9
  44.5 14.5 %all-to-all-start.1 = ((bf16[4,112,1024]{2,1,0:T(8,128)(2,1)}), bf16[4,112,1024]{2,1,0:T(8,128)(2,1)S(1)}, u32[]{:S(2)}, u32[]{:S(2)}) async-start(bf16[4,112,1024]{2,1,0:T(8,128)(2,1)} %broadcast_in_dim.9), calls=%async_computation.1 | async-start | bytes 1835008 | tf_op jit(solution)/shard_map/all_to_all | solution.py:22
  59.0 13.8 %all-gather = bf16[8,56,1024]{2,1,0:T(8,128)(2,1)S(1)} all-gather(bf16[2,56,1024]{2,1,0:T(8,128)(2,1)S(1)} %pad_maximum_fusion.1), channel_id=2, replica_groups=mesh['layer'=4,'quarter'=4,'y'=4,'half'=2,'x'=4,'core'=2] {'y'}, dimensions={0}, use_global_device_ids=true | all-gather | bytes 1146880 | tf_op jit(solution)/shard_map/all_gather | solution.py:48
  72.8 6.6 %all-to-all-done.1 = bf16[4,112,1024]{2,1,0:T(8,128)(2,1)S(1)} async-done(((bf16[4,112,1024]{2,1,0:T(8,128)(2,1)}), bf16[4,112,1024]{2,1,0:T(8,128)(2,1)S(1)}, u32[]{:S(2)}, u32[]{:S(2)}) %all-to-all-start.1) | async-done | bytes 917536 | tf_op jit(solution)/shard_map/all_to_all | solution.py:22
  79.4 1.9 %collective-permute-start.1 = (bf16[4,2,56,1024]{3,2,1,0:T(8,128)(2,1)S(1)}, bf16[4,2,56,1024]{3,2,1,0:T(8,128)(2,1)S(1)}, u32[]{:S(2)}, u32[]{:S(2)}) collective-permute-start(bf16[4,2,56,1024]{3,2,1,0:T(8,128)(2,1)S(1)} %bitcast.28), channel_id=1, source_target_pairs={{0,1},{1,0},{2,3},{3,2},{4,5},{5,4},{6,7},{7,6},{8,9},{9,8},{10,11... | collective-permute-start | bytes 2752520 | tf_op jit(solution)/shard_map/ppermute | solution.py:50
  81.3 2.4 %collective-permute-done.1 = bf16[4,2,56,1024]{3,2,1,0:T(8,128)(2,1)S(1)} collective-permute-done((bf16[4,2,56,1024]{3,2,1,0:T(8,128)(2,1)S(1)}, bf16[4,2,56,1024]{3,2,1,0:T(8,128)(2,1)S(1)}, u32[]{:S(2)}, u32[]{:S(2)}) %collective-permute-start.1) | collective-permute-done | bytes 917536 | tf_op jit(solution)/shard_map/ppermute | solution.py:50
  83.9 0.2 maximum_bitcast_fusion
  84.1 0.2 pad_maximum_fusion
  84.2 1.1 convolution_convert_fusion.1
  85.4 15.4 %all_to_all.26 = bf16[4,112,896]{2,1,0:T(8,128)(2,1)S(1)} all-to-all(bf16[4,112,896]{2,1,0:T(8,128)(2,1)S(1)} %bitcast.37), channel_id=1, replica_groups=mesh['layer'=4,'quarter'=4,'y'=4,'half'=2,'x'=4,'core'=2] {'x'}, dimensions={0} | all-to-all | bytes 1605632 | tf_op jit(solution)/shard_map/all_to_all | solution.py:22
  101.0 14.4 %all_gather.17 = bf16[448,896]{1,0:T(8,128)(2,1)S(1)} all-gather(bf16[112,896]{1,0:T(8,128)(2,1)S(1)} %reduce_sum.45), channel_id=1, replica_groups=mesh['layer'=4,'quarter'=4,'y'=4,'half'=2,'x'=4,'core'=2] {'x'}, dimensions={0}, use_global_device_ids=true | all-gather | bytes 1003520 | tf_op jit(solution)/shard_map/all_gather | solution.py:56
  115.3 1.1 convolution_convert_fusion
  116.4 13.4 %all_to_all.27 = bf16[4,112,1024]{2,1,0:T(8,128)(2,1)S(1)} all-to-all(bf16[4,112,1024]{2,1,0:T(8,128)(2,1)S(1)} %bitcast.34), channel_id=1, replica_groups=mesh['layer'=4,'quarter'=4,'y'=4,'half'=2,'x'=4,'core'=2] {'y'}, dimensions={0} | all-to-all | bytes 1835008 | tf_op jit(solution)/shard_map/all_to_all | solution.py:22
  129.9 0.2 select_reduce_fusion.1
  130.1 1.9 %collective-permute-start.3 = (bf16[112,512]{1,0:T(8,128)(2,1)S(1)}, bf16[112,512]{1,0:T(8,128)(2,1)S(1)}, u32[]{:S(2)}, u32[]{:S(2)}) collective-permute-start(bf16[112,512]{1,0:T(8,128)(2,1)S(1)} %get-tuple-element.14), channel_id=1, source_target_pairs={{0,1},{1,0},{2,3},{3,2},{4,5},{5,4},{6,7},{7,6},{8,9},{9,8},{10,11... | collective-permute-start | bytes 344072 | tf_op jit(solution)/shard_map/ppermute | solution.py:63
  132.0 2.4 %collective-permute-start.2 = (bf16[448,448]{1,0:T(8,128)(2,1)S(1)}, bf16[448,448]{1,0:T(8,128)(2,1)S(1)}, u32[]{:S(2)}, u32[]{:S(2)}) collective-permute-start(bf16[448,448]{1,0:T(8,128)(2,1)S(1)} %slice.54), channel_id=1, source_target_pairs={{0,1},{1,0},{2,3},{3,2},{4,5},{5,4},{6,7},{7,6},{8,9},{9,8},{10,11... | collective-permute-start | bytes 1204232 | tf_op jit(solution)/shard_map/ppermute | solution.py:58
  134.6 13.6 %all-gather.1 = bf16[2,448,512]{2,1,0:T(8,128)(2,1)S(1)} all-gather(bf16[2,112,512]{2,1,0:T(8,128)(2,1)S(1)} %pad_maximum_fusion.2), channel_id=3, replica_groups=mesh['layer'=4,'quarter'=4,'y'=4,'half'=2,'x'=4,'core'=2] {'y'}, dimensions={1}, use_global_device_ids=true | all-gather | bytes 1146880 | tf_op jit(solution)/shard_map/all_gather | solution.py:65
  148.2 0.7 convolution_convert_fusion.2
  148.8 14.5 %all_to_all.28 = bf16[4,112,512]{2,1,0:T(8,128)(2,1)S(1)} all-to-all(bf16[4,112,512]{2,1,0:T(8,128)(2,1)S(1)} %bitcast.41), channel_id=1, replica_groups=mesh['layer'=4,'quarter'=4,'y'=4,'half'=2,'x'=4,'core'=2] {'quarter'}, dimensions={0} | all-to-all | bytes 917504 | tf_op jit(solution)/shard_map/all_to_all | solution.py:22
  163.5 0.7 convert_element_type.53
  (16 shorter events, 0.6 us)
Async XLA Ops:
  11.0 32.4 %collective-permute-start = (bf16[56,1024]{1,0:T(8,128)(2,1)S(1)}, bf16[56,1024]{1,0:T(8,128)(2,1)S(1)}, u32[]{:S(2)}, u32[]{:S(2)}) collective-permute-start(bf16[56,1024]{1,0:T(8,128)(2,1)S(1)} %reshape.46), channel_id=1, source_target_pairs={{0,8},{8,0},{1,9},{9,1},{2,10},{10,2},{3,11},{11,3},{4,12},{12,4},... | collective-permute-start | bytes 344072 | tf_op jit(solution)/shard_map/ppermute | solution.py:44
  44.5 34.9 %all-to-all-start.1 = ((bf16[4,112,1024]{2,1,0:T(8,128)(2,1)}), bf16[4,112,1024]{2,1,0:T(8,128)(2,1)S(1)}, u32[]{:S(2)}, u32[]{:S(2)}) async-start(bf16[4,112,1024]{2,1,0:T(8,128)(2,1)} %broadcast_in_dim.9), calls=%async_computation.1 | async-start | bytes 1835008 | tf_op jit(solution)/shard_map/all_to_all | solution.py:22
  79.4 4.4 %collective-permute-start.1 = (bf16[4,2,56,1024]{3,2,1,0:T(8,128)(2,1)S(1)}, bf16[4,2,56,1024]{3,2,1,0:T(8,128)(2,1)S(1)}, u32[]{:S(2)}, u32[]{:S(2)}) collective-permute-start(bf16[4,2,56,1024]{3,2,1,0:T(8,128)(2,1)S(1)} %bitcast.28), channel_id=1, source_target_pairs={{0,1},{1,0},{2,3},{3,2},{4,5},{5,4},{6,7},{7,6},{8,9},{9,8},{10,11... | collective-permute-start | bytes 2752520 | tf_op jit(solution)/shard_map/ppermute | solution.py:50
  130.1 4.4 %collective-permute-start.3 = (bf16[112,512]{1,0:T(8,128)(2,1)S(1)}, bf16[112,512]{1,0:T(8,128)(2,1)S(1)}, u32[]{:S(2)}, u32[]{:S(2)}) collective-permute-start(bf16[112,512]{1,0:T(8,128)(2,1)S(1)} %get-tuple-element.14), channel_id=1, source_target_pairs={{0,1},{1,0},{2,3},{3,2},{4,5},{5,4},{6,7},{7,6},{8,9},{9,8},{10,11... | collective-permute-start | bytes 344072 | tf_op jit(solution)/shard_map/ppermute | solution.py:63
  132.0 16.1 %collective-permute-start.2 = (bf16[448,448]{1,0:T(8,128)(2,1)S(1)}, bf16[448,448]{1,0:T(8,128)(2,1)S(1)}, u32[]{:S(2)}, u32[]{:S(2)}) collective-permute-start(bf16[448,448]{1,0:T(8,128)(2,1)S(1)} %slice.54), channel_id=1, source_target_pairs={{0,1},{1,0},{2,3},{3,2},{4,5},{5,4},{6,7},{7,6},{8,9},{9,8},{10,11... | collective-permute-start | bytes 1204232 | tf_op jit(solution)/shard_map/ppermute | solution.py:58
